TPU v7x, 32 devices: a whole 2x2x4 slice. The times are simulated.
32 devices in a mesh: grp: 2 (over y), node: 4 (over x, core), feat: 4 (over z).
Axes of the slice: x: 2, y: 2, z: 4, core: 2. Of those that a mesh axis runs over, the one named last changes fastest.
Arguments:
- features: bfloat16 [32768, 256], P(('grp', 'node')), parts along dimension 0, may hold values from -6 to 6
- band_cols: int32 [256, 16], P(('grp', 'node', 'feat')), parts along dimension 0, may hold values from 0 to 95
- band_adj: int32 [256, 16, 128, 128], P(('grp', 'node', 'feat')), parts along dimension 0, may hold values 0 or 1
- far_cols: int32 [8, 4, 4, 3], P(('grp', 'node'), 'feat'), parts along dimension 0, may hold values from 0 to 31
- far_rows: int32 [8, 4, 4, 3], P(('grp', 'node'), 'feat'), parts along dimension 0, may hold values from 0 to 7
- far_live: int32 [8, 4, 4], P(('grp', 'node'), 'feat'), parts along dimension 0, may hold values from 0 to 3
- far_adj: int32 [8, 4, 4, 3, 128, 128], P(('grp', 'node'), 'feat'), parts along dimension 0, may hold values 0 or 1
- degree: int32 [32768], P(('grp', 'node', 'feat')), parts along dimension 0, may hold values from 16 to 128
- w_self: bfloat16 [256, 256], replicated, may hold values from -0.375 to 0.375
- w_neigh: bfloat16 [256, 256], replicated, may hold values from -1.5 to 1.5
- grad_out: bfloat16 [32768, 256], P(('grp', 'node', 'feat')), parts along dimension 0, may hold values from -6 to 6
Outputs:
- layer_out: bfloat16 [32768, 256], P(('grp', 'node', 'feat')), parts along dimension 0
- grad_features: float32 [32768, 256], P(('grp', 'node', 'feat')), parts along dimension 0
- grad_self: float32 [512, 256], P('grp'), parts along dimension 0
- grad_neigh: float32 [512, 256], P('grp'), parts along dimension 0
There are 2 independent parts, one for each index of `grp`. A program takes and returns all parts, laid end to end along the dimension named above; an argument that names none is the same for every part. Nothing has to cross between parts.
Inputs may be any that keep to these rules, and one draw needn't show every extreme that they name: far_live[e, k, d] counts the leading slots of entry (e, k, d) that hold edges; the others are ignored.
All inputs are finite; a program needn't handle non-finite values. No bound on the sum of `band_adj` or of `far_adj` on one device may be relied on, other than what follows from the above.
Results may differ from a plain program's by a relative error of at most 0.0065.
Values may be sent and summed in bfloat16 or wider, within the bound.
A program may use at most 128 MiB of HBM per device.

v0:
```python
import math

import jax
import jax.numpy as jnp
from jax import lax
from jax.sharding import PartitionSpec as P


def padded(array, sides, width):
    for axis, dim in sides:
        devices, length = (lax.axis_size(axis), array.shape[dim])
        up = [(i, (i + 1) % devices) for i in range(devices)]
        down = [(j, i) for i, j in up]
        last = lax.slice_in_dim(array, length - width, length, axis=dim)
        initial = lax.slice_in_dim(array, 0, width, axis=dim)
        before = lax.ppermute(last, axis, up)
        after = lax.ppermute(initial, axis, down)
        array = jnp.concatenate([before, array, after], axis=dim)
    return array


def passed_along(block, axis, distance):
    devices = range(lax.axis_size(axis))
    route = [((i - distance) % len(devices), i) for i in devices]
    return lax.ppermute(block, axis, route)


def shards(
    features,
    band_cols,
    band_adj,
    far_cols,
    far_rows,
    far_live,
    far_adj,
    degree,
    w_self,
    w_neigh,
    grad_out,
):
    block_rows, feat_width = features.shape
    tile_size = band_adj.shape[-1]
    blocks = block_rows // tile_size
    group_size = lax.axis_size("feat")
    sub_rows = block_rows // group_size
    sub_tiles = sub_rows // tile_size
    loop_size = lax.axis_size("node")
    far_slots = far_adj.shape[3]
    member = lax.axis_index("feat")
    own_rows = lax.dynamic_slice_in_dim(features, member * sub_rows, sub_rows, 0)
    extended = padded(features, (("node", 0),), block_rows)
    ext_tiles = extended.reshape(3 * blocks, tile_size, feat_width)
    picked = ext_tiles[band_cols]
    band_blocks = band_adj.astype(jnp.bfloat16)
    near_sum = jnp.einsum("tsij,tsjf->tif", band_blocks, picked, preferred_element_type=jnp.float32)
    own_tiles = features.reshape(blocks, tile_size, feat_width)
    far_c = far_cols.reshape(loop_size, far_slots)
    far_r = far_rows.reshape(loop_size, far_slots)
    live_mask = (
        jnp.arange(far_slots, dtype=jnp.int32)[None, :] < far_live.reshape(loop_size)[:, None]
    )
    far_blocks = far_adj.reshape(loop_size, far_slots, tile_size, tile_size).astype(jnp.bfloat16)
    source_tiles = own_tiles[far_c]
    partial_value = jnp.einsum(
        "psij,psjf->psif", far_blocks, source_tiles, preferred_element_type=jnp.float32
    ).astype(jnp.bfloat16)
    partial_value = partial_value * live_mask[:, :, None, None].astype(jnp.bfloat16)
    got_parts, got_rows = (
        lax.all_to_all(partial_value, "node", split_axis=0, concat_axis=0, tiled=True),
        lax.all_to_all(far_r, "node", split_axis=0, concat_axis=0, tiled=True),
    )
    far_sum = jnp.zeros((sub_tiles, tile_size, feat_width), jnp.float32)
    far_sum = far_sum.at[got_rows.reshape(-1)].add(
        got_parts.reshape(-1, tile_size, feat_width).astype(jnp.float32)
    )
    deg_f = degree.astype(jnp.float32)[:, None]
    aggregate = ((near_sum + far_sum).reshape(sub_rows, feat_width) / deg_f).astype(jnp.bfloat16)
    pre_act = jnp.dot(own_rows, w_self, preferred_element_type=jnp.float32) + jnp.dot(
        aggregate, w_neigh, preferred_element_type=jnp.float32
    )
    layer_out = jax.nn.silu(pre_act).astype(jnp.bfloat16)
    sigmoid_z = jax.nn.sigmoid(pre_act)
    grad_z = (
        grad_out.astype(jnp.float32) * (sigmoid_z * (1.0 + pre_act * (1.0 - sigmoid_z)))
    ).astype(jnp.bfloat16)
    part_self = jnp.dot(own_rows.T, grad_z, preferred_element_type=jnp.float32)
    part_neigh = jnp.dot(aggregate.T, grad_z, preferred_element_type=jnp.float32)
    sum_self, sum_neigh = lax.psum((part_self, part_neigh), ("node", "feat"))
    grad_scale = 1.0 / math.sqrt(block_rows * loop_size)
    grad_self = sum_self * grad_scale
    grad_neigh = sum_neigh * grad_scale
    back_signal = (jnp.dot(grad_z, w_neigh.T, preferred_element_type=jnp.float32) / deg_f).astype(
        jnp.bfloat16
    )
    self_back = jnp.dot(grad_z, w_self.T, preferred_element_type=jnp.float32)
    back_tiles = back_signal.reshape(sub_tiles, tile_size, feat_width)
    spread = jnp.einsum(
        "tsij,tif->tsjf", band_blocks, back_tiles, preferred_element_type=jnp.float32
    )
    wide = jnp.zeros((3 * blocks, tile_size, feat_width), jnp.float32)
    wide = wide.at[band_cols.reshape(-1)].add(spread.reshape(-1, tile_size, feat_width))
    send_back = back_tiles[got_rows]
    returned = lax.all_to_all(send_back, "node", split_axis=0, concat_axis=0, tiled=True)
    far_back = jnp.einsum(
        "psij,psif->psjf", far_blocks, returned, preferred_element_type=jnp.float32
    )
    far_back = far_back * live_mask[:, :, None, None].astype(jnp.float32)
    wide = wide.at[blocks + far_c.reshape(-1)].add(far_back.reshape(-1, tile_size, feat_width))
    stacked = wide.reshape(3, block_rows, feat_width)
    from_next = passed_along(stacked[0].astype(jnp.bfloat16), "node", -1).astype(jnp.float32)
    from_prev = passed_along(stacked[2].astype(jnp.bfloat16), "node", 1).astype(jnp.float32)
    combined = stacked[1] + from_next + from_prev
    own_grad = lax.psum_scatter(
        combined.astype(jnp.bfloat16), "feat", scatter_dimension=0, tiled=True
    ).astype(jnp.float32)
    grad_features = own_grad + self_back
    return (layer_out, grad_features, grad_self, grad_neigh)


def solution(mesh):
    placed = (
        P(("grp", "node"), None),
        P(("grp", "node", "feat"), None),
        P(("grp", "node", "feat"), None, None, None),
        P(("grp", "node"), "feat", None, None),
        P(("grp", "node"), "feat", None, None),
        P(("grp", "node"), "feat", None),
        P(("grp", "node"), "feat", None, None, None, None),
        P(("grp", "node", "feat")),
        P(),
        P(),
        P(("grp", "node", "feat"), None),
    )
    return jax.shard_map(
        shards,
        mesh=mesh,
        in_specs=placed,
        out_specs=(
            P(("grp", "node", "feat"), None),
            P(("grp", "node", "feat"), None),
            P("grp", None),
            P("grp", None),
        ),
        check_vma=False,
    )
```

profile of v0, /device:TPU:0, one launch (start us, length us, event | category | flops | bytes accessed | tf_op | source)
XLA Modules:
  0.0 341.7 jit_solution(10213638800736339229)
XLA Ops:
  8.0 0.5 collective-permute-start
  8.5 2.0 collective-permute-start.1
  10.5 1.3 copy.54
  11.9 3.5 %all-to-all-start = ((s32[4,1,3]{2,1,0:T(1,128)}), s32[4,1,3]{2,1,0:T(1,128)S(1)}, u32[]{:S(2)}, u32[]{:S(2)}) async-start(s32[4,1,3]{2,1,0:T(1,128)} %copy.54), calls=%async_computation | async-start | bytes 4096 | tf_op jit(solution)/shard_map/all_to_all | solution.py:70
  15.4 0.7 compare_select_fusion
  16.1 0.8 reshape.250
  16.8 0.7 compare_select_fusion.2
  17.5 0.7 broadcast_add_fusion.1
  18.2 0.1 copy.55
  18.3 0.1 reshape.265
  18.4 0.1 reshape.257
  18.5 0.1 copy.61
  18.6 0.1 add.127
  18.6 0.1 copy.62
  18.7 0.1 add.130
  18.8 2.2 gather_fusion.1
  21.0 0.7 fusion.21
  21.8 2.3 fusion.15
  24.1 2.6 fusion.11
  26.7 30.2 %all-to-all-done = s32[4,1,3]{2,1,0:T(1,128)S(1)} async-done(((s32[4,1,3]{2,1,0:T(1,128)}), s32[4,1,3]{2,1,0:T(1,128)S(1)}, u32[]{:S(2)}, u32[]{:S(2)}) %all-to-all-start) | async-done | bytes 80 | tf_op jit(solution)/shard_map/all_to_all | solution.py:70
  56.9 3.6 %all-to-all-start.1 = ((bf16[4,3,128,256]{2,3,1,0:T(8,128)(2,1)}), bf16[4,3,128,256]{2,3,1,0:T(8,128)(2,1)S(1)}, u32[]{:S(2)}, u32[]{:S(2)}) async-start(bf16[4,3,128,256]{2,3,1,0:T(8,128)(2,1)} %fusion.11), calls=%async_computation.1 | async-start | bytes 1572864 | tf_op jit(solution)/shard_map/all_to_all | solution.py:69
  60.5 0.5 broadcast.167
  61.0 0.7 reduce.3
  61.7 0.1 reshape.246
  61.7 0.1 copy.63
  61.8 0.1 copy.64
  61.9 0.1 reshape.273
  62.0 10.2 %all-to-all-done.1 = bf16[4,3,128,256]{2,3,1,0:T(8,128)(2,1)S(1)} async-done(((bf16[4,3,128,256]{2,3,1,0:T(8,128)(2,1)}), bf16[4,3,128,256]{2,3,1,0:T(8,128)(2,1)S(1)}, u32[]{:S(2)}, u32[]{:S(2)}) %all-to-all-start.1) | async-done | bytes 786464 | tf_op jit(solution)/shard_map/all_to_all | solution.py:69
  72.2 1.4 bitcast_convert_fusion
  73.6 3.0 copy.58
  76.7 16.6 %pad_maximum_fusion = bf16[12288,256]{1,0:T(8,128)(2,1)} fusion(bf16[4096,256]{1,0:T(8,128)(2,1)} %collective-permute-done.1, bf16[4096,256]{1,0:T(8,128)(2,1)S(1)} %copy-done.2, bf16[4096,256]{1,0:T(8,128)(2,1)} %collective-permute-done), kind=kLoop, calls=%fused_computation.6 | loop fusion | flops 18874368 | bytes 12582912 | tf_op jit(solution)/shard_map/concatenate | solution.py:18
  93.2 9.4 %gather_fusion = bf16[128,128,256]{2,1,0:T(8,128)(2,1)} fusion(bf16[96,128,256]{2,1,0:T(8,128)(2,1)} %bitcast.76, s32[1024]{0:T(1024)S(1)} %pad_clamp_fusion.2), kind=kCustom, calls=%fused_computation | custom fusion | bytes 16777728 | tf_op jit(solution)/shard_map/gather | solution.py:53
  102.6 9.6 %fusion.6 = f32[8,128,256]{1,2,0:T(8,128)} fusion(bf16[8,16,128,256]{3,2,1,0:T(8,128)(2,1)} %bitcast.77, s32[8,16,128,128]{3,2,1,0:T(8,128)} %param.13), kind=kOutput, calls=%fused_computation.16 | convolution fusion | flops 1075838976 | bytes 17825792 | tf_op jit(solution)/shard_map/tsij,tsjf->tif/dot_general | solution.py:55
  112.3 1.6 copy.57
  113.8 2.0 scatter_fusion
  115.8 0.2 fusion.12
  116.1 3.0 multiply_convert_fusion
  119.1 0.8 copy-done.4
  119.9 0.3 fusion.9
  120.2 0.6 gather_fusion.2
  120.9 1.2 copy.65
  122.0 3.5 %all-to-all-start.2 = ((bf16[4,3,128,256]{2,3,1,0:T(8,128)(2,1)}), bf16[4,3,128,256]{2,3,1,0:T(8,128)(2,1)S(1)}, u32[]{:S(2)}, u32[]{:S(2)}) async-start(bf16[4,3,128,256]{2,3,1,0:T(8,128)(2,1)} %bitcast.22), calls=%async_computation.2 | async-start | bytes 1572864 | tf_op jit(solution)/shard_map/all_to_all | solution.py:103
  125.5 0.0 all-reduce.3.cloned.1.call-start
  125.6 11.5 %fusion.2 = f32[8,256,16,128]{3,1,2,0:T(8,128)} fusion(bf16[8,128,256,1]{2,1,3,0:T(8,128)(2,1)S(1)} %bitcast.81, s32[8,16,128,128]{3,2,1,0:T(8,128)} %param.13), kind=kOutput, calls=%fused_computation.10 | convolution fusion | flops 1075838976 | bytes 25690112 | tf_op jit(solution)/shard_map/tsij,tif->tsjf/dot_general | solution.py:97
  137.1 17.5 %copy.60 = f32[128,128,256]{2,1,0:T(8,128)} copy(f32[128,128,256]{1,2,0:T(8,128)} %bitcast.75) | data formatting | bytes 33554432 | tf_op jit(solution)/shard_map/reshape | solution.py:101
  154.5 6.1 %broadcast_in_dim.5 = f32[96,128,256]{2,1,0:T(8,128)} broadcast(f32[]{:T(128)} %constant.19.clone.1), dimensions={} | broadcast | bytes 12582916 | tf_op jit(solution)/shard_map/broadcast_in_dim | solution.py:100
  160.6 38.6 %scatter_fusion.1 = f32[96,128,256]{2,1,0:T(8,128)} fusion(f32[96,128,256]{2,1,0:T(8,128)} %broadcast_in_dim.5, s32[128]{0:T(128)S(1)} %fusion.24, f32[128,128,256]{2,1,0:T(8,128)} %copy.60), kind=kCustom, calls=%fused_computation.4 | custom fusion | flops 4194304 | bytes 50332160 | tf_op jit(solution)/shard_map/scatter-add | solution.py:101
  199.2 1.5 convolution_multiply_fusion
  200.7 0.5 copy.66
  201.2 4.1 %scatter_fusion.2 = f32[96,128,256]{2,1,0:T(8,128)} fusion(f32[96,128,256]{2,1,0:T(8,128)} %scatter_fusion.1, s32[12]{0:T(128)S(1)} %fusion.25, f32[12,128,256]{2,1,0:T(8,128)S(1)} %copy.66), kind=kCustom, calls=%fused_computation.5 | custom fusion | flops 393216 | bytes 4718640 | tf_op jit(solution)/shard_map/scatter-add | solution.py:108
  205.3 5.5 %convert.5 = bf16[96,128,256]{2,1,0:T(8,128)(2,1)S(1)} convert(f32[96,128,256]{2,1,0:T(8,128)} %scatter_fusion.2) | non-fusion elementwise | flops 3145728 | bytes 18874368 | tf_op jit(solution)/shard_map/convert.2
  210.8 2.3 fusion.28
  213.1 1.8 collective-permute-start.2
  215.0 2.1 fusion.13
  217.1 1.0 fusion.30
  218.1 0.0 reduce-scatter.2.cloned.1.call-start
  218.2 2.6 slice.23
  220.8 42.2 %collective-permute-done.2 = bf16[4096,256]{1,0:T(8,128)(2,1)S(1)} collective-permute-done((bf16[4096,256]{1,0:T(8,128)(2,1)}, bf16[4096,256]{1,0:T(8,128)(2,1)S(1)}, u32[]{:S(2)}, u32[]{:S(2)}) %collective-permute-start.2) | collective-permute-done | bytes 2097184 | tf_op jit(solution)/shard_map/ppermute | solution.py:25
  263.0 1.1 collective-permute-done.3
  264.2 3.8 %fusion.1 = bf16[4096,256]{1,0:T(8,128)(2,1)} fusion(f32[32,128,256]{2,1,0:T(8,128)S(1)} %slice.23, bf16[4096,256]{1,0:T(8,128)(2,1)} %collective-permute-done.3, bf16[4096,256]{1,0:T(8,128)(2,1)S(1)} %collective-permute-done.2), kind=kLoop, calls=%fused_computation.9 | loop fusion | flops 5242880 | bytes 10485760 | tf_op jit(solution)/shard_map/convert_element_type | solution.py:114
  268.0 0.3 fusion.29
  268.4 61.9 %all-reduce.3.cloned.1.call-done = (f32[256,256]{1,0:T(8,128)}, f32[256,256]{1,0:T(8,128)}) async-done(((f32[256,256]{1,0:T(8,128)}, f32[256,256]{1,0:T(8,128)}), (f32[256,256]{1,0:T(8,128)}, f32[256,256]{1,0:T(8,128)})) %all-reduce.3.cloned.1.call-update) | async-done | bytes 524304 | tf_op jit(solution)/shard_map/psum | solution.py:88
  330.2 1.9 broadcast_multiply_fusion
  332.1 2.1 convert_add_fusion
  (36 shorter events, 0.1 us)
Async XLA Ops:
  8.0 108.1 %copy-start = (bf16[256,256]{1,0:T(8,128)(2,1)S(1)}, bf16[256,256]{1,0:T(8,128)(2,1)}, u32[]{:S(2)}) copy-start(bf16[256,256]{1,0:T(8,128)(2,1)} %param.20) | copy-start | bytes 393220
  8.0 52.4 %copy-start.10 = (s32[1024]{0:T(1024)S(1)}, s32[1024]{0:T(1024)}, u32[]{:S(2)}) copy-start(s32[1024]{0:T(1024)} %param.18) | copy-start | bytes 12292
  8.0 68.6 %collective-permute-start = (bf16[4096,256]{1,0:T(8,128)(2,1)}, bf16[4096,256]{1,0:T(8,128)(2,1)}, u32[]{:S(2)}, u32[]{:S(2)}) collective-permute-start(bf16[4096,256]{1,0:T(8,128)(2,1)} %param.11), channel_id=1, source_target_pairs={{0,4},{4,8},{8,12},{12,0},{1,5},{5,9},{9,13},{13,1},{2,6},{6,10},{... | collective-permute-start | bytes 6291464 | tf_op jit(solution)/shard_map/ppermute | solution.py:16
  8.5 68.1 %collective-permute-start.1 = (bf16[4096,256]{1,0:T(8,128)(2,1)}, bf16[4096,256]{1,0:T(8,128)(2,1)}, u32[]{:S(2)}, u32[]{:S(2)}) collective-permute-start(bf16[4096,256]{1,0:T(8,128)(2,1)} %param.11), channel_id=1, source_target_pairs={{4,0},{8,4},{12,8},{0,12},{5,1},{9,5},{13,9},{1,13},{6,2},{10,6},{... | collective-permute-start | bytes 6291464 | tf_op jit(solution)/shard_map/ppermute | solution.py:17
  11.9 45.0 %all-to-all-start = ((s32[4,1,3]{2,1,0:T(1,128)}), s32[4,1,3]{2,1,0:T(1,128)S(1)}, u32[]{:S(2)}, u32[]{:S(2)}) async-start(s32[4,1,3]{2,1,0:T(1,128)} %copy.54), calls=%async_computation | async-start | bytes 4096 | tf_op jit(solution)/shard_map/all_to_all | solution.py:70
  24.1 52.6 %copy-start.2 = (bf16[4096,256]{1,0:T(8,128)(2,1)S(1)}, bf16[4096,256]{1,0:T(8,128)(2,1)}, u32[]{:S(2)}) copy-start(bf16[4096,256]{1,0:T(8,128)(2,1)} %param.11) | copy-start | bytes 6291460
  56.9 15.4 %all-to-all-start.1 = ((bf16[4,3,128,256]{2,3,1,0:T(8,128)(2,1)}), bf16[4,3,128,256]{2,3,1,0:T(8,128)(2,1)S(1)}, u32[]{:S(2)}, u32[]{:S(2)}) async-start(bf16[4,3,128,256]{2,3,1,0:T(8,128)(2,1)} %fusion.11), calls=%async_computation.1 | async-start | bytes 1572864 | tf_op jit(solution)/shard_map/all_to_all | solution.py:69
  102.6 11.2 %copy-start.3 = (f32[12,128,256]{2,1,0:T(8,128)S(1)}, f32[12,128,256]{2,1,0:T(8,128)}, u32[]{:S(2)}) copy-start(f32[12,128,256]{2,1,0:T(8,128)} %copy.58) | copy-start | bytes 4718596
  116.1 4.2 %copy-start.7 = (bf16[1024,256]{1,0:T(8,128)(2,1)}, bf16[1024,256]{1,0:T(8,128)(2,1)S(1)}, u32[]{:S(2)}) copy-start(bf16[1024,256]{1,0:T(8,128)(2,1)S(1)} %fusion.12) | copy-start | bytes 1572868
  119.1 0.8 copy-start.4
  122.0 77.2 %all-to-all-start.2 = ((bf16[4,3,128,256]{2,3,1,0:T(8,128)(2,1)}), bf16[4,3,128,256]{2,3,1,0:T(8,128)(2,1)S(1)}, u32[]{:S(2)}, u32[]{:S(2)}) async-start(bf16[4,3,128,256]{2,3,1,0:T(8,128)(2,1)} %bitcast.22), calls=%async_computation.2 | async-start | bytes 1572864 | tf_op jit(solution)/shard_map/all_to_all | solution.py:103
  125.5 204.7 %all-reduce.3.cloned.1.call-start = ((), (), s32[]{:S(2)}) async-start(), calls=%async_computation.5 | async-start | bytes 1048576 | tf_op jit(solution)/shard_map/psum | solution.py:88
  210.8 4.2 %copy-start.5 = (bf16[1024,256]{1,0:T(8,128)(2,1)S(1)}, bf16[1024,256]{1,0:T(8,128)(2,1)}, u32[]{:S(2)}) copy-start(bf16[1024,256]{1,0:T(8,128)(2,1)} %copy-done.4) | copy-start | bytes 1572868
  210.8 6.3 %copy-start.8 = (bf16[1024,256]{1,0:T(8,128)(2,1)S(1)}, bf16[1024,256]{1,0:T(8,128)(2,1)}, u32[]{:S(2)}) copy-start(bf16[1024,256]{1,0:T(8,128)(2,1)} %copy-done.7) | copy-start | bytes 1572868
  213.1 49.9 %collective-permute-start.2 = (bf16[4096,256]{1,0:T(8,128)(2,1)}, bf16[4096,256]{1,0:T(8,128)(2,1)S(1)}, u32[]{:S(2)}, u32[]{:S(2)}) collective-permute-start(bf16[4096,256]{1,0:T(8,128)(2,1)} %bitcast.26), channel_id=1, source_target_pairs={{4,0},{8,4},{12,8},{0,12},{5,1},{9,5},{13,9},{1,13},{6,2},{10,6},{... | collective-permute-start | bytes 6291464 | tf_op jit(solution)/shard_map/ppermute | solution.py:25
  215.0 49.2 %collective-permute-start.3 = (bf16[4096,256]{1,0:T(8,128)(2,1)}, bf16[4096,256]{1,0:T(8,128)(2,1)}, u32[]{:S(2)}, u32[]{:S(2)}) collective-permute-start(bf16[4096,256]{1,0:T(8,128)(2,1)} %bitcast.27), channel_id=1, source_target_pairs={{12,0},{0,4},{4,8},{8,12},{13,1},{1,5},{5,9},{9,13},{14,2},{2,6},{... | collective-permute-start | bytes 6291464 | tf_op jit(solution)/shard_map/ppermute | solution.py:25
  218.1 114.0 %reduce-scatter.2.cloned.1.call-start = ((), (), s32[]{:S(2)}) async-start(), calls=%async_computation.4 | async-start | bytes 2621440 | tf_op jit(solution)/shard_map/reduce_scatter | solution.py:113
  220.8 47.2 %copy-start.6 = (bf16[1024,256]{1,0:T(8,128)(2,1)S(1)}, bf16[1024,256]{1,0:T(8,128)(2,1)}, u32[]{:S(2)}) copy-start(bf16[1024,256]{1,0:T(8,128)(2,1)} %copy-done.4) | copy-start | bytes 1572868
  220.8 47.2 %copy-start.9 = (bf16[256,256]{1,0:T(8,128)(2,1)S(1)}, bf16[256,256]{1,0:T(8,128)(2,1)}, u32[]{:S(2)}) copy-start(bf16[256,256]{1,0:T(8,128)(2,1)} %param.19) | copy-start | bytes 393220
  264.2 70.0 %copy-start.1 = (bf16[256,256]{1,0:T(8,128)(2,1)S(1)}, bf16[256,256]{1,0:T(8,128)(2,1)}, u32[]{:S(2)}) copy-start(bf16[256,256]{1,0:T(8,128)(2,1)} %param.20) | copy-start | bytes 393220
Sparse Core Ops, SparseCore 0:
  218.2 111.9 all-reduce.2
Sparse Core Ops, SparseCore 1:
  268.1 45.6 reduce-scatter.1
where the time goes:
time: 343 us; the launch traced here: 342 us
  waiting for transfers between devices  146 us (43%)
  other arithmetic  79.6 us (23%)
  local copies, waits for them, and re-layouts  51.3 us (15%)
  matrix products  34.3 us (10%)
  between operations  15.7 us (5%)
  starting transfers between devices  15 us (4%)
    psum x1, waiting for transfers between devices, shards(): sum_self, sum_neigh = lax.psum((part_self, part_neigh), ('node', 'feat'))  61.9 us
    ppermute x2, waiting for transfers between devices, passed_along(): return lax.ppermute(block, axis, route)  43.4 us
    scatter-add x1, other arithmetic, shards(): wide.at[band_cols.reshape(-1)]  38.6 us
    all_to_all x1, waiting for transfers between devices, shards(): lax.all_to_all(far_r, 'node', split_axis=0, concat_axis=0, tiled=True)  30.2 us
    reshape x1, local copies, waits for them, and re-layouts, shards(): spread.reshape(-1, tile_size, feat_width)  17.5 us
    concatenate x1, other arithmetic, padded(): array = jnp.concatenate([before, array, after], axis=dim)  16.6 us
    dot_general x1, matrix products, shards(): jnp.einsum('tsij,tif->tsjf', band_blocks, back_tiles, preferred_element_t...  11.5 us
    all_to_all x1, waiting for transfers between devices, shards(): lax.all_to_all(partial_value, 'node', split_axis=0, concat_axis=0, tiled=...  10.2 us
  transfers between devices with their start and end apart: 9, of which 5 were waited for; matrix products, arithmetic and copies ran while one was open for 30% of the time, Pallas kernels for 0%

commit v1 on v0

v1 whole, which is shorter than its diff:
```python
import functools
import math

import jax
import jax.numpy as jnp
from jax import lax
from jax.experimental import pallas as pl
from jax.experimental.pallas import tpu as pltpu
from jax.sharding import PartitionSpec as P

F32 = jnp.float32
BF16 = jnp.bfloat16


def outer(a, b):
    return lax.dot_general(a, b, (((0,), (0,)), ((), ())), preferred_element_type=F32)


def times_t(a, b):
    return lax.dot_general(a, b, (((1,), (1,)), ((), ())), preferred_element_type=F32)


def far_kernel(slots, cols, live, feat_ref, adj_ref, out_ref):
    p = pl.program_id(0)
    for s in range(slots):
        value = jnp.dot(
            adj_ref[0, s].astype(BF16), feat_ref[cols[p, s]], preferred_element_type=F32
        )
        out_ref[0, s] = jnp.where(s < live[p], value, 0.0).astype(BF16)


def main_kernel(
    dims,
    cols,
    rows,
    spot,
    own_hbm,
    in_hbm,
    *rest,
):
    blocks, slots, n_cross, n_feat, n_far, n_parts = dims
    cross_hbm, rest = rest[:n_cross], rest[n_cross:]
    part_refs, rest = rest[:n_parts], rest[n_parts:]
    adj_ref, deg_ref, ws_ref, wn_ref, go_ref = rest[:5]
    rest = rest[5:]
    out_ref, self_ref, gs_ref, gn_ref, own_ref, in_ref = rest[:6]
    rest = rest[6:]
    cross_refs, rest = rest[:n_feat], rest[n_feat:]
    send_refs, rest = rest[:n_parts], rest[n_parts:]
    ext, wide, back, acc, sems = rest
    t = pl.program_id(0)
    last = pl.num_programs(0) - 1
    sub = blocks // n_feat

    @pl.when(t == 0)
    def _():
        moves = [
            pltpu.make_async_copy(own_hbm, ext.at[pl.ds(0, blocks)], sems.at[0]),
            pltpu.make_async_copy(in_hbm, ext.at[pl.ds(blocks, blocks)], sems.at[1]),
        ]
        each = blocks // n_cross
        for i, ref in enumerate(cross_hbm):
            moves.append(
                pltpu.make_async_copy(ref, ext.at[pl.ds(2 * blocks + i * each, each)], sems.at[2 + i])
            )
        for move in moves:
            move.start()
        wide[...] = jnp.zeros_like(wide)
        gs_ref[...] = jnp.zeros_like(gs_ref)
        gn_ref[...] = jnp.zeros_like(gn_ref)
        for move in moves:
            move.wait()

    adj = [adj_ref[0, s].astype(BF16) for s in range(slots)]
    near = None
    for s in range(0, slots, 2):
        left = jnp.concatenate([adj[s], adj[s + 1]], axis=1)
        right = jnp.concatenate([ext[cols[t, s]], ext[cols[t, s + 1]]], axis=0)
        term = jnp.dot(left, right, preferred_element_type=F32)
        near = term if near is None else near + term
    acc[...] = near
    for k, ref in enumerate(part_refs):
        for s in range(n_far):

            @pl.when(rows[k, s] == t)
            def _():
                acc[...] += ref[s].astype(F32)

    deg = jnp.broadcast_to(deg_ref[0].astype(F32), (deg_ref.shape[2], deg_ref.shape[2])).T
    deg = jnp.concatenate([deg, deg], axis=1)
    agg = (acc[...] / deg).astype(BF16)
    mine = ext[spot[0] + t]
    pre = jnp.dot(mine, ws_ref[...], preferred_element_type=F32) + jnp.dot(
        agg, wn_ref[...], preferred_element_type=F32
    )
    sig = jax.nn.sigmoid(pre)
    out_ref[...] = (pre * sig).astype(BF16)
    gz = (go_ref[...].astype(F32) * (sig * (1.0 + pre * (1.0 - sig)))).astype(BF16)
    gs_ref[...] += outer(mine, gz)
    gn_ref[...] += outer(agg, gz)
    bk = (times_t(gz, wn_ref[...]) / deg).astype(BF16)
    self_ref[...] = times_t(gz, ws_ref[...])
    back[t] = bk
    for s in range(slots):
        wide[cols[t, s]] += outer(adj[s], bk)

    @pl.when(t == last)
    def _():
        own_ref[...] = wide[pl.ds(0, blocks)]
        in_ref[...] = wide[pl.ds(blocks, blocks)].astype(BF16)
        for d in range(n_feat):
            cross_refs[d][...] = wide[pl.ds(spot[1 + d], sub)].astype(BF16)
        for k in range(n_parts):
            for s in range(n_far):
                send_refs[k][s] = back[rows[k, s]]


def join_kernel(slots, n_parts, cols, live, own_ref, in_ref, adj_ref, *rest):
    ret_refs, out_ref = rest[:n_parts], rest[n_parts]
    out_ref[...] = own_ref[...] + in_ref[...].astype(F32)
    for k in range(n_parts):
        for s in range(slots):

            @pl.when(s < live[k])
            def _():
                out_ref[cols[k, s]] += outer(adj_ref[k, s].astype(BF16), ret_refs[k][s])


def shards(
    features,
    band_cols,
    band_adj,
    far_cols,
    far_rows,
    far_live,
    far_adj,
    degree,
    w_self,
    w_neigh,
    grad_out,
):
    block_rows, width = features.shape
    sub_tiles, slots, tile, _ = band_adj.shape
    hidden = w_self.shape[1]
    blocks = block_rows // tile
    n_feat = lax.axis_size("feat")
    n_node = lax.axis_size("node")
    far_slots = far_adj.shape[3]
    sub_rows = sub_tiles * tile
    half = blocks // 2
    node = lax.axis_index("node")
    member = lax.axis_index("feat")
    h = member % 2
    even = node % 2 == 0
    in_pairs = [(i, i ^ 1) for i in range(n_node)]
    cross_of = [(i + 1) % n_node if i % 2 else (i - 1) % n_node for i in range(n_node)]
    cross_pairs = list(enumerate(cross_of))
    feat_pairs = [(i, i ^ 1) for i in range(n_feat)]

    def dist(k):
        return [(i, (i + k) % n_node) for i in range(n_node)]

    tiles = features.reshape(blocks, tile, width)
    order = (node + jnp.arange(n_node, dtype=jnp.int32)) % n_node
    far_c = far_cols.reshape(n_node, far_slots)[order]
    far_r = far_rows.reshape(n_node, far_slots)[order]
    live = far_live.reshape(n_node)[order]
    fadj = far_adj.reshape(n_node, far_slots, tile, tile)
    got_rows = [far_r[0]] + [lax.ppermute(far_r[k], "node", dist(k)) for k in range(1, n_node)]
    rows = jnp.stack(got_rows)

    from_in = lax.ppermute(tiles, "node", in_pairs)
    n_pieces = 2
    each = half // n_pieces
    direct, relayed = [], []
    for i in range(n_pieces):
        piece = lax.dynamic_slice_in_dim(tiles, h * half + i * each, each, 0)
        direct.append(lax.ppermute(piece, "node", cross_pairs))
    for piece in direct:
        relayed.append(lax.ppermute(piece, "feat", feat_pairs))

    far_fn = pl.pallas_call(
        lambda c, l, o, f, a, out: far_kernel(far_slots, c, l, f, a, out),
        out_shape=jax.ShapeDtypeStruct((n_node, far_slots, tile, width), BF16),
        grid_spec=pltpu.PrefetchScalarGridSpec(
            num_scalar_prefetch=3,
            grid=(n_node,),
            in_specs=[
                pl.BlockSpec((blocks, tile, width), lambda p, c, l, o: (0, 0, 0)),
                pl.BlockSpec((1, far_slots, tile, tile), lambda p, c, l, o: (o[p], 0, 0, 0)),
            ],
            out_specs=pl.BlockSpec((1, far_slots, tile, width), lambda p, c, l, o: (p, 0, 0, 0)),
        ),
        compiler_params=pltpu.CompilerParams(vmem_limit_bytes=32 * 1024 * 1024),
        name="far_partial",
    )
    parts = far_fn(far_c, live, order, tiles, fadj)
    got = [parts[0]] + [lax.ppermute(parts[k], "node", dist(k)) for k in range(1, n_node)]

    kind, local = band_cols // blocks, band_cols % blocks
    is_in = kind == jnp.where(even, 2, 0)
    cross_place = 2 * blocks + ((local // half) ^ h) * half + local % half
    place = jnp.where(kind == 1, local, jnp.where(is_in, blocks + local, cross_place))
    spots = [member * sub_tiles]
    for d in range(n_feat):
        first = (member ^ d) * sub_tiles
        spots.append(2 * blocks + ((first // half) ^ h) * half + first % half)
    spot = jnp.stack(spots).astype(jnp.int32)

    cross_in = direct + relayed
    n_cross = len(cross_in)
    vmem = lambda shape: pl.BlockSpec(shape, lambda t, *_: (0,) * len(shape))
    any_spec = pl.BlockSpec(memory_space=pl.ANY)
    far_shape = (far_slots, tile, width)
    dims = (blocks, slots, n_cross, n_feat, far_slots, n_node)
    results = pl.pallas_call(
        functools.partial(main_kernel, dims),
        out_shape=[
            jax.ShapeDtypeStruct((sub_rows, hidden), BF16),
            jax.ShapeDtypeStruct((sub_rows, width), F32),
            jax.ShapeDtypeStruct((width, hidden), F32),
            jax.ShapeDtypeStruct((width, hidden), F32),
            jax.ShapeDtypeStruct((blocks, tile, width), F32),
            jax.ShapeDtypeStruct((blocks, tile, width), BF16),
        ]
        + [jax.ShapeDtypeStruct((sub_tiles, tile, width), BF16)] * n_feat
        + [jax.ShapeDtypeStruct(far_shape, BF16)] * n_node,
        grid_spec=pltpu.PrefetchScalarGridSpec(
            num_scalar_prefetch=3,
            grid=(sub_tiles,),
            in_specs=[any_spec] * (2 + n_cross)
            + [vmem(far_shape)] * n_node
            + [
                pl.BlockSpec((1, slots, tile, tile), lambda t, *_: (t, 0, 0, 0)),
                pl.BlockSpec((1, 1, tile), lambda t, *_: (t, 0, 0)),
                vmem((width, hidden)),
                vmem((width, hidden)),
                pl.BlockSpec((tile, hidden), lambda t, *_: (t, 0)),
            ],
            out_specs=[
                pl.BlockSpec((tile, hidden), lambda t, *_: (t, 0)),
                pl.BlockSpec((tile, width), lambda t, *_: (t, 0)),
                vmem((width, hidden)),
                vmem((width, hidden)),
                vmem((blocks, tile, width)),
                vmem((blocks, tile, width)),
            ]
            + [vmem((sub_tiles, tile, width))] * n_feat
            + [vmem(far_shape)] * n_node,
            scratch_shapes=[
                pltpu.VMEM((3 * blocks, tile, width), BF16),
                pltpu.VMEM((3 * blocks, tile, width), F32),
                pltpu.VMEM((sub_tiles, tile, width), BF16),
                pltpu.VMEM((tile, width), F32),
                pltpu.SemaphoreType.DMA((2 + n_cross,)),
            ],
        ),
        compiler_params=pltpu.CompilerParams(vmem_limit_bytes=58 * 1024 * 1024),
        name="layer",
    )(
        place,
        rows,
        spot,
        tiles,
        from_in,
        *cross_in,
        *got,
        band_adj,
        degree.reshape(sub_tiles, 1, tile),
        w_self,
        w_neigh,
        grad_out,
    )
    layer_out, self_back, part_self, part_neigh, own_wide, in_wide = results[:6]
    cross_wide = results[6 : 6 + n_feat]
    send_back = results[6 + n_feat :]

    returned = [send_back[0]] + [
        lax.ppermute(send_back[k], "node", dist(n_node - k)) for k in range(1, n_node)
    ]
    in_terms = lax.ppermute(in_wide, "node", in_pairs)
    far_first = list(range(n_feat - 1, -1, -1))
    cross_terms = {d: lax.ppermute(cross_wide[d], "node", cross_pairs) for d in far_first}
    sum_self, sum_neigh = lax.psum((part_self, part_neigh), ("node", "feat"))
    grad_scale = 1.0 / math.sqrt(block_rows * n_node)

    base = pl.pallas_call(
        functools.partial(join_kernel, far_slots, n_node),
        out_shape=jax.ShapeDtypeStruct((blocks, tile, width), F32),
        in_specs=[pl.BlockSpec(memory_space=pltpu.SMEM)] * 2
        + [pl.BlockSpec(memory_space=pltpu.VMEM)] * (3 + n_node),
        out_specs=pl.BlockSpec(memory_space=pltpu.VMEM),
        compiler_params=pltpu.CompilerParams(vmem_limit_bytes=40 * 1024 * 1024),
        name="join",
    )(far_c, live, own_wide, in_terms, fadj[order], *returned)

    total = self_back
    for d in far_first:
        chunk = lax.dynamic_slice_in_dim(base, (member ^ d) * sub_tiles, sub_tiles, 0)
        chunk = (chunk + cross_terms[d].astype(F32)).astype(BF16)
        if d:
            chunk = lax.ppermute(chunk, "feat", [(i, i ^ d) for i in range(n_feat)])
        total = total + chunk.reshape(sub_rows, width).astype(F32)
    return (layer_out, total, sum_self * grad_scale, sum_neigh * grad_scale)


def solution(mesh):
    placed = (
        P(("grp", "node"), None),
        P(("grp", "node", "feat"), None),
        P(("grp", "node", "feat"), None, None, None),
        P(("grp", "node"), "feat", None, None),
        P(("grp", "node"), "feat", None, None),
        P(("grp", "node"), "feat", None),
        P(("grp", "node"), "feat", None, None, None, None),
        P(("grp", "node", "feat")),
        P(),
        P(),
        P(("grp", "node", "feat"), None),
    )
    return jax.shard_map(
        shards,
        mesh=mesh,
        in_specs=placed,
        out_specs=(
            P(("grp", "node", "feat"), None),
            P(("grp", "node", "feat"), None),
            P("grp", None),
            P("grp", None),
        ),
        check_vma=False,
    )
```

time: 343 us -> 266 us (0.78)
  other arithmetic: 79.6 us -> 8.38 us
  local copies, waits for them, and re-layouts: 51.3 us -> 11.6 us
  matrix products: 34.3 us -> 0 us
  waiting for transfers between devices: 146 us -> 180 us
  Pallas kernels: 0 us -> 27.4 us
  starting transfers between devices: 15 us -> 24.3 us
    psum x1, waiting for transfers between devices: 61.9 us -> 112 us  [shards(): sum_self, sum_neigh = lax.psum((part_self, part_neigh), ('node', 'feat'))]
    scatter-add x3 -> x0, other arithmetic: 44.7 us -> none  [the longest x1 38.6 us: shards(): wide.at[band_cols.reshape(-1)]]
    all_to_all x3 -> x0, waiting for transfers between devices: 40.4 us -> none  [the longest x1 30.2 us: shards(): lax.all_to_all(far_r, 'node', split_axis=0, concat_axis=0, tiled=True)]
    dot_general x10 -> x0, matrix products: 34.3 us -> none  [the longest x1 11.5 us: shards(): jnp.einsum('tsij,tif->tsjf', band_blocks, back_tiles, preferred_element_t...]
    pallas_call x0 -> x3, Pallas kernels: none -> 27.4 us  [the longest x1 22.6 us: shards(): pl.pallas_call(functools.partial(main_kernel, dims), out_shape=[jax.Shape...]
    ppermute x4 -> x22, waiting for transfers between devices: 43.4 us -> 67.8 us  [the longest x4 35.3 us: shards(): lax.ppermute(cross_wide[d], 'node', cross_pairs)]
    ppermute x4 -> x22, starting transfers between devices: 4.34 us -> 24.2 us  [the longest x4 5.59 us: shards(): lax.ppermute(cross_wide[d], 'node', cross_pairs)]
    reshape x4 -> x0, local copies, waits for them, and re-layouts: 18.8 us -> none  [the longest x1 17.5 us: shards(): spread.reshape(-1, tile_size, feat_width)]
  transfers between devices with their start and end apart: 9 -> 23, of which waited for: 5 -> 14; matrix products, arithmetic and copies ran while one was open for 30% -> 3% of each run, Pallas kernels for 0% -> 2%
where the time goes in v1:
time: 266 us
  waiting for transfers between devices  180 us (68%)
  Pallas kernels  27.4 us (10%)
  starting transfers between devices  24.3 us (9%)
  between operations  14.2 us (5%)
  local copies, waits for them, and re-layouts  11.6 us (4%)
  other arithmetic  8.38 us (3%)
    psum x1, waiting for transfers between devices, shards(): sum_self, sum_neigh = lax.psum((part_self, part_neigh), ('node', 'feat'))  112 us
    ppermute x4, waiting for transfers between devices, shards(): lax.ppermute(cross_wide[d], 'node', cross_pairs)  35.3 us
    pallas_call x1, Pallas kernels, shards(): pl.pallas_call(functools.partial(main_kernel, dims), out_shape=[jax.Shape...  22.6 us
    ppermute x2, waiting for transfers between devices, shards(): direct.append(lax.ppermute(piece, 'node', cross_pairs))  15.1 us
    ppermute x3, waiting for transfers between devices, shards(): lax.ppermute(send_back[k], 'node', dist(n_node - k))  6.26 us
    ppermute x3, waiting for transfers between devices, shards(): lax.ppermute(far_r[k], 'node', dist(k))  5.88 us
    ppermute x4, starting transfers between devices, shards(): lax.ppermute(cross_wide[d], 'node', cross_pairs)  5.59 us
    unnamed x36, local copies, waits for them, and re-layouts  5.51 us
  transfers between devices with their start and end apart: 23, of which 14 were waited for; matrix products, arithmetic and copies ran while one was open for 3% of the time, Pallas kernels for 2%

profile of v1, /device:TPU:0, one launch (start us, length us, event | category | flops | bytes accessed | tf_op | source)
XLA Modules:
  0.0 265.9 jit_solution(5451857469739926323)
XLA Ops:
  7.2 0.0 copy-start
  7.2 0.0 copy-start.1
  7.2 0.0 all-reduce.3.cloned.1.call-start
  7.2 0.5 collective-permute-start.3
  7.8 2.3 constant_dynamic-slice_fusion
  10.1 2.5 collective-permute-start.4
  12.6 0.0 collective-permute-start.5
  12.7 0.1 copy.18
  12.8 0.6 gather_fusion.1
  13.3 0.6 gather_fusion.2
  14.0 0.0 copy-start.3
  14.0 1.1 copy-done.3
  15.1 1.4 far_partial.1
  16.6 0.7 slice_bitcast_fusion
  17.3 1.7 collective-permute-start.10
  19.0 0.1 copy.17
  19.1 0.6 gather_fusion
  19.7 5.5 %collective-permute-done.4.rest_0_ = bf16[8,128,256]{2,1,0:T(8,128)(2,1)S(1)} collective-permute-done((bf16[8,128,256]{2,1,0:T(8,128)(2,1)}, bf16[8,128,256]{2,1,0:T(8,128)(2,1)S(1)}, u32[]{:S(2)}, u32[]{:S(2)}) %collective-permute-start.4) | collective-permute-done | bytes 524320 | tf_op jit(solution)/shard_map/ppermute | solution.py:178
  25.2 1.6 collective-permute-start.6
  26.8 9.5 %collective-permute-done.5.rest_1_ = bf16[8,128,256]{2,1,0:T(8,128)(2,1)S(1)} collective-permute-done((bf16[8,128,256]{2,1,0:T(8,128)(2,1)}, bf16[8,128,256]{2,1,0:T(8,128)(2,1)S(1)}, u32[]{:S(2)}, u32[]{:S(2)}) %collective-permute-start.5) | collective-permute-done | bytes 524320 | tf_op jit(solution)/shard_map/ppermute | solution.py:178
  36.3 1.4 collective-permute-start.7
  37.7 0.4 collective-permute-start
  38.2 2.5 collective-permute-done
  40.7 1.5 collective-permute-start.1
  42.2 2.0 collective-permute-done.1
  44.2 0.0 collective-permute-start.2
  44.2 1.3 collective-permute-done.2
  45.5 1.8 collective-permute-start.8
  47.4 0.5 collective-permute-start.9
  47.9 0.6 fusion.5.cols
  48.5 0.7 stack.39.spot
  49.2 0.5 pad_add_fusion.rows
  49.7 1.1 collective-permute-done.8.rest_5_
  50.8 4.2 %collective-permute-done.9.rest_6_ = bf16[3,128,256]{2,1,0:T(8,128)(2,1)S(1)} collective-permute-done((bf16[3,128,256]{2,1,0:T(8,128)(2,1)S(1)}, bf16[3,128,256]{2,1,0:T(8,128)(2,1)S(1)}, u32[]{:S(2)}, u32[]{:S(2)}) %collective-permute-start.9) | collective-permute-done | bytes 196640 | tf_op jit(solution)/shard_map/ppermute | solution.py:198
  55.1 0.0 collective-permute-done.6.rest_2_
  55.1 0.0 collective-permute-done.7.rest_3_
  55.1 0.6 copy-done.13
  55.8 0.2 copy-done.9
  55.9 0.2 copy-done.10
  56.1 22.6 %layer.1 = (bf16[1024,256]{1,0:T(8,128)(2,1)}, f32[1024,256]{1,0:T(8,128)}, f32[256,256]{1,0:T(8,128)}, f32[256,256]{1,0:T(8,128)}, f32[32,128,256]{2,1,0:T(8,12...) custom-call(s32[8,16]{1,0:T(8,128)} %fusion.5.cols, ...), custom_call_target="tpu_custom_call" | custom-call | tf_op jit(solution)/shard_map/layer/pallas_call | solution.py:216
  78.8 0.1 collective-permute-start.11
  78.8 1.0 collective-permute-start.12
  79.8 1.2 collective-permute-start.13
  81.0 1.7 collective-permute-start.15
  82.7 2.7 %collective-permute-done.12.rest_1_ = bf16[3,128,256]{2,1,0:T(8,128)(2,1)S(1)} collective-permute-done((bf16[3,128,256]{2,1,0:T(8,128)(2,1)}, bf16[3,128,256]{2,1,0:T(8,128)(2,1)S(1)}, u32[]{:S(2)}, u32[]{:S(2)}) %collective-permute-start.12) | collective-permute-done | bytes 196640 | tf_op jit(solution)/shard_map/ppermute | solution.py:279
  85.4 2.1 collective-permute-start.17
  87.5 3.6 %collective-permute-done.13.rest_2_ = bf16[3,128,256]{2,1,0:T(8,128)(2,1)S(1)} collective-permute-done((bf16[3,128,256]{2,1,0:T(8,128)(2,1)}, bf16[3,128,256]{2,1,0:T(8,128)(2,1)S(1)}, u32[]{:S(2)}, u32[]{:S(2)}) %collective-permute-start.13) | collective-permute-done | bytes 196640 | tf_op jit(solution)/shard_map/ppermute | solution.py:279
  91.1 1.7 collective-permute-start.21
  92.8 0.6 gather_fusion.3
  93.5 2.2 copy-done.2
  95.7 0.9 copy-done.5
  96.6 3.4 %join.1 = f32[32,128,256]{2,1,0:T(8,128)S(1)} custom-call(s32[4,3]{1,0:T(4,128)S(1)} %gather_fusion.1, s32[4]{0:T(128)S(1)} %gather_fusion.2, f32[32,128,256]{2,1,0:T(8,128)S(1)} %copy-done.2, bf16[32,128,256]{2,1,0:T(8,128)(2,1)} %collective-permute-done.11.in_ref, s32[4,3,128,128]{3,2,1,0:T(8,128)S(1)} %gather_fusion.3, ...), custom_call_target="tpu_custom_call" | custom-call | tf_op jit(solution)/shard_map/join/pallas_call | solution.py:287
  99.9 1.5 collective-permute-done.15
  101.4 11.2 %collective-permute-done.17 = bf16[8,128,256]{2,1,0:T(8,128)(2,1)S(1)} collective-permute-done((bf16[8,128,256]{2,1,0:T(8,128)(2,1)}, bf16[8,128,256]{2,1,0:T(8,128)(2,1)S(1)}, u32[]{:S(2)}, u32[]{:S(2)}) %collective-permute-start.17) | collective-permute-done | bytes 524320 | tf_op jit(solution)/shard_map/ppermute | solution.py:283
  112.7 11.3 %collective-permute-done.19 = bf16[8,128,256]{2,1,0:T(8,128)(2,1)} collective-permute-done((bf16[8,128,256]{2,1,0:T(8,128)(2,1)}, bf16[8,128,256]{2,1,0:T(8,128)(2,1)}, u32[]{:S(2)}, u32[]{:S(2)}) %collective-permute-start.19) | collective-permute-done | bytes 524320 | tf_op jit(solution)/shard_map/ppermute | solution.py:283
  124.0 11.2 %collective-permute-done.21 = bf16[8,128,256]{2,1,0:T(8,128)(2,1)} collective-permute-done((bf16[8,128,256]{2,1,0:T(8,128)(2,1)}, bf16[8,128,256]{2,1,0:T(8,128)(2,1)}, u32[]{:S(2)}, u32[]{:S(2)}) %collective-permute-start.21) | collective-permute-done | bytes 524320 | tf_op jit(solution)/shard_map/ppermute | solution.py:283
  135.2 3.0 %add_convert_fusion.3 = (bf16[8,128,256]{2,1,0:T(8,128)(2,1)}, bf16[8,128,256]{2,1,0:T(8,128)(2,1)S(1)}, bf16[8,128,256]{2,1,0:T(8,128)(2,1)S(1)}, bf16[8,128,256]{2,1,0:T(8,128)(2,1)}) fusion(bf16[8,128,256]{2,1,0:T(8,128)(2,1)S(1)} %collective-permute-done.15, f32[32,128,256]{2,1,0:T(8,128)S(1)} %join.1, s32[]{:T(128)S(6)} %select_n.129, ...), kind=kLoop, calls=%fused_computation.11 | loop fusion | flops 3145728 | bytes 8388624 | tf_op jit(solution)/shard_map/convert_element_type | solution.py:300
  138.2 2.5 collective-permute-start.16
  140.7 0.1 collective-permute-start.18
  140.8 1.8 collective-permute-start.20
  142.6 0.0 all-reduce.3.cloned.1.call-update
  142.7 112.2 %all-reduce.3.cloned.1.call-done = (f32[256,256]{1,0:T(8,128)}, f32[256,256]{1,0:T(8,128)}) async-done(((f32[256,256]{1,0:T(8,128)}, f32[256,256]{1,0:T(8,128)}), (f32[256,256]{1,0:T(8,128)}, f32[256,256]{1,0:T(8,128)})) %all-reduce.3.cloned.1.call-update) | async-done | bytes 524304 | tf_op jit(solution)/shard_map/psum | solution.py:284
  254.9 1.9 broadcast_multiply_fusion
  256.7 2.4 convert_add_fusion
  (38 shorter events, 0.1 us)
Async XLA Ops:
  7.2 6.2 %copy-start = (s32[1,1,4]{2,1,0:T(1,128)S(1)}, s32[1,1,4]{2,1,0:T(1,128)}, u32[]{:S(2)}) copy-start(s32[1,1,4]{2,1,0:T(1,128)} %param.16) | copy-start | bytes 52
  7.2 6.8 %copy-start.1 = (bf16[4096,256]{1,0:T(8,128)(2,1)S(1)}, bf16[4096,256]{1,0:T(8,128)(2,1)}, u32[]{:S(2)}) copy-start(bf16[4096,256]{1,0:T(8,128)(2,1)} %param.11) | copy-start | bytes 6291460
  7.2 5.5 %copy-start.15 = (s32[1,1,4,3]{2,1,3,0:T(1,128)S(1)}, s32[1,1,4,3]{2,1,3,0:T(1,128)}, u32[]{:S(2)}) copy-start(s32[1,1,4,3]{2,1,3,0:T(1,128)} %param.14) | copy-start | bytes 148
  7.2 247.7 %all-reduce.3.cloned.1.call-start = ((), (), s32[]{:S(2)}) async-start(), calls=%async_computation | async-start | bytes 1048576 | tf_op jit(solution)/shard_map/psum | solution.py:284
  7.2 47.8 %collective-permute-start.3 = (bf16[32,128,256]{2,1,0:T(8,128)(2,1)}, bf16[32,128,256]{2,1,0:T(8,128)(2,1)}, u32[]{:S(2)}, u32[]{:S(2)}) collective-permute-start(bf16[32,128,256]{2,1,0:T(8,128)(2,1)} %bitcast.43), channel_id=1, source_target_pairs={{0,4},{4,0},{8,12},{12,8},{1,5},{5,1},{9,13},{13,9},{2,6},{6,2},{1... | collective-permute-start | bytes 6291464 | tf_op jit(solution)/shard_map/ppermute | solution.py:172
  10.1 15.1 %collective-permute-start.4 = (bf16[8,128,256]{2,1,0:T(8,128)(2,1)}, bf16[8,128,256]{2,1,0:T(8,128)(2,1)S(1)}, u32[]{:S(2)}, u32[]{:S(2)}) collective-permute-start(bf16[8,128,256]{2,1,0:T(8,128)(2,1)} %get-tuple-element.39), channel_id=1, source_target_pairs={{0,12},{4,8},{8,4},{12,0},{1,13},{5,9},{9,5},{13,1},{2,14},{6,10},... | collective-permute-start | bytes 1572872 | tf_op jit(solution)/shard_map/ppermute | solution.py:178
  12.6 23.7 %collective-permute-start.5 = (bf16[8,128,256]{2,1,0:T(8,128)(2,1)}, bf16[8,128,256]{2,1,0:T(8,128)(2,1)S(1)}, u32[]{:S(2)}, u32[]{:S(2)}) collective-permute-start(bf16[8,128,256]{2,1,0:T(8,128)(2,1)} %get-tuple-element.38), channel_id=1, source_target_pairs={{0,12},{4,8},{8,4},{12,0},{1,13},{5,9},{9,5},{13,1},{2,14},{6,10},... | collective-permute-start | bytes 1572872 | tf_op jit(solution)/shard_map/ppermute | solution.py:178
  14.0 1.1 copy-start.3
  15.1 3.9 %copy-start.16 = (s32[1,1,4,3]{2,1,3,0:T(1,128)S(1)}, s32[1,1,4,3]{2,1,3,0:T(1,128)}, u32[]{:S(2)}) copy-start(s32[1,1,4,3]{2,1,3,0:T(1,128)} %param.15) | copy-start | bytes 148
  15.1 32.8 %copy-start.14 = (s32[8,16]{1,0:T(8,128)S(1)}, s32[8,16]{1,0:T(8,128)}, u32[]{:S(2)}) copy-start(s32[8,16]{1,0:T(8,128)} %param.12) | copy-start | bytes 1540
  17.3 30.0 %collective-permute-start.10 = (bf16[3,128,256]{2,1,0:T(8,128)(2,1)S(1)}, bf16[3,128,256]{2,1,0:T(8,128)(2,1)S(1)}, u32[]{:S(2)}, u32[]{:S(2)}) collective-permute-start(bf16[3,128,256]{2,1,0:T(8,128)(2,1)S(1)} %get-tuple-element.40), channel_id=1, source_target_pairs={{0,12},{4,0},{8,4},{12,8},{1,13},{5,1},{9,5},{13,9},{2,14},{6,2},{... | collective-permute-start | bytes 589832 | tf_op jit(solution)/shard_map/ppermute | solution.py:198
  25.2 30.5 %copy-start.7 = (bf16[8,128,256]{2,1,0:T(8,128)(2,1)}, bf16[8,128,256]{2,1,0:T(8,128)(2,1)S(1)}, u32[]{:S(2)}) copy-start(bf16[8,128,256]{2,1,0:T(8,128)(2,1)S(1)} %collective-permute-done.4.rest_0_) | copy-start | bytes 1572868
  25.2 29.9 %collective-permute-start.6 = (bf16[8,128,256]{2,1,0:T(8,128)(2,1)S(1)}, bf16[8,128,256]{2,1,0:T(8,128)(2,1)S(1)}, u32[]{:S(2)}, u32[]{:S(2)}) collective-permute-start(bf16[8,128,256]{2,1,0:T(8,128)(2,1)S(1)} %collective-permute-done.4.rest_0_), channel_id=1, source_target_pairs={{0,1},{1,0},{2,3},{3,2},{4,5},{5,4},{6,7},{7,6},{8,9},{9,8},{10,11... | collective-permute-start | bytes 1572872 | tf_op jit(solution)/shard_map/ppermute | solution.py:180
  36.3 19.4 %copy-start.8 = (bf16[8,128,256]{2,1,0:T(8,128)(2,1)}, bf16[8,128,256]{2,1,0:T(8,128)(2,1)S(1)}, u32[]{:S(2)}) copy-start(bf16[8,128,256]{2,1,0:T(8,128)(2,1)S(1)} %collective-permute-done.5.rest_1_) | copy-start | bytes 1572868
  36.3 18.7 %collective-permute-start.7 = (bf16[8,128,256]{2,1,0:T(8,128)(2,1)S(1)}, bf16[8,128,256]{2,1,0:T(8,128)(2,1)S(1)}, u32[]{:S(2)}, u32[]{:S(2)}) collective-permute-start(bf16[8,128,256]{2,1,0:T(8,128)(2,1)S(1)} %collective-permute-done.5.rest_1_), channel_id=1, source_target_pairs={{0,1},{1,0},{2,3},{3,2},{4,5},{5,4},{6,7},{7,6},{8,9},{9,8},{10,11... | collective-permute-start | bytes 1572872 | tf_op jit(solution)/shard_map/ppermute | solution.py:180
  37.7 3.0 %collective-permute-start = (s32[3]{0:T(128)S(1)}, s32[3]{0:T(128)S(1)}, u32[]{:S(2)}, u32[]{:S(2)}) collective-permute-start(s32[3]{0:T(128)S(1)} %get-tuple-element.46), channel_id=1, source_target_pairs={{0,4},{4,8},{8,12},{12,0},{1,5},{5,9},{9,13},{13,1},{2,6},{6,10},{... | collective-permute-start | bytes 44 | tf_op jit(solution)/shard_map/ppermute | solution.py:169
  40.7 3.5 %collective-permute-start.1 = (s32[3]{0:T(128)S(1)}, s32[3]{0:T(128)S(1)}, u32[]{:S(2)}, u32[]{:S(2)}) collective-permute-start(s32[3]{0:T(128)S(1)} %get-tuple-element.45), channel_id=1, source_target_pairs={{0,8},{4,12},{8,0},{12,4},{1,9},{5,13},{9,1},{13,5},{2,10},{6,14},... | collective-permute-start | bytes 44 | tf_op jit(solution)/shard_map/ppermute | solution.py:169
  44.2 1.3 collective-permute-start.2
  45.5 5.3 %collective-permute-start.8 = (bf16[3,128,256]{2,1,0:T(8,128)(2,1)S(1)}, bf16[3,128,256]{2,1,0:T(8,128)(2,1)S(1)}, u32[]{:S(2)}, u32[]{:S(2)}) collective-permute-start(bf16[3,128,256]{2,1,0:T(8,128)(2,1)S(1)} %get-tuple-element.42), channel_id=1, source_target_pairs={{0,4},{4,8},{8,12},{12,0},{1,5},{5,9},{9,13},{13,1},{2,6},{6,10},{... | collective-permute-start | bytes 589832 | tf_op jit(solution)/shard_map/ppermute | solution.py:198
  47.4 8.4 %copy-start.11 = (bf16[3,128,256]{2,1,0:T(8,128)(2,1)}, bf16[3,128,256]{2,1,0:T(8,128)(2,1)S(1)}, u32[]{:S(2)}) copy-start(bf16[3,128,256]{2,1,0:T(8,128)(2,1)S(1)} %collective-permute-done.10.rest_7_) | copy-start | bytes 589828
  47.4 7.7 %collective-permute-start.9 = (bf16[3,128,256]{2,1,0:T(8,128)(2,1)S(1)}, bf16[3,128,256]{2,1,0:T(8,128)(2,1)S(1)}, u32[]{:S(2)}, u32[]{:S(2)}) collective-permute-start(bf16[3,128,256]{2,1,0:T(8,128)(2,1)S(1)} %get-tuple-element.41), channel_id=1, source_target_pairs={{0,8},{4,12},{8,0},{12,4},{1,9},{5,13},{9,1},{13,5},{2,10},{6,14},... | collective-permute-start | bytes 589832 | tf_op jit(solution)/shard_map/ppermute | solution.py:198
  50.8 4.9 %copy-start.12 = (bf16[3,128,256]{2,1,0:T(8,128)(2,1)}, bf16[3,128,256]{2,1,0:T(8,128)(2,1)S(1)}, u32[]{:S(2)}) copy-start(bf16[3,128,256]{2,1,0:T(8,128)(2,1)S(1)} %collective-permute-done.8.rest_5_) | copy-start | bytes 589828
  55.1 0.7 copy-start.13
  55.1 0.9 copy-start.9
  55.1 1.1 copy-start.10
  56.1 36.7 %copy-start.4 = (s32[1,1,4,3,128,128]{5,4,3,2,1,0:T(8,128)S(1)}, s32[1,1,4,3,128,128]{5,4,3,2,1,0:T(8,128)}, u32[]{:S(2)}) copy-start(s32[1,1,4,3,128,128]{5,4,3,2,1,0:T(8,128)} %param.17) | copy-start | bytes 2359300
  78.8 14.7 %collective-permute-start.11 = (bf16[32,128,256]{2,1,0:T(8,128)(2,1)}, bf16[32,128,256]{2,1,0:T(8,128)(2,1)}, u32[]{:S(2)}, u32[]{:S(2)}) collective-permute-start(bf16[32,128,256]{2,1,0:T(8,128)(2,1)} %get-tuple-element.21), channel_id=1, source_target_pairs={{0,4},{4,0},{8,12},{12,8},{1,5},{5,1},{9,13},{13,9},{2,6},{6,2},{1... | collective-permute-start | bytes 6291464 | tf_op jit(solution)/shard_map/ppermute | solution.py:281
  78.8 6.6 %collective-permute-start.12 = (bf16[3,128,256]{2,1,0:T(8,128)(2,1)}, bf16[3,128,256]{2,1,0:T(8,128)(2,1)S(1)}, u32[]{:S(2)}, u32[]{:S(2)}) collective-permute-start(bf16[3,128,256]{2,1,0:T(8,128)(2,1)} %get-tuple-element.23), channel_id=1, source_target_pairs={{0,12},{4,0},{8,4},{12,8},{1,13},{5,1},{9,5},{13,9},{2,14},{6,2},{... | collective-permute-start | bytes 589832 | tf_op jit(solution)/shard_map/ppermute | solution.py:279
  79.8 11.3 %collective-permute-start.13 = (bf16[3,128,256]{2,1,0:T(8,128)(2,1)}, bf16[3,128,256]{2,1,0:T(8,128)(2,1)S(1)}, u32[]{:S(2)}, u32[]{:S(2)}) collective-permute-start(bf16[3,128,256]{2,1,0:T(8,128)(2,1)} %get-tuple-element.24), channel_id=1, source_target_pairs={{0,8},{4,12},{8,0},{12,4},{1,9},{5,13},{9,1},{13,5},{2,10},{6,14},... | collective-permute-start | bytes 589832 | tf_op jit(solution)/shard_map/ppermute | solution.py:279
  81.0 10.1 %collective-permute-start.14 = (bf16[3,128,256]{2,1,0:T(8,128)(2,1)}, bf16[3,128,256]{2,1,0:T(8,128)(2,1)S(1)}, u32[]{:S(2)}, u32[]{:S(2)}) collective-permute-start(bf16[3,128,256]{2,1,0:T(8,128)(2,1)} %get-tuple-element.25), channel_id=1, source_target_pairs={{0,4},{4,8},{8,12},{12,0},{1,5},{5,9},{9,13},{13,1},{2,6},{6,10},{... | collective-permute-start | bytes 589832 | tf_op jit(solution)/shard_map/ppermute | solution.py:279
  81.0 20.5 %collective-permute-start.15 = (bf16[8,128,256]{2,1,0:T(8,128)(2,1)}, bf16[8,128,256]{2,1,0:T(8,128)(2,1)S(1)}, u32[]{:S(2)}, u32[]{:S(2)}) collective-permute-start(bf16[8,128,256]{2,1,0:T(8,128)(2,1)} %get-tuple-element.26), channel_id=1, source_target_pairs={{0,12},{4,8},{8,4},{12,0},{1,13},{5,9},{9,5},{13,1},{2,14},{6,10},... | collective-permute-start | bytes 1572872 | tf_op jit(solution)/shard_map/ppermute | solution.py:283
  85.4 27.2 %collective-permute-start.17 = (bf16[8,128,256]{2,1,0:T(8,128)(2,1)}, bf16[8,128,256]{2,1,0:T(8,128)(2,1)S(1)}, u32[]{:S(2)}, u32[]{:S(2)}) collective-permute-start(bf16[8,128,256]{2,1,0:T(8,128)(2,1)} %get-tuple-element.27), channel_id=1, source_target_pairs={{0,12},{4,8},{8,4},{12,0},{1,13},{5,9},{9,5},{13,1},{2,14},{6,10},... | collective-permute-start | bytes 1572872 | tf_op jit(solution)/shard_map/ppermute | solution.py:283
  91.1 32.9 %collective-permute-start.19 = (bf16[8,128,256]{2,1,0:T(8,128)(2,1)}, bf16[8,128,256]{2,1,0:T(8,128)(2,1)}, u32[]{:S(2)}, u32[]{:S(2)}) collective-permute-start(bf16[8,128,256]{2,1,0:T(8,128)(2,1)} %get-tuple-element.28), channel_id=1, source_target_pairs={{0,12},{4,8},{8,4},{12,0},{1,13},{5,9},{9,5},{13,1},{2,14},{6,10},... | collective-permute-start | bytes 1572872 | tf_op jit(solution)/shard_map/ppermute | solution.py:283
  91.1 44.2 %collective-permute-start.21 = (bf16[8,128,256]{2,1,0:T(8,128)(2,1)}, bf16[8,128,256]{2,1,0:T(8,128)(2,1)}, u32[]{:S(2)}, u32[]{:S(2)}) collective-permute-start(bf16[8,128,256]{2,1,0:T(8,128)(2,1)} %get-tuple-element.29), channel_id=1, source_target_pairs={{0,12},{4,8},{8,4},{12,0},{1,13},{5,9},{9,5},{13,1},{2,14},{6,10},... | collective-permute-start | bytes 1572872 | tf_op jit(solution)/shard_map/ppermute | solution.py:283
  93.5 2.2 copy-start.2
  95.6 0.9 copy-start.5
  138.2 118.5 %copy-start.6 = (f32[1024,256]{1,0:T(8,128)S(1)}, f32[1024,256]{1,0:T(8,128)}, u32[]{:S(2)}) copy-start(f32[1024,256]{1,0:T(8,128)} %get-tuple-element.19) | copy-start | bytes 3145732
  138.2 118.5 %collective-permute-start.16 = (bf16[8,128,256]{2,1,0:T(8,128)(2,1)}, bf16[8,128,256]{2,1,0:T(8,128)(2,1)S(1)}, u32[]{:S(2)}, u32[]{:S(2)}) collective-permute-start(bf16[8,128,256]{2,1,0:T(8,128)(2,1)} %get-tuple-element.34), channel_id=1, source_target_pairs={{0,3},{1,2},{2,1},{3,0},{4,7},{5,6},{6,5},{7,4},{8,11},{9,10},{10,... | collective-permute-start | bytes 1572872 | tf_op jit(solution)/shard_map/ppermute | solution.py:302
  140.7 116.0 %collective-permute-start.18 = (bf16[8,128,256]{2,1,0:T(8,128)(2,1)}, bf16[8,128,256]{2,1,0:T(8,128)(2,1)S(1)}, u32[]{:S(2)}, u32[]{:S(2)}) collective-permute-start(bf16[8,128,256]{2,1,0:T(8,128)(2,1)} %get-tuple-element.37), channel_id=1, source_target_pairs={{0,2},{1,3},{2,0},{3,1},{4,6},{5,7},{6,4},{7,5},{8,10},{9,11},{10,... | collective-permute-start | bytes 1572872 | tf_op jit(solution)/shard_map/ppermute | solution.py:302
  140.8 115.9 %collective-permute-start.20 = (bf16[8,128,256]{2,1,0:T(8,128)(2,1)S(1)}, bf16[8,128,256]{2,1,0:T(8,128)(2,1)}, u32[]{:S(2)}, u32[]{:S(2)}) collective-permute-start(bf16[8,128,256]{2,1,0:T(8,128)(2,1)S(1)} %get-tuple-element.36), channel_id=1, source_target_pairs={{0,1},{1,0},{2,3},{3,2},{4,5},{5,4},{6,7},{7,6},{8,9},{9,8},{10,11... | collective-permute-start | bytes 1572872 | tf_op jit(solution)/shard_map/ppermute | solution.py:302
Sparse Core Ops, SparseCore 0:
  142.8 112.0 all-reduce.2

commit v2 on v1

--- a/solution.py
+++ b/solution.py
@@ -20,13 +20,20 @@
     return lax.dot_general(a, b, (((1,), (1,)), ((), ())), preferred_element_type=F32)
 
 
-def far_kernel(slots, cols, live, feat_ref, adj_ref, out_ref):
-    p = pl.program_id(0)
-    for s in range(slots):
-        value = jnp.dot(
-            adj_ref[0, s].astype(BF16), feat_ref[cols[p, s]], preferred_element_type=F32
-        )
-        out_ref[0, s] = jnp.where(s < live[p], value, 0.0).astype(BF16)
+def far_kernel(slots, n_node, cols, rows, live, node, feat_ref, adj_ref, *outs):
+    tile, width = feat_ref.shape[1:]
+    for k, out_ref in enumerate(outs):
+        p = lax.rem(node[0] + k, n_node)
+        for s in range(slots):
+            value = jnp.dot(
+                adj_ref[p, s].astype(BF16), feat_ref[cols[p, s]], preferred_element_type=F32
+            )
+            out_ref[s * tile : (s + 1) * tile] = jnp.where(s < live[p], value, 0.0).astype(BF16)
+        line = lax.broadcasted_iota(jnp.int32, (16, width), 0)
+        named = jnp.zeros((16, width), F32)
+        for s in range(slots):
+            named = jnp.where(line == s, rows[p, s].astype(F32), named)
+        out_ref[slots * tile :] = named.astype(BF16)
 
 
 def main_kernel(
@@ -84,7 +91,7 @@
 
             @pl.when(rows[k, s] == t)
             def _():
-                acc[...] += ref[s].astype(F32)
+                acc[...] += ref[s * acc.shape[0] : (s + 1) * acc.shape[0]].astype(F32)
 
     deg = jnp.broadcast_to(deg_ref[0].astype(F32), (deg_ref.shape[2], deg_ref.shape[2])).T
     deg = jnp.concatenate([deg, deg], axis=1)
@@ -115,15 +122,39 @@
                 send_refs[k][s] = back[rows[k, s]]
 
 
-def join_kernel(slots, n_parts, cols, live, own_ref, in_ref, adj_ref, *rest):
+def join_kernel(slots, n_parts, cols, live, node, own_ref, in_ref, adj_ref, *rest):
     ret_refs, out_ref = rest[:n_parts], rest[n_parts]
     out_ref[...] = own_ref[...] + in_ref[...].astype(F32)
     for k in range(n_parts):
+        p = lax.rem(node[0] + k, n_parts)
         for s in range(slots):
 
-            @pl.when(s < live[k])
+            @pl.when(s < live[p])
             def _():
-                out_ref[cols[k, s]] += outer(adj_ref[k, s].astype(BF16), ret_refs[k][s])
+                out_ref[cols[p, s]] += outer(adj_ref[p, s].astype(BF16), ret_refs[k][s])
+
+
+def summed(value, node, member, n_node, n_feat):
+    rounds = [("node", node, n_node), ("feat", member, n_feat)]
+    for axis, at, size in rounds:
+        half = value.shape[0] // 2
+        bit = at % 2
+        pairs = [(i, i ^ 1) for i in range(size)]
+        away = lax.dynamic_slice_in_dim(value, (1 - bit) * half, half, 0)
+        kept = lax.dynamic_slice_in_dim(value, bit * half, half, 0)
+        value = kept + lax.ppermute(away, axis, pairs)
+    for axis, size in (("feat", n_feat), ("node", n_node)):
+        step = 2
+        while step < size:
+            value = value + lax.ppermute(value, axis, [(i, i ^ step) for i in range(size)])
+            step *= 2
+    for axis, at, size in rounds[::-1]:
+        other = lax.ppermute(value, axis, [(i, i ^ 1) for i in range(size)])
+        first = at % 2 == 0
+        value = jnp.concatenate(
+            [jnp.where(first, value, other), jnp.where(first, other, value)], axis=0
+        )
+    return value
 
 
 def shards(
@@ -161,13 +192,27 @@
         return [(i, (i + k) % n_node) for i in range(n_node)]
 
     tiles = features.reshape(blocks, tile, width)
-    order = (node + jnp.arange(n_node, dtype=jnp.int32)) % n_node
-    far_c = far_cols.reshape(n_node, far_slots)[order]
-    far_r = far_rows.reshape(n_node, far_slots)[order]
-    live = far_live.reshape(n_node)[order]
+    far_c = far_cols.reshape(n_node, far_slots)
+    far_r = far_rows.reshape(n_node, far_slots)
+    live = far_live.reshape(n_node)
     fadj = far_adj.reshape(n_node, far_slots, tile, tile)
-    got_rows = [far_r[0]] + [lax.ppermute(far_r[k], "node", dist(k)) for k in range(1, n_node)]
-    rows = jnp.stack(got_rows)
+    here = node.reshape(1)
+    smem = pl.BlockSpec(memory_space=pltpu.SMEM)
+    whole = pl.BlockSpec(memory_space=pltpu.VMEM)
+
+    far_len = -(-far_slots // 16) * 16 + far_slots * tile
+    parts = pl.pallas_call(
+        functools.partial(far_kernel, far_slots, n_node),
+        out_shape=[jax.ShapeDtypeStruct((far_len, width), BF16)] * n_node,
+        in_specs=[smem] * 4 + [whole] * 2,
+        out_specs=[whole] * n_node,
+        compiler_params=pltpu.CompilerParams(vmem_limit_bytes=32 * 1024 * 1024),
+        name="far_partial",
+    )(far_c, far_r, live, here, tiles, fadj)
+    got = [parts[0]] + [lax.ppermute(parts[k], "node", dist(k)) for k in range(1, n_node)]
+    rows = jnp.stack(
+        [g[far_slots * tile : far_slots * tile + far_slots, 0].astype(jnp.int32) for g in got]
+    )
 
     from_in = lax.ppermute(tiles, "node", in_pairs)
     n_pieces = 2
@@ -175,27 +220,11 @@
     direct, relayed = [], []
     for i in range(n_pieces):
         piece = lax.dynamic_slice_in_dim(tiles, h * half + i * each, each, 0)
+        if i:
+            piece, _ = lax.optimization_barrier((piece, parts[0]))
         direct.append(lax.ppermute(piece, "node", cross_pairs))
     for piece in direct:
         relayed.append(lax.ppermute(piece, "feat", feat_pairs))
-
-    far_fn = pl.pallas_call(
-        lambda c, l, o, f, a, out: far_kernel(far_slots, c, l, f, a, out),
-        out_shape=jax.ShapeDtypeStruct((n_node, far_slots, tile, width), BF16),
-        grid_spec=pltpu.PrefetchScalarGridSpec(
-            num_scalar_prefetch=3,
-            grid=(n_node,),
-            in_specs=[
-                pl.BlockSpec((blocks, tile, width), lambda p, c, l, o: (0, 0, 0)),
-                pl.BlockSpec((1, far_slots, tile, tile), lambda p, c, l, o: (o[p], 0, 0, 0)),
-            ],
-            out_specs=pl.BlockSpec((1, far_slots, tile, width), lambda p, c, l, o: (p, 0, 0, 0)),
-        ),
-        compiler_params=pltpu.CompilerParams(vmem_limit_bytes=32 * 1024 * 1024),
-        name="far_partial",
-    )
-    parts = far_fn(far_c, live, order, tiles, fadj)
-    got = [parts[0]] + [lax.ppermute(parts[k], "node", dist(k)) for k in range(1, n_node)]
 
     kind, local = band_cols // blocks, band_cols % blocks
     is_in = kind == jnp.where(even, 2, 0)
@@ -229,7 +258,7 @@
             num_scalar_prefetch=3,
             grid=(sub_tiles,),
             in_specs=[any_spec] * (2 + n_cross)
-            + [vmem(far_shape)] * n_node
+            + [vmem((far_len, width))] * n_node
             + [
                 pl.BlockSpec((1, slots, tile, tile), lambda t, *_: (t, 0, 0, 0)),
                 pl.BlockSpec((1, 1, tile), lambda t, *_: (t, 0, 0)),
@@ -279,29 +308,55 @@
         lax.ppermute(send_back[k], "node", dist(n_node - k)) for k in range(1, n_node)
     ]
     in_terms = lax.ppermute(in_wide, "node", in_pairs)
-    far_first = list(range(n_feat - 1, -1, -1))
-    cross_terms = {d: lax.ppermute(cross_wide[d], "node", cross_pairs) for d in far_first}
-    sum_self, sum_neigh = lax.psum((part_self, part_neigh), ("node", "feat"))
+    odd_first = sorted(range(n_feat), key=lambda d: ((d & -d) if d else n_feat, -d))
+    cross_terms = {}
+    for d in odd_first:
+        outgoing = cross_wide[d]
+        if d % 2 == 0:
+            outgoing, _ = lax.optimization_barrier((outgoing, in_terms if d == 0 else returned[1]))
+        cross_terms[d] = lax.ppermute(outgoing, "node", cross_pairs)
     grad_scale = 1.0 / math.sqrt(block_rows * n_node)
+    both, _ = lax.optimization_barrier(
+        (jnp.concatenate([part_self, part_neigh], 0), returned[n_node - 1])
+    )
+    both = summed(both, node, member, n_node, n_feat)
+    both = both * grad_scale
 
     base = pl.pallas_call(
         functools.partial(join_kernel, far_slots, n_node),
         out_shape=jax.ShapeDtypeStruct((blocks, tile, width), F32),
-        in_specs=[pl.BlockSpec(memory_space=pltpu.SMEM)] * 2
+        in_specs=[smem] * 3
         + [pl.BlockSpec(memory_space=pltpu.VMEM)] * (3 + n_node),
         out_specs=pl.BlockSpec(memory_space=pltpu.VMEM),
         compiler_params=pltpu.CompilerParams(vmem_limit_bytes=40 * 1024 * 1024),
         name="join",
-    )(far_c, live, own_wide, in_terms, fadj[order], *returned)
-
-    total = self_back
-    for d in far_first:
+    )(far_c, live, here, own_wide, in_terms, fadj, *returned)
+
+    total = self_back.reshape(sub_tiles, tile, width)
+    extra = [[] for _ in range(n_feat)]
+    sent = None
+    for d in odd_first:
+        cross = cross_terms[d]
+        if sent is not None:
+            cross, _ = lax.optimization_barrier((cross, sent))
         chunk = lax.dynamic_slice_in_dim(base, (member ^ d) * sub_tiles, sub_tiles, 0)
-        chunk = (chunk + cross_terms[d].astype(F32)).astype(BF16)
-        if d:
-            chunk = lax.ppermute(chunk, "feat", [(i, i ^ d) for i in range(n_feat)])
-        total = total + chunk.reshape(sub_rows, width).astype(F32)
-    return (layer_out, total, sum_self * grad_scale, sum_neigh * grad_scale)
+        chunk = chunk + cross.astype(F32)
+        for term in extra[d]:
+            chunk = chunk + term.astype(F32)
+        if d == 0:
+            total = total + chunk
+            break
+        sent = chunk.astype(BF16)
+        step = d & -d
+        extra[d ^ step].append(
+            lax.ppermute(sent, "feat", [(i, i ^ step) for i in range(n_feat)])
+        )
+    return (
+        layer_out,
+        total.reshape(sub_rows, width),
+        both[:width],
+        both[width:],
+    )
 
 
 def solution(mesh):

time: 266 us -> 163 us (0.61)
  waiting for transfers between devices: 180 us -> 83.2 us
  between operations: 14.2 us -> 0.86 us
  starting transfers between devices: 24.3 us -> 29 us
  local copies, waits for them, and re-layouts: 11.6 us -> 15.5 us
    psum x1 -> x0, waiting for transfers between devices: 112 us -> none  [shards(): sum_self, sum_neigh = lax.psum((part_self, part_neigh), ('node', 'feat'))]
    ppermute x10 -> x13, starting transfers between devices: 11.9 us -> 18.9 us  [the longest x3 7.58 us: shards(): lax.ppermute(sent, 'feat', [(i, i ^ step) for i in range(n_feat)])]
    ppermute x10 -> x13, waiting for transfers between devices: 41.2 us -> 47.5 us  [the longest x3 18.9 us: shards(): lax.ppermute(sent, 'feat', [(i, i ^ step) for i in range(n_feat)])]
    ppermute x2, waiting for transfers between devices: 0.01 us -> 6.18 us  [shards(): relayed.append(lax.ppermute(piece, 'feat', feat_pairs))]
    unnamed x36 -> x34, local copies, waits for them, and re-layouts: 5.51 us -> 9.56 us
    ppermute x2, waiting for transfers between devices: 15.1 us -> 18.8 us  [shards(): direct.append(lax.ppermute(piece, 'node', cross_pairs))]
  transfers between devices with their start and end apart: 23 -> 25, of which waited for: 14 -> 16; matrix products, arithmetic and copies ran while one was open for 3% -> 9% of each run, Pallas kernels for 2% -> 2%
where the time goes in v2:
time: 163 us
  waiting for transfers between devices  83.2 us (51%)
  starting transfers between devices  29 us (18%)
  Pallas kernels  25.1 us (15%)
  local copies, waits for them, and re-layouts  15.5 us (10%)
  other arithmetic  8.82 us (5%)
    pallas_call x1, Pallas kernels, shards(): pl.pallas_call(functools.partial(main_kernel, dims), out_shape=[jax.Shape...  22.6 us
    ppermute x3, waiting for transfers between devices, shards(): lax.ppermute(sent, 'feat', [(i, i ^ step) for i in range(n_feat)])  18.9 us
    ppermute x2, waiting for transfers between devices, shards(): direct.append(lax.ppermute(piece, 'node', cross_pairs))  18.8 us
    ppermute x4, waiting for transfers between devices, shards(): cross_terms[d] = lax.ppermute(outgoing, 'node', cross_pairs)  11.9 us
    ppermute x2, waiting for transfers between devices, summed(): lax.ppermute(value, axis, [(i, i ^ step) for i in range(size)])  11.4 us
    unnamed x34, local copies, waits for them, and re-layouts  9.56 us
    ppermute x3, starting transfers between devices, shards(): lax.ppermute(sent, 'feat', [(i, i ^ step) for i in range(n_feat)])  7.58 us
    ppermute x2, waiting for transfers between devices, shards(): relayed.append(lax.ppermute(piece, 'feat', feat_pairs))  6.18 us
  transfers between devices with their start and end apart: 25, of which 16 were waited for; matrix products, arithmetic and copies ran while one was open for 9% of the time, Pallas kernels for 2%

profile of v2, /device:TPU:0, one launch (start us, length us, event | category | flops | bytes accessed | tf_op | source)
XLA Modules:
  0.0 162.5 jit_solution(10777355052646111867)
XLA Ops:
  0.6 0.5 collective-permute-start.3
  1.2 0.8 copy.17
  1.9 0.8 copy.18
  2.7 1.6 copy-done
  4.3 1.1 copy-done.2
  5.4 0.7 copy-done.6
  6.1 1.0 far_partial.1
  7.0 1.0 constant_dynamic-slice_fusion.2
  8.1 2.6 %collective-permute-start.5 = (bf16[8,128,256]{2,1,0:T(8,128)(2,1)}, bf16[8,128,256]{2,1,0:T(8,128)(2,1)S(1)}, u32[]{:S(2)}, u32[]{:S(2)}) collective-permute-start(bf16[8,128,256]{2,1,0:T(8,128)(2,1)} %get-tuple-element.33), channel_id=1, source_target_pairs={{0,12},{4,8},{8,4},{12,0},{1,13},{5,9},{9,5},{13,1},{2,14},{6,10},... | collective-permute-start | bytes 1572872 | tf_op jit(solution)/shard_map/ppermute | solution.py:225
  10.8 2.1 %collective-permute-start.1 = (bf16[400,256]{1,0:T(8,128)(2,1)S(1)}, bf16[400,256]{1,0:T(8,128)(2,1)}, u32[]{:S(2)}, u32[]{:S(2)}) collective-permute-start(bf16[400,256]{1,0:T(8,128)(2,1)S(1)} %get-tuple-element.31), channel_id=1, source_target_pairs={{0,8},{4,12},{8,0},{12,4},{1,9},{5,13},{9,1},{13,5},{2,10},{6,14},... | collective-permute-start | bytes 614408 | tf_op jit(solution)/shard_map/ppermute | solution.py:212
  12.8 0.6 fusion.5.cols
  13.5 0.7 stack.34.spot
  14.1 9.2 %collective-permute-done.5.rest_1_ = bf16[8,128,256]{2,1,0:T(8,128)(2,1)S(1)} collective-permute-done((bf16[8,128,256]{2,1,0:T(8,128)(2,1)}, bf16[8,128,256]{2,1,0:T(8,128)(2,1)S(1)}, u32[]{:S(2)}, u32[]{:S(2)}) %collective-permute-start.5) | collective-permute-done | bytes 524320 | tf_op jit(solution)/shard_map/ppermute | solution.py:225
  23.3 1.6 collective-permute-start.7
  24.9 9.7 %collective-permute-done.4.rest_0_ = bf16[8,128,256]{2,1,0:T(8,128)(2,1)} collective-permute-done((bf16[8,128,256]{2,1,0:T(8,128)(2,1)}, bf16[8,128,256]{2,1,0:T(8,128)(2,1)}, u32[]{:S(2)}, u32[]{:S(2)}) %collective-permute-start.4) | collective-permute-done | bytes 524320 | tf_op jit(solution)/shard_map/ppermute | solution.py:225
  34.5 1.6 collective-permute-start.6
  36.2 2.7 %collective-permute-done.rest_5_ = bf16[400,256]{1,0:T(8,128)(2,1)} collective-permute-done((bf16[400,256]{1,0:T(8,128)(2,1)S(1)}, bf16[400,256]{1,0:T(8,128)(2,1)}, u32[]{:S(2)}, u32[]{:S(2)}) %collective-permute-start) | collective-permute-done | bytes 204832 | tf_op jit(solution)/shard_map/ppermute | solution.py:212
  38.9 0.7 slice_reduce_fusion.2
  39.6 0.8 slice_reduce_fusion.1
  40.4 2.1 %collective-permute-done.2.rest_7_ = bf16[400,256]{1,0:T(8,128)(2,1)S(1)} collective-permute-done((bf16[400,256]{1,0:T(8,128)(2,1)S(1)}, bf16[400,256]{1,0:T(8,128)(2,1)S(1)}, u32[]{:S(2)}, u32[]{:S(2)}) %collective-permute-start.2) | collective-permute-done | bytes 204832 | tf_op jit(solution)/shard_map/ppermute | solution.py:212
  42.7 0.6 maximum_convert_fusion.rows
  43.3 6.2 %collective-permute-done.6.rest_2_ = bf16[8,128,256]{2,1,0:T(8,128)(2,1)S(1)} collective-permute-done((bf16[8,128,256]{2,1,0:T(8,128)(2,1)}, bf16[8,128,256]{2,1,0:T(8,128)(2,1)S(1)}, u32[]{:S(2)}, u32[]{:S(2)}) %collective-permute-start.6) | collective-permute-done | bytes 524320 | tf_op jit(solution)/shard_map/ppermute | solution.py:227
  49.5 0.7 copy-done.12
  50.3 0.8 copy-done.8
  51.0 22.6 %layer.1 = (bf16[1024,256]{1,0:T(8,128)(2,1)}, f32[1024,256]{1,0:T(8,128)}, f32[256,256]{1,0:T(8,128)}, f32[256,256]{1,0:T(8,128)}, f32[32,128,256]{2,1,0:T(8,12...) custom-call(s32[8,16]{1,0:T(8,128)} %fusion.5.cols, ...), custom_call_target="tpu_custom_call" | custom-call | tf_op jit(solution)/shard_map/layer/pallas_call | solution.py:245
  73.7 0.2 collective-permute-start.8
  73.8 0.4 collective-permute-start.11
  74.2 1.9 %pad_maximum_fusion = f32[512,256]{1,0:T(8,128)} fusion(f32[256,256]{1,0:T(8,128)} %get-tuple-element.52, f32[256,256]{1,0:T(8,128)} %get-tuple-element.51), kind=kLoop, calls=%fused_computation.4 | loop fusion | flops 131072 | bytes 1048576 | tf_op jit(solution)/shard_map/concatenate | solution.py:320
  76.1 3.0 %collective-permute-done.11.rest_3_ = bf16[3,128,256]{2,1,0:T(8,128)(2,1)S(1)} collective-permute-done((bf16[3,128,256]{2,1,0:T(8,128)(2,1)}, bf16[3,128,256]{2,1,0:T(8,128)(2,1)S(1)}, u32[]{:S(2)}, u32[]{:S(2)}) %collective-permute-start.11) | collective-permute-done | bytes 196640 | tf_op jit(solution)/shard_map/ppermute | solution.py:308
  79.1 1.0 constant_dynamic-slice_fusion.1
  80.2 1.6 %collective-permute-done.19 = f32[256,256]{1,0:T(8,128)} collective-permute-done((f32[256,256]{1,0:T(8,128)S(1)}, f32[256,256]{1,0:T(8,128)}, u32[]{:S(2)}, u32[]{:S(2)}) %collective-permute-start.19) | collective-permute-done | bytes 262176 | tf_op jit(solution)/shard_map/ppermute | solution.py:145
  81.8 1.1 dynamic-slice_add_fusion
  82.9 0.7 constant_dynamic-slice_fusion
  83.6 1.5 collective-permute-start.20
  85.1 0.6 collective-permute-start.15
  85.7 3.6 %collective-permute-done.20 = f32[128,256]{1,0:T(8,128)S(1)} collective-permute-done((f32[128,256]{1,0:T(8,128)}, f32[128,256]{1,0:T(8,128)S(1)}, u32[]{:S(2)}, u32[]{:S(2)}) %collective-permute-start.20) | collective-permute-done | bytes 131104 | tf_op jit(solution)/shard_map/ppermute | solution.py:145
  89.3 2.6 %collective-permute-start.21 = (f32[128,256]{1,0:T(8,128)S(1)}, f32[128,256]{1,0:T(8,128)S(1)}, u32[]{:S(2)}, u32[]{:S(2)}) collective-permute-start(f32[128,256]{1,0:T(8,128)S(1)} %dynamic-slice_add_fusion.1), channel_id=1, source_target_pairs={{0,2},{1,3},{2,0},{3,1},{4,6},{5,7},{6,4},{7,5},{8,10},{9,11},{10,... | collective-permute-start | bytes 393224 | tf_op jit(solution)/shard_map/ppermute | solution.py:149
  91.9 1.1 collective-permute-start.10
  93.1 4.9 %collective-permute-done.21 = f32[128,256]{1,0:T(8,128)S(1)} collective-permute-done((f32[128,256]{1,0:T(8,128)S(1)}, f32[128,256]{1,0:T(8,128)S(1)}, u32[]{:S(2)}, u32[]{:S(2)}) %collective-permute-start.21) | collective-permute-done | bytes 131104 | tf_op jit(solution)/shard_map/ppermute | solution.py:149
  97.9 0.7 add.188
  98.6 1.1 collective-permute-start.22
  99.7 2.8 %collective-permute-done.9.rest_1_ = bf16[3,128,256]{2,1,0:T(8,128)(2,1)S(1)} collective-permute-done((bf16[3,128,256]{2,1,0:T(8,128)(2,1)}, bf16[3,128,256]{2,1,0:T(8,128)(2,1)S(1)}, u32[]{:S(2)}, u32[]{:S(2)}) %collective-permute-start.9) | collective-permute-done | bytes 196640 | tf_op jit(solution)/shard_map/ppermute | solution.py:308
  102.5 1.8 %collective-permute-start.14 = (bf16[8,128,256]{2,1,0:T(8,128)(2,1)}, bf16[8,128,256]{2,1,0:T(8,128)(2,1)S(1)}, u32[]{:S(2)}, u32[]{:S(2)}) collective-permute-start(bf16[8,128,256]{2,1,0:T(8,128)(2,1)} %get-tuple-element.46), channel_id=1, source_target_pairs={{0,12},{4,8},{8,4},{12,0},{1,13},{5,9},{9,5},{13,1},{2,14},{6,10},... | collective-permute-start | bytes 1572872 | tf_op jit(solution)/shard_map/ppermute | solution.py:317
  104.3 6.5 %collective-permute-done.22 = f32[128,256]{1,0:T(8,128)} collective-permute-done((f32[128,256]{1,0:T(8,128)}, f32[128,256]{1,0:T(8,128)}, u32[]{:S(2)}, u32[]{:S(2)}) %collective-permute-start.22) | collective-permute-done | bytes 131104 | tf_op jit(solution)/shard_map/ppermute | solution.py:149
  110.9 1.0 add.189
  111.9 0.6 collective-permute-start.23
  112.5 2.2 %copy-done.1 = f32[32,128,256]{2,1,0:T(8,128)S(1)} copy-done((f32[32,128,256]{2,1,0:T(8,128)S(1)}, f32[32,128,256]{2,1,0:T(8,128)}, u32[]{:S(2)}) %copy-start.1) | copy-done | bytes 4194328
  114.7 0.9 copy-done.5
  115.6 1.6 join.1
  117.2 1.3 add_convert_fusion.2
  118.5 2.3 %collective-permute-start.16 = (bf16[8,128,256]{2,1,0:T(8,128)(2,1)S(1)}, bf16[8,128,256]{2,1,0:T(8,128)(2,1)S(1)}, u32[]{:S(2)}, u32[]{:S(2)}) collective-permute-start(bf16[8,128,256]{2,1,0:T(8,128)(2,1)S(1)} %add_convert_fusion.2), channel_id=1, source_target_pairs={{0,1},{1,0},{2,3},{3,2},{4,5},{5,4},{6,7},{7,6},{8,9},{9,8},{10,11... | collective-permute-start | bytes 1572872 | tf_op jit(solution)/shard_map/ppermute | solution.py:352
  120.9 1.0 collective-permute-start.24
  121.8 0.1 add_convert_fusion.1
  122.0 1.1 collective-permute-start.17
  123.1 6.8 %collective-permute-done.13 = bf16[8,128,256]{2,1,0:T(8,128)(2,1)S(1)} collective-permute-done((bf16[8,128,256]{2,1,0:T(8,128)(2,1)}, bf16[8,128,256]{2,1,0:T(8,128)(2,1)S(1)}, u32[]{:S(2)}, u32[]{:S(2)}) %collective-permute-start.13) | collective-permute-done | bytes 524320 | tf_op jit(solution)/shard_map/ppermute | solution.py:317
  129.9 2.1 %collective-permute-start.12 = (bf16[8,128,256]{2,1,0:T(8,128)(2,1)S(1)}, bf16[8,128,256]{2,1,0:T(8,128)(2,1)S(1)}, u32[]{:S(2)}, u32[]{:S(2)}) collective-permute-start(bf16[8,128,256]{2,1,0:T(8,128)(2,1)S(1)} %copy-done.15), channel_id=1, source_target_pairs={{0,12},{4,8},{8,4},{12,0},{1,13},{5,9},{9,5},{13,1},{2,14},{6,10},... | collective-permute-start | bytes 1572872 | tf_op jit(solution)/shard_map/ppermute | solution.py:317
  132.0 0.9 collective-permute-done.16
  132.9 0.2 add_convert_fusion
  133.1 4.2 %collective-permute-start.18 = (bf16[8,128,256]{2,1,0:T(8,128)(2,1)S(1)}, bf16[8,128,256]{2,1,0:T(8,128)(2,1)S(1)}, u32[]{:S(2)}, u32[]{:S(2)}) collective-permute-start(bf16[8,128,256]{2,1,0:T(8,128)(2,1)S(1)} %add_convert_fusion), channel_id=1, source_target_pairs={{0,2},{1,3},{2,0},{3,1},{4,6},{5,7},{6,4},{7,5},{8,10},{9,11},{10,... | collective-permute-start | bytes 1572872 | tf_op jit(solution)/shard_map/ppermute | solution.py:352
  137.4 0.8 fusion.10
  138.2 5.1 %collective-permute-done.12 = bf16[8,128,256]{2,1,0:T(8,128)(2,1)S(1)} collective-permute-done((bf16[8,128,256]{2,1,0:T(8,128)(2,1)S(1)}, bf16[8,128,256]{2,1,0:T(8,128)(2,1)S(1)}, u32[]{:S(2)}, u32[]{:S(2)}) %collective-permute-start.12) | collective-permute-done | bytes 524320 | tf_op jit(solution)/shard_map/ppermute | solution.py:317
  143.3 8.6 %collective-permute-done.17 = bf16[8,128,256]{2,1,0:T(8,128)(2,1)S(1)} collective-permute-done((bf16[8,128,256]{2,1,0:T(8,128)(2,1)S(1)}, bf16[8,128,256]{2,1,0:T(8,128)(2,1)S(1)}, u32[]{:S(2)}, u32[]{:S(2)}) %collective-permute-start.17) | collective-permute-done | bytes 524320 | tf_op jit(solution)/shard_map/ppermute | solution.py:352
  151.9 9.4 %collective-permute-done.18 = bf16[8,128,256]{2,1,0:T(8,128)(2,1)S(1)} collective-permute-done((bf16[8,128,256]{2,1,0:T(8,128)(2,1)S(1)}, bf16[8,128,256]{2,1,0:T(8,128)(2,1)S(1)}, u32[]{:S(2)}, u32[]{:S(2)}) %collective-permute-start.18) | collective-permute-done | bytes 524320 | tf_op jit(solution)/shard_map/ppermute | solution.py:352
  161.3 1.2 add_add_fusion
  (47 shorter events, 0.6 us)
Async XLA Ops:
  0.6 12.2 %copy-start.14 = (s32[8,16]{1,0:T(8,128)S(1)}, s32[8,16]{1,0:T(8,128)}, u32[]{:S(2)}) copy-start(s32[8,16]{1,0:T(8,128)} %param.12) | copy-start | bytes 1540
  0.6 48.9 %collective-permute-start.3 = (bf16[32,128,256]{2,1,0:T(8,128)(2,1)}, bf16[32,128,256]{2,1,0:T(8,128)(2,1)S(1)}, u32[]{:S(2)}, u32[]{:S(2)}) collective-permute-start(bf16[32,128,256]{2,1,0:T(8,128)(2,1)} %bitcast.18), channel_id=1, source_target_pairs={{0,4},{4,0},{8,12},{12,8},{1,5},{5,1},{9,13},{13,9},{2,6},{6,2},{1... | collective-permute-start | bytes 6291464 | tf_op jit(solution)/shard_map/ppermute | solution.py:217
  2.7 1.6 copy-start
  4.3 1.1 copy-start.2
  5.4 0.7 copy-start.6
  7.0 42.5 %copy-start.4 = (bf16[400,256]{1,0:T(8,128)(2,1)}, bf16[400,256]{1,0:T(8,128)(2,1)S(1)}, u32[]{:S(2)}) copy-start(bf16[400,256]{1,0:T(8,128)(2,1)S(1)} %get-tuple-element.29.rest_4_) | copy-start | bytes 614404
  8.1 15.2 %collective-permute-start.5 = (bf16[8,128,256]{2,1,0:T(8,128)(2,1)}, bf16[8,128,256]{2,1,0:T(8,128)(2,1)S(1)}, u32[]{:S(2)}, u32[]{:S(2)}) collective-permute-start(bf16[8,128,256]{2,1,0:T(8,128)(2,1)} %get-tuple-element.33), channel_id=1, source_target_pairs={{0,12},{4,8},{8,4},{12,0},{1,13},{5,9},{9,5},{13,1},{2,14},{6,10},... | collective-permute-start | bytes 1572872 | tf_op jit(solution)/shard_map/ppermute | solution.py:225
  10.7 23.8 %collective-permute-start.4 = (bf16[8,128,256]{2,1,0:T(8,128)(2,1)}, bf16[8,128,256]{2,1,0:T(8,128)(2,1)}, u32[]{:S(2)}, u32[]{:S(2)}) collective-permute-start(bf16[8,128,256]{2,1,0:T(8,128)(2,1)} %get-tuple-element.55), channel_id=1, source_target_pairs={{0,12},{4,8},{8,4},{12,0},{1,13},{5,9},{9,5},{13,1},{2,14},{6,10},... | collective-permute-start | bytes 1572872 | tf_op jit(solution)/shard_map/ppermute | solution.py:225
  10.7 28.2 %collective-permute-start = (bf16[400,256]{1,0:T(8,128)(2,1)S(1)}, bf16[400,256]{1,0:T(8,128)(2,1)}, u32[]{:S(2)}, u32[]{:S(2)}) collective-permute-start(bf16[400,256]{1,0:T(8,128)(2,1)S(1)} %get-tuple-element.30), channel_id=1, source_target_pairs={{0,4},{4,8},{8,12},{12,0},{1,5},{5,9},{9,13},{13,1},{2,6},{6,10},{... | collective-permute-start | bytes 614408 | tf_op jit(solution)/shard_map/ppermute | solution.py:212
  10.8 28.9 %collective-permute-start.1 = (bf16[400,256]{1,0:T(8,128)(2,1)S(1)}, bf16[400,256]{1,0:T(8,128)(2,1)}, u32[]{:S(2)}, u32[]{:S(2)}) collective-permute-start(bf16[400,256]{1,0:T(8,128)(2,1)S(1)} %get-tuple-element.31), channel_id=1, source_target_pairs={{0,8},{4,12},{8,0},{12,4},{1,9},{5,13},{9,1},{13,5},{2,10},{6,14},... | collective-permute-start | bytes 614408 | tf_op jit(solution)/shard_map/ppermute | solution.py:212
  23.3 26.2 %copy-start.10 = (bf16[8,128,256]{2,1,0:T(8,128)(2,1)}, bf16[8,128,256]{2,1,0:T(8,128)(2,1)S(1)}, u32[]{:S(2)}) copy-start(bf16[8,128,256]{2,1,0:T(8,128)(2,1)S(1)} %collective-permute-done.5.rest_1_) | copy-start | bytes 1572868
  23.3 20.0 %collective-permute-start.7 = (bf16[8,128,256]{2,1,0:T(8,128)(2,1)S(1)}, bf16[8,128,256]{2,1,0:T(8,128)(2,1)S(1)}, u32[]{:S(2)}, u32[]{:S(2)}) collective-permute-start(bf16[8,128,256]{2,1,0:T(8,128)(2,1)S(1)} %collective-permute-done.5.rest_1_), channel_id=1, source_target_pairs={{0,1},{1,0},{2,3},{3,2},{4,5},{5,4},{6,7},{7,6},{8,9},{9,8},{10,11... | collective-permute-start | bytes 1572872 | tf_op jit(solution)/shard_map/ppermute | solution.py:227
  34.5 15.0 %collective-permute-start.6 = (bf16[8,128,256]{2,1,0:T(8,128)(2,1)}, bf16[8,128,256]{2,1,0:T(8,128)(2,1)S(1)}, u32[]{:S(2)}, u32[]{:S(2)}) collective-permute-start(bf16[8,128,256]{2,1,0:T(8,128)(2,1)} %collective-permute-done.4.rest_0_), channel_id=1, source_target_pairs={{0,1},{1,0},{2,3},{3,2},{4,5},{5,4},{6,7},{7,6},{8,9},{9,8},{10,11... | collective-permute-start | bytes 1572872 | tf_op jit(solution)/shard_map/ppermute | solution.py:227
  38.9 3.7 %collective-permute-start.2 = (bf16[400,256]{1,0:T(8,128)(2,1)S(1)}, bf16[400,256]{1,0:T(8,128)(2,1)S(1)}, u32[]{:S(2)}, u32[]{:S(2)}) collective-permute-start(bf16[400,256]{1,0:T(8,128)(2,1)S(1)} %get-tuple-element.32), channel_id=1, source_target_pairs={{0,12},{4,0},{8,4},{12,8},{1,13},{5,1},{9,5},{13,9},{2,14},{6,2},{... | collective-permute-start | bytes 614408 | tf_op jit(solution)/shard_map/ppermute | solution.py:212
  42.6 6.9 %copy-start.13 = (bf16[400,256]{1,0:T(8,128)(2,1)}, bf16[400,256]{1,0:T(8,128)(2,1)S(1)}, u32[]{:S(2)}) copy-start(bf16[400,256]{1,0:T(8,128)(2,1)S(1)} %collective-permute-done.2.rest_7_) | copy-start | bytes 614404
  43.3 6.2 %copy-start.11 = (bf16[8,128,256]{2,1,0:T(8,128)(2,1)}, bf16[8,128,256]{2,1,0:T(8,128)(2,1)S(1)}, u32[]{:S(2)}) copy-start(bf16[8,128,256]{2,1,0:T(8,128)(2,1)S(1)} %collective-permute-done.7.rest_3_) | copy-start | bytes 1572868
  49.5 0.8 copy-start.12
  49.5 1.5 copy-start.8
  51.0 61.4 %copy-start.7 = (s32[1,1,4]{2,1,0:T(1,128)S(1)}, s32[1,1,4]{2,1,0:T(1,128)}, u32[]{:S(2)}) copy-start(s32[1,1,4]{2,1,0:T(1,128)} %param.16) | copy-start | bytes 52
  73.7 38.8 %copy-start.3 = (s32[1,1,4,3,128,128]{5,4,3,2,1,0:T(8,128)S(1)}, s32[1,1,4,3,128,128]{5,4,3,2,1,0:T(8,128)}, u32[]{:S(2)}) copy-start(s32[1,1,4,3,128,128]{5,4,3,2,1,0:T(8,128)} %param.17) | copy-start | bytes 2359300
  73.7 38.8 %collective-permute-start.8 = (bf16[32,128,256]{2,1,0:T(8,128)(2,1)}, bf16[32,128,256]{2,1,0:T(8,128)(2,1)S(1)}, u32[]{:S(2)}, u32[]{:S(2)}) collective-permute-start(bf16[32,128,256]{2,1,0:T(8,128)(2,1)} %get-tuple-element.37), channel_id=1, source_target_pairs={{0,4},{4,0},{8,12},{12,8},{1,5},{5,1},{9,13},{13,9},{2,6},{6,2},{1... | collective-permute-start | bytes 6291464 | tf_op jit(solution)/shard_map/ppermute | solution.py:310
  73.8 5.3 %collective-permute-start.11 = (bf16[3,128,256]{2,1,0:T(8,128)(2,1)}, bf16[3,128,256]{2,1,0:T(8,128)(2,1)S(1)}, u32[]{:S(2)}, u32[]{:S(2)}) collective-permute-start(bf16[3,128,256]{2,1,0:T(8,128)(2,1)} %get-tuple-element.41), channel_id=1, source_target_pairs={{0,4},{4,8},{8,12},{12,0},{1,5},{5,9},{9,13},{13,1},{2,6},{6,10},{... | collective-permute-start | bytes 589832 | tf_op jit(solution)/shard_map/ppermute | solution.py:308
  80.1 1.7 %collective-permute-start.19 = (f32[256,256]{1,0:T(8,128)S(1)}, f32[256,256]{1,0:T(8,128)}, u32[]{:S(2)}, u32[]{:S(2)}) collective-permute-start(f32[256,256]{1,0:T(8,128)S(1)} %constant_dynamic-slice_fusion.1), channel_id=1, source_target_pairs={{0,4},{4,0},{8,12},{12,8},{1,5},{5,1},{9,13},{13,9},{2,6},{6,2},{1... | collective-permute-start | bytes 786440 | tf_op jit(solution)/shard_map/ppermute | solution.py:145
  83.6 5.7 %collective-permute-start.20 = (f32[128,256]{1,0:T(8,128)}, f32[128,256]{1,0:T(8,128)S(1)}, u32[]{:S(2)}, u32[]{:S(2)}) collective-permute-start(f32[128,256]{1,0:T(8,128)} %constant_dynamic-slice_fusion), channel_id=1, source_target_pairs={{0,1},{1,0},{2,3},{3,2},{4,5},{5,4},{6,7},{7,6},{8,9},{9,8},{10,11... | collective-permute-start | bytes 393224 | tf_op jit(solution)/shard_map/ppermute | solution.py:145
  85.1 32.1 %collective-permute-start.15 = (bf16[8,128,256]{2,1,0:T(8,128)(2,1)}, bf16[8,128,256]{2,1,0:T(8,128)(2,1)}, u32[]{:S(2)}, u32[]{:S(2)}) collective-permute-start(bf16[8,128,256]{2,1,0:T(8,128)(2,1)} %get-tuple-element.47), channel_id=1, source_target_pairs={{0,12},{4,8},{8,4},{12,0},{1,13},{5,9},{9,5},{13,1},{2,14},{6,10},... | collective-permute-start | bytes 1572872 | tf_op jit(solution)/shard_map/ppermute | solution.py:317
  89.3 8.6 %collective-permute-start.21 = (f32[128,256]{1,0:T(8,128)S(1)}, f32[128,256]{1,0:T(8,128)S(1)}, u32[]{:S(2)}, u32[]{:S(2)}) collective-permute-start(f32[128,256]{1,0:T(8,128)S(1)} %dynamic-slice_add_fusion.1), channel_id=1, source_target_pairs={{0,2},{1,3},{2,0},{3,1},{4,6},{5,7},{6,4},{7,5},{8,10},{9,11},{10,... | collective-permute-start | bytes 393224 | tf_op jit(solution)/shard_map/ppermute | solution.py:149
  91.9 10.6 %collective-permute-start.9 = (bf16[3,128,256]{2,1,0:T(8,128)(2,1)}, bf16[3,128,256]{2,1,0:T(8,128)(2,1)S(1)}, u32[]{:S(2)}, u32[]{:S(2)}) collective-permute-start(bf16[3,128,256]{2,1,0:T(8,128)(2,1)} %get-tuple-element.39), channel_id=1, source_target_pairs={{0,12},{4,0},{8,4},{12,8},{1,13},{5,1},{9,5},{13,9},{2,14},{6,2},{... | collective-permute-start | bytes 589832 | tf_op jit(solution)/shard_map/ppermute | solution.py:308
  91.9 19.9 %collective-permute-start.10 = (bf16[3,128,256]{2,1,0:T(8,128)(2,1)}, bf16[3,128,256]{2,1,0:T(8,128)(2,1)S(1)}, u32[]{:S(2)}, u32[]{:S(2)}) collective-permute-start(bf16[3,128,256]{2,1,0:T(8,128)(2,1)} %get-tuple-element.40), channel_id=1, source_target_pairs={{0,8},{4,12},{8,0},{12,4},{1,9},{5,13},{9,1},{13,5},{2,10},{6,14},... | collective-permute-start | bytes 589832 | tf_op jit(solution)/shard_map/ppermute | solution.py:308
  98.6 12.3 %collective-permute-start.22 = (f32[128,256]{1,0:T(8,128)}, f32[128,256]{1,0:T(8,128)}, u32[]{:S(2)}, u32[]{:S(2)}) collective-permute-start(f32[128,256]{1,0:T(8,128)} %add.188), channel_id=1, source_target_pairs={{0,8},{4,12},{8,0},{12,4},{1,9},{5,13},{9,1},{13,5},{2,10},{6,14},... | collective-permute-start | bytes 393224 | tf_op jit(solution)/shard_map/ppermute | solution.py:149
  102.5 19.3 %collective-permute-start.14 = (bf16[8,128,256]{2,1,0:T(8,128)(2,1)}, bf16[8,128,256]{2,1,0:T(8,128)(2,1)S(1)}, u32[]{:S(2)}, u32[]{:S(2)}) collective-permute-start(bf16[8,128,256]{2,1,0:T(8,128)(2,1)} %get-tuple-element.46), channel_id=1, source_target_pairs={{0,12},{4,8},{8,4},{12,0},{1,13},{5,9},{9,5},{13,1},{2,14},{6,10},... | collective-permute-start | bytes 1572872 | tf_op jit(solution)/shard_map/ppermute | solution.py:317
  110.9 19.0 %collective-permute-start.13 = (bf16[8,128,256]{2,1,0:T(8,128)(2,1)}, bf16[8,128,256]{2,1,0:T(8,128)(2,1)S(1)}, u32[]{:S(2)}, u32[]{:S(2)}) collective-permute-start(bf16[8,128,256]{2,1,0:T(8,128)(2,1)} %get-tuple-element.45), channel_id=1, source_target_pairs={{0,12},{4,8},{8,4},{12,0},{1,13},{5,9},{9,5},{13,1},{2,14},{6,10},... | collective-permute-start | bytes 1572872 | tf_op jit(solution)/shard_map/ppermute | solution.py:317
  111.9 8.9 %collective-permute-start.23 = (f32[128,256]{1,0:T(8,128)S(1)}, f32[128,256]{1,0:T(8,128)S(1)}, u32[]{:S(2)}, u32[]{:S(2)}) collective-permute-start(f32[128,256]{1,0:T(8,128)S(1)} %add.189), channel_id=1, source_target_pairs={{0,1},{1,0},{2,3},{3,2},{4,5},{5,4},{6,7},{7,6},{8,9},{9,8},{10,11... | collective-permute-start | bytes 393224 | tf_op jit(solution)/shard_map/ppermute | solution.py:152
  112.5 2.2 %copy-start.1 = (f32[32,128,256]{2,1,0:T(8,128)S(1)}, f32[32,128,256]{2,1,0:T(8,128)}, u32[]{:S(2)}) copy-start(f32[32,128,256]{2,1,0:T(8,128)} %get-tuple-element.36.own_ref) | copy-start | bytes 12582916
  114.7 0.9 copy-start.5
  117.2 12.7 %copy-start.15 = (bf16[8,128,256]{2,1,0:T(8,128)(2,1)S(1)}, bf16[8,128,256]{2,1,0:T(8,128)(2,1)}, u32[]{:S(2)}) copy-start(bf16[8,128,256]{2,1,0:T(8,128)(2,1)} %get-tuple-element.43) | copy-start | bytes 1572868
  118.5 14.4 %collective-permute-start.16 = (bf16[8,128,256]{2,1,0:T(8,128)(2,1)S(1)}, bf16[8,128,256]{2,1,0:T(8,128)(2,1)S(1)}, u32[]{:S(2)}, u32[]{:S(2)}) collective-permute-start(bf16[8,128,256]{2,1,0:T(8,128)(2,1)S(1)} %add_convert_fusion.2), channel_id=1, source_target_pairs={{0,1},{1,0},{2,3},{3,2},{4,5},{5,4},{6,7},{7,6},{8,9},{9,8},{10,11... | collective-permute-start | bytes 1572872 | tf_op jit(solution)/shard_map/ppermute | solution.py:352
  120.8 40.5 %copy-start.9 = (f32[1024,256]{1,0:T(8,128)S(1)}, f32[1024,256]{1,0:T(8,128)}, u32[]{:S(2)}) copy-start(f32[1024,256]{1,0:T(8,128)} %get-tuple-element.35) | copy-start | bytes 3145732
  120.9 16.4 %collective-permute-start.24 = (f32[256,256]{1,0:T(8,128)S(1)}, f32[256,256]{1,0:T(8,128)S(1)}, u32[]{:S(2)}, u32[]{:S(2)}) collective-permute-start(f32[256,256]{1,0:T(8,128)S(1)} %pad_maximum_fusion.1), channel_id=1, source_target_pairs={{0,4},{4,0},{8,12},{12,8},{1,5},{5,1},{9,13},{13,9},{2,6},{6,2},{1... | collective-permute-start | bytes 786440 | tf_op jit(solution)/shard_map/ppermute | solution.py:152
  122.0 29.9 %collective-permute-start.17 = (bf16[8,128,256]{2,1,0:T(8,128)(2,1)S(1)}, bf16[8,128,256]{2,1,0:T(8,128)(2,1)S(1)}, u32[]{:S(2)}, u32[]{:S(2)}) collective-permute-start(bf16[8,128,256]{2,1,0:T(8,128)(2,1)S(1)} %add_convert_fusion.1), channel_id=1, source_target_pairs={{0,1},{1,0},{2,3},{3,2},{4,5},{5,4},{6,7},{7,6},{8,9},{9,8},{10,11... | collective-permute-start | bytes 1572872 | tf_op jit(solution)/shard_map/ppermute | solution.py:352
  129.9 13.4 %collective-permute-start.12 = (bf16[8,128,256]{2,1,0:T(8,128)(2,1)S(1)}, bf16[8,128,256]{2,1,0:T(8,128)(2,1)S(1)}, u32[]{:S(2)}, u32[]{:S(2)}) collective-permute-start(bf16[8,128,256]{2,1,0:T(8,128)(2,1)S(1)} %copy-done.15), channel_id=1, source_target_pairs={{0,12},{4,8},{8,4},{12,0},{1,13},{5,9},{9,5},{13,1},{2,14},{6,10},... | collective-permute-start | bytes 1572872 | tf_op jit(solution)/shard_map/ppermute | solution.py:317
  133.1 28.2 %collective-permute-start.18 = (bf16[8,128,256]{2,1,0:T(8,128)(2,1)S(1)}, bf16[8,128,256]{2,1,0:T(8,128)(2,1)S(1)}, u32[]{:S(2)}, u32[]{:S(2)}) collective-permute-start(bf16[8,128,256]{2,1,0:T(8,128)(2,1)S(1)} %add_convert_fusion), channel_id=1, source_target_pairs={{0,2},{1,3},{2,0},{3,1},{4,6},{5,7},{6,4},{7,5},{8,10},{9,11},{10,... | collective-permute-start | bytes 1572872 | tf_op jit(solution)/shard_map/ppermute | solution.py:352

commit v3 on v2

--- a/solution.py
+++ b/solution.py
@@ -310,18 +310,12 @@
     in_terms = lax.ppermute(in_wide, "node", in_pairs)
     odd_first = sorted(range(n_feat), key=lambda d: ((d & -d) if d else n_feat, -d))
     cross_terms = {}
-    for d in odd_first:
+    for i, d in enumerate(odd_first):
         outgoing = cross_wide[d]
-        if d % 2 == 0:
-            outgoing, _ = lax.optimization_barrier((outgoing, in_terms if d == 0 else returned[1]))
+        if i:
+            outgoing, _ = lax.optimization_barrier((outgoing, returned[min(i, n_node - 1)]))
         cross_terms[d] = lax.ppermute(outgoing, "node", cross_pairs)
     grad_scale = 1.0 / math.sqrt(block_rows * n_node)
-    both, _ = lax.optimization_barrier(
-        (jnp.concatenate([part_self, part_neigh], 0), returned[n_node - 1])
-    )
-    both = summed(both, node, member, n_node, n_feat)
-    both = both * grad_scale
-
     base = pl.pallas_call(
         functools.partial(join_kernel, far_slots, n_node),
         out_shape=jax.ShapeDtypeStruct((blocks, tile, width), F32),
@@ -331,6 +325,12 @@
         compiler_params=pltpu.CompilerParams(vmem_limit_bytes=40 * 1024 * 1024),
         name="join",
     )(far_c, live, here, own_wide, in_terms, fadj, *returned)
+
+    both, _ = lax.optimization_barrier(
+        (jnp.concatenate([part_self, part_neigh], 0), base)
+    )
+    both = summed(both, node, member, n_node, n_feat)
+    both = both * grad_scale
 
     total = self_back.reshape(sub_tiles, tile, width)
     extra = [[] for _ in range(n_feat)]

time: 163 us -> 173 us (1.061)
  waiting for transfers between devices: 83.2 us -> 88.1 us
  other arithmetic: 8.82 us -> 12 us
    ppermute x2, waiting for transfers between devices: 0.01 us -> 14 us  [summed(): other = lax.ppermute(value, axis, [(i, i ^ 1) for i in range(size)])]
    ppermute x3, waiting for transfers between devices: 18.9 us -> 7.29 us  [shards(): lax.ppermute(sent, 'feat', [(i, i ^ step) for i in range(n_feat)])]
    ppermute x4, waiting for transfers between devices: 11.9 us -> 23 us  [shards(): cross_terms[d] = lax.ppermute(outgoing, 'node', cross_pairs)]
    ppermute x2, waiting for transfers between devices: 11.4 us -> 5.41 us  [summed(): lax.ppermute(value, axis, [(i, i ^ step) for i in range(size)])]
    ppermute x2, waiting for transfers between devices: 5.27 us -> 0.01 us  [summed(): value = kept + lax.ppermute(away, axis, pairs)]
    convert_element_type x3, other arithmetic: 1.63 us -> 6.02 us  [shards(): sent = chunk.astype(BF16)]
    ppermute x3, starting transfers between devices: 7.58 us -> 4.83 us  [shards(): lax.ppermute(sent, 'feat', [(i, i ^ step) for i in range(n_feat)])]
    ppermute x3, waiting for transfers between devices: 5.86 us -> 8.62 us  [shards(): lax.ppermute(send_back[k], 'node', dist(n_node - k))]
  transfers between devices with their start and end apart: 25 -> 25, of which waited for: 16 -> 13; matrix products, arithmetic and copies ran while one was open for 9% -> 10% of each run, Pallas kernels for 2% -> 1%
where the time goes in v3:
time: 173 us
  waiting for transfers between devices  88.1 us (51%)
  starting transfers between devices  30.3 us (18%)
  Pallas kernels  25.3 us (15%)
  local copies, waits for them, and re-layouts  15.9 us (9%)
  other arithmetic  12 us (7%)
    ppermute x4, waiting for transfers between devices, shards(): cross_terms[d] = lax.ppermute(outgoing, 'node', cross_pairs)  23 us
    pallas_call x1, Pallas kernels, shards(): pl.pallas_call(functools.partial(main_kernel, dims), out_shape=[jax.Shape...  22.6 us
    ppermute x2, waiting for transfers between devices, shards(): direct.append(lax.ppermute(piece, 'node', cross_pairs))  18.8 us
    ppermute x2, waiting for transfers between devices, summed(): other = lax.ppermute(value, axis, [(i, i ^ 1) for i in range(size)])  14 us
    unnamed x36, local copies, waits for them, and re-layouts  11.5 us
    ppermute x3, waiting for transfers between devices, shards(): lax.ppermute(send_back[k], 'node', dist(n_node - k))  8.62 us
    ppermute x3, waiting for transfers between devices, shards(): lax.ppermute(sent, 'feat', [(i, i ^ step) for i in range(n_feat)])  7.29 us
    ppermute x2, waiting for transfers between devices, shards(): relayed.append(lax.ppermute(piece, 'feat', feat_pairs))  6.18 us
  transfers between devices with their start and end apart: 25, of which 13 were waited for; matrix products, arithmetic and copies ran while one was open for 10% of the time, Pallas kernels for 1%

profile of v3, /device:TPU:0, one launch (start us, length us, event | category | flops | bytes accessed | tf_op | source)
XLA Modules:
  0.0 172.6 jit_solution(8928100122007148272)
XLA Ops:
  0.6 0.5 collective-permute-start.3
  1.2 0.8 copy.17
  1.9 0.8 copy.18
  2.7 1.6 copy-done.1
  4.3 1.1 copy-done.3
  5.4 0.7 copy-done.7
  6.1 1.0 far_partial.1
  7.0 1.1 constant_dynamic-slice_fusion.2
  8.1 2.6 %collective-permute-start.5 = (bf16[8,128,256]{2,1,0:T(8,128)(2,1)}, bf16[8,128,256]{2,1,0:T(8,128)(2,1)S(1)}, u32[]{:S(2)}, u32[]{:S(2)}) collective-permute-start(bf16[8,128,256]{2,1,0:T(8,128)(2,1)} %get-tuple-element.34), channel_id=1, source_target_pairs={{0,12},{4,8},{8,4},{12,0},{1,13},{5,9},{9,5},{13,1},{2,14},{6,10},... | collective-permute-start | bytes 1572872 | tf_op jit(solution)/shard_map/ppermute | solution.py:225
  10.7 0.0 collective-permute-start.4
  10.8 0.0 collective-permute-start
  10.8 2.1 %collective-permute-start.1 = (bf16[400,256]{1,0:T(8,128)(2,1)S(1)}, bf16[400,256]{1,0:T(8,128)(2,1)}, u32[]{:S(2)}, u32[]{:S(2)}) collective-permute-start(bf16[400,256]{1,0:T(8,128)(2,1)S(1)} %get-tuple-element.32), channel_id=1, source_target_pairs={{0,8},{4,12},{8,0},{12,4},{1,9},{5,13},{9,1},{13,5},{2,10},{6,14},... | collective-permute-start | bytes 614408 | tf_op jit(solution)/shard_map/ppermute | solution.py:212
  12.9 0.6 fusion.5.cols
  13.5 0.7 stack.34.spot
  14.2 9.1 %collective-permute-done.5.rest_1_ = bf16[8,128,256]{2,1,0:T(8,128)(2,1)S(1)} collective-permute-done((bf16[8,128,256]{2,1,0:T(8,128)(2,1)}, bf16[8,128,256]{2,1,0:T(8,128)(2,1)S(1)}, u32[]{:S(2)}, u32[]{:S(2)}) %collective-permute-start.5) | collective-permute-done | bytes 524320 | tf_op jit(solution)/shard_map/ppermute | solution.py:225
  23.3 1.6 collective-permute-start.7
  24.9 9.7 %collective-permute-done.4.rest_0_ = bf16[8,128,256]{2,1,0:T(8,128)(2,1)} collective-permute-done((bf16[8,128,256]{2,1,0:T(8,128)(2,1)}, bf16[8,128,256]{2,1,0:T(8,128)(2,1)}, u32[]{:S(2)}, u32[]{:S(2)}) %collective-permute-start.4) | collective-permute-done | bytes 524320 | tf_op jit(solution)/shard_map/ppermute | solution.py:225
  34.5 1.6 collective-permute-start.6
  36.1 0.1 slice_reduce_fusion.3
  36.2 2.7 %collective-permute-done.rest_5_ = bf16[400,256]{1,0:T(8,128)(2,1)} collective-permute-done((bf16[400,256]{1,0:T(8,128)(2,1)S(1)}, bf16[400,256]{1,0:T(8,128)(2,1)}, u32[]{:S(2)}, u32[]{:S(2)}) %collective-permute-start) | collective-permute-done | bytes 204832 | tf_op jit(solution)/shard_map/ppermute | solution.py:212
  38.9 0.8 slice_reduce_fusion.2
  39.7 0.8 slice_reduce_fusion.1
  40.5 2.1 %collective-permute-done.2.rest_7_ = bf16[400,256]{1,0:T(8,128)(2,1)S(1)} collective-permute-done((bf16[400,256]{1,0:T(8,128)(2,1)S(1)}, bf16[400,256]{1,0:T(8,128)(2,1)S(1)}, u32[]{:S(2)}, u32[]{:S(2)}) %collective-permute-start.2) | collective-permute-done | bytes 204832 | tf_op jit(solution)/shard_map/ppermute | solution.py:212
  42.6 0.1 slice_reduce_fusion
  42.7 0.6 maximum_convert_fusion.rows
  43.3 6.2 %collective-permute-done.6.rest_2_ = bf16[8,128,256]{2,1,0:T(8,128)(2,1)S(1)} collective-permute-done((bf16[8,128,256]{2,1,0:T(8,128)(2,1)}, bf16[8,128,256]{2,1,0:T(8,128)(2,1)S(1)}, u32[]{:S(2)}, u32[]{:S(2)}) %collective-permute-start.6) | collective-permute-done | bytes 524320 | tf_op jit(solution)/shard_map/ppermute | solution.py:227
  49.6 0.7 copy-done.14
  50.3 0.8 copy-done.9
  51.1 22.6 %layer.1 = (bf16[1024,256]{1,0:T(8,128)(2,1)}, f32[1024,256]{1,0:T(8,128)}, f32[256,256]{1,0:T(8,128)}, f32[256,256]{1,0:T(8,128)}, f32[32,128,256]{2,1,0:T(8,12...) custom-call(s32[8,16]{1,0:T(8,128)} %fusion.5.cols, ...), custom_call_target="tpu_custom_call" | custom-call | tf_op jit(solution)/shard_map/layer/pallas_call | solution.py:245
  73.7 0.2 collective-permute-start.8
  73.9 1.1 collective-permute-start.9
  75.0 1.0 collective-permute-start.10
  75.9 1.1 pad_maximum_fusion
  77.0 3.5 %collective-permute-done.9.rest_1_ = bf16[3,128,256]{2,1,0:T(8,128)(2,1)S(1)} collective-permute-done((bf16[3,128,256]{2,1,0:T(8,128)(2,1)}, bf16[3,128,256]{2,1,0:T(8,128)(2,1)S(1)}, u32[]{:S(2)}, u32[]{:S(2)}) %collective-permute-start.9) | collective-permute-done | bytes 196640 | tf_op jit(solution)/shard_map/ppermute | solution.py:308
  80.5 5.1 %collective-permute-done.10.rest_2_ = bf16[3,128,256]{2,1,0:T(8,128)(2,1)S(1)} collective-permute-done((bf16[3,128,256]{2,1,0:T(8,128)(2,1)}, bf16[3,128,256]{2,1,0:T(8,128)(2,1)S(1)}, u32[]{:S(2)}, u32[]{:S(2)}) %collective-permute-start.10) | collective-permute-done | bytes 196640 | tf_op jit(solution)/shard_map/ppermute | solution.py:308
  85.7 2.2 %copy-done.2 = f32[32,128,256]{2,1,0:T(8,128)S(1)} copy-done((f32[32,128,256]{2,1,0:T(8,128)S(1)}, f32[32,128,256]{2,1,0:T(8,128)}, u32[]{:S(2)}) %copy-start.2) | copy-done | bytes 4194328
  87.8 0.9 copy-done.6
  88.8 1.7 join.1
  90.5 2.0 %copy-done = f32[32,128,256]{2,1,0:T(8,128)} copy-done((f32[32,128,256]{2,1,0:T(8,128)}, f32[32,128,256]{2,1,0:T(8,128)S(1)}, u32[]{:S(2)}) %copy-start) | copy-done | bytes 4194328
  92.5 0.1 collective-permute-start.19
  92.6 0.8 collective-permute-start.15
  93.4 1.0 collective-permute-start.13
  94.4 0.7 collective-permute-start.14
  95.1 1.0 dynamic-slice_add_fusion
  96.1 3.2 %collective-permute-start.20 = (f32[128,256]{1,0:T(8,128)S(1)}, f32[128,256]{1,0:T(8,128)S(1)}, u32[]{:S(2)}, u32[]{:S(2)}) collective-permute-start(f32[128,256]{1,0:T(8,128)S(1)} %constant_dynamic-slice_fusion), channel_id=1, source_target_pairs={{0,1},{1,0},{2,3},{3,2},{4,5},{5,4},{6,7},{7,6},{8,9},{9,8},{10,11... | collective-permute-start | bytes 393224 | tf_op jit(solution)/shard_map/ppermute | solution.py:145
  99.3 7.2 %collective-permute-done.15 = bf16[8,128,256]{2,1,0:T(8,128)(2,1)S(1)} collective-permute-done((bf16[8,128,256]{2,1,0:T(8,128)(2,1)}, bf16[8,128,256]{2,1,0:T(8,128)(2,1)S(1)}, u32[]{:S(2)}, u32[]{:S(2)}) %collective-permute-start.15) | collective-permute-done | bytes 524320 | tf_op jit(solution)/shard_map/ppermute | solution.py:317
  106.5 2.1 %add_convert_fusion.2 = bf16[8,128,256]{2,1,0:T(8,128)(2,1)} fusion(bf16[8,128,256]{2,1,0:T(8,128)(2,1)S(1)} %collective-permute-done.15, f32[32,128,256]{2,1,0:T(8,128)} %copy-done, s32[]{:T(128)S(6)} %select_n.152), kind=kLoop, calls=%fused_computation.3 | loop fusion | flops 786432 | bytes 2097156 | tf_op jit(solution)/shard_map/convert_element_type | solution.py:349
  108.6 2.6 %collective-permute-start.16 = (bf16[8,128,256]{2,1,0:T(8,128)(2,1)}, bf16[8,128,256]{2,1,0:T(8,128)(2,1)}, u32[]{:S(2)}, u32[]{:S(2)}) collective-permute-start(bf16[8,128,256]{2,1,0:T(8,128)(2,1)} %add_convert_fusion.2), channel_id=1, source_target_pairs={{0,1},{1,0},{2,3},{3,2},{4,5},{5,4},{6,7},{7,6},{8,9},{9,8},{10,11... | collective-permute-start | bytes 1572872 | tf_op jit(solution)/shard_map/ppermute | solution.py:352
  111.2 1.9 %collective-permute-start.12 = (bf16[8,128,256]{2,1,0:T(8,128)(2,1)}, bf16[8,128,256]{2,1,0:T(8,128)(2,1)S(1)}, u32[]{:S(2)}, u32[]{:S(2)}) collective-permute-start(bf16[8,128,256]{2,1,0:T(8,128)(2,1)} %get-tuple-element.44), channel_id=1, source_target_pairs={{0,12},{4,8},{8,4},{12,0},{1,13},{5,9},{9,5},{13,1},{2,14},{6,10},... | collective-permute-start | bytes 1572872 | tf_op jit(solution)/shard_map/ppermute | solution.py:317
  113.2 15.8 %collective-permute-done.14 = bf16[8,128,256]{2,1,0:T(8,128)(2,1)S(1)} collective-permute-done((bf16[8,128,256]{2,1,0:T(8,128)(2,1)}, bf16[8,128,256]{2,1,0:T(8,128)(2,1)S(1)}, u32[]{:S(2)}, u32[]{:S(2)}) %collective-permute-start.14) | collective-permute-done | bytes 524320 | tf_op jit(solution)/shard_map/ppermute | solution.py:317
  129.0 3.4 %collective-permute-start.21 = (f32[128,256]{1,0:T(8,128)S(1)}, f32[128,256]{1,0:T(8,128)S(1)}, u32[]{:S(2)}, u32[]{:S(2)}) collective-permute-start(f32[128,256]{1,0:T(8,128)S(1)} %dynamic-slice_add_fusion.1), channel_id=1, source_target_pairs={{0,2},{1,3},{2,0},{3,1},{4,6},{5,7},{6,4},{7,5},{8,10},{9,11},{10,... | collective-permute-start | bytes 393224 | tf_op jit(solution)/shard_map/ppermute | solution.py:149
  132.4 1.3 add_convert_fusion.1
  133.7 1.9 %collective-permute-start.17 = (bf16[8,128,256]{2,1,0:T(8,128)(2,1)S(1)}, bf16[8,128,256]{2,1,0:T(8,128)(2,1)S(1)}, u32[]{:S(2)}, u32[]{:S(2)}) collective-permute-start(bf16[8,128,256]{2,1,0:T(8,128)(2,1)S(1)} %add_convert_fusion.1), channel_id=1, source_target_pairs={{0,1},{1,0},{2,3},{3,2},{4,5},{5,4},{6,7},{7,6},{8,9},{9,8},{10,11... | collective-permute-start | bytes 1572872 | tf_op jit(solution)/shard_map/ppermute | solution.py:352
  135.6 3.5 %collective-permute-done.21 = f32[128,256]{1,0:T(8,128)S(1)} collective-permute-done((f32[128,256]{1,0:T(8,128)S(1)}, f32[128,256]{1,0:T(8,128)S(1)}, u32[]{:S(2)}, u32[]{:S(2)}) %collective-permute-start.21) | collective-permute-done | bytes 131104 | tf_op jit(solution)/shard_map/ppermute | solution.py:149
  139.1 1.0 collective-permute-start.22
  140.2 2.5 %add_convert_fusion = bf16[8,128,256]{2,1,0:T(8,128)(2,1)} fusion(bf16[8,128,256]{2,1,0:T(8,128)(2,1)} %collective-permute-done.16, bf16[8,128,256]{2,1,0:T(8,128)(2,1)} %collective-permute-done.13, f32[32,128,256]{2,1,0:T(8,128)} %copy-done, s32[]{:T(128)S(6)} %select_n.150), kind=kLoop, calls=%fused_computation.1 | loop fusion | flops 1310720 | bytes 2621444 | tf_op jit(solution)/shard_map/convert_element_type | solution.py:349
  142.7 0.3 collective-permute-start.18
  143.0 1.9 %collective-permute-done.22 = f32[128,256]{1,0:T(8,128)S(1)} collective-permute-done((f32[128,256]{1,0:T(8,128)S(1)}, f32[128,256]{1,0:T(8,128)S(1)}, u32[]{:S(2)}, u32[]{:S(2)}) %collective-permute-start.22) | collective-permute-done | bytes 131104 | tf_op jit(solution)/shard_map/ppermute | solution.py:149
  144.9 2.7 %collective-permute-start.23 = (f32[128,256]{1,0:T(8,128)S(1)}, f32[128,256]{1,0:T(8,128)S(1)}, u32[]{:S(2)}, u32[]{:S(2)}) collective-permute-start(f32[128,256]{1,0:T(8,128)S(1)} %add.189), channel_id=1, source_target_pairs={{0,1},{1,0},{2,3},{3,2},{4,5},{5,4},{6,7},{7,6},{8,9},{9,8},{10,11... | collective-permute-start | bytes 393224 | tf_op jit(solution)/shard_map/ppermute | solution.py:152
  147.6 14.0 %collective-permute-done.23 = f32[128,256]{1,0:T(8,128)S(1)} collective-permute-done((f32[128,256]{1,0:T(8,128)S(1)}, f32[128,256]{1,0:T(8,128)S(1)}, u32[]{:S(2)}, u32[]{:S(2)}) %collective-permute-start.23) | collective-permute-done | bytes 131104 | tf_op jit(solution)/shard_map/ppermute | solution.py:152
  161.7 0.1 collective-permute-start.24
  161.8 7.3 %collective-permute-done.18 = bf16[8,128,256]{2,1,0:T(8,128)(2,1)} collective-permute-done((bf16[8,128,256]{2,1,0:T(8,128)(2,1)}, bf16[8,128,256]{2,1,0:T(8,128)(2,1)}, u32[]{:S(2)}, u32[]{:S(2)}) %collective-permute-start.18) | collective-permute-done | bytes 524320 | tf_op jit(solution)/shard_map/ppermute | solution.py:352
  169.1 2.6 %add_add_fusion = f32[8,128,256]{2,1,0:T(8,128)} fusion(f32[8,128,256]{2,1,0:T(8,128)S(1)} %bitcast.29, bf16[8,128,256]{2,1,0:T(8,128)(2,1)} %collective-permute-done.18, bf16[8,128,256]{2,1,0:T(8,128)(2,1)S(1)} %collective-permute-done.17, bf16[8,128,256]{2,1,0:T(8,128)(2,1)S(1)} %collective-permute-done.12, f32[32,128,256]{2,1,0:T(8,128)} %copy-done, ...), kind=kLoop, calls=%fused_computation | loop fusion | flops 1835008 | bytes 4718596 | tf_op jit(solution)/shard_map/add | solution.py:347
  171.7 0.8 fusion.10
  (49 shorter events, 0.3 us)
Async XLA Ops:
  0.6 12.2 %copy-start.16 = (s32[8,16]{1,0:T(8,128)S(1)}, s32[8,16]{1,0:T(8,128)}, u32[]{:S(2)}) copy-start(s32[8,16]{1,0:T(8,128)} %param.12) | copy-start | bytes 1540
  0.6 48.9 %collective-permute-start.3 = (bf16[32,128,256]{2,1,0:T(8,128)(2,1)}, bf16[32,128,256]{2,1,0:T(8,128)(2,1)S(1)}, u32[]{:S(2)}, u32[]{:S(2)}) collective-permute-start(bf16[32,128,256]{2,1,0:T(8,128)(2,1)} %bitcast.18), channel_id=1, source_target_pairs={{0,4},{4,0},{8,12},{12,8},{1,5},{5,1},{9,13},{13,9},{2,6},{6,2},{1... | collective-permute-start | bytes 6291464 | tf_op jit(solution)/shard_map/ppermute | solution.py:217
  2.7 1.6 copy-start.1
  4.3 1.1 copy-start.3
  5.4 0.7 copy-start.7
  7.0 42.5 %copy-start.5 = (bf16[400,256]{1,0:T(8,128)(2,1)}, bf16[400,256]{1,0:T(8,128)(2,1)S(1)}, u32[]{:S(2)}) copy-start(bf16[400,256]{1,0:T(8,128)(2,1)S(1)} %get-tuple-element.30.rest_4_) | copy-start | bytes 614404
  8.1 15.2 %collective-permute-start.5 = (bf16[8,128,256]{2,1,0:T(8,128)(2,1)}, bf16[8,128,256]{2,1,0:T(8,128)(2,1)S(1)}, u32[]{:S(2)}, u32[]{:S(2)}) collective-permute-start(bf16[8,128,256]{2,1,0:T(8,128)(2,1)} %get-tuple-element.34), channel_id=1, source_target_pairs={{0,12},{4,8},{8,4},{12,0},{1,13},{5,9},{9,5},{13,1},{2,14},{6,10},... | collective-permute-start | bytes 1572872 | tf_op jit(solution)/shard_map/ppermute | solution.py:225
  10.7 23.8 %collective-permute-start.4 = (bf16[8,128,256]{2,1,0:T(8,128)(2,1)}, bf16[8,128,256]{2,1,0:T(8,128)(2,1)}, u32[]{:S(2)}, u32[]{:S(2)}) collective-permute-start(bf16[8,128,256]{2,1,0:T(8,128)(2,1)} %get-tuple-element.57), channel_id=1, source_target_pairs={{0,12},{4,8},{8,4},{12,0},{1,13},{5,9},{9,5},{13,1},{2,14},{6,10},... | collective-permute-start | bytes 1572872 | tf_op jit(solution)/shard_map/ppermute | solution.py:225
  10.8 28.2 %collective-permute-start = (bf16[400,256]{1,0:T(8,128)(2,1)S(1)}, bf16[400,256]{1,0:T(8,128)(2,1)}, u32[]{:S(2)}, u32[]{:S(2)}) collective-permute-start(bf16[400,256]{1,0:T(8,128)(2,1)S(1)} %get-tuple-element.31), channel_id=1, source_target_pairs={{0,4},{4,8},{8,12},{12,0},{1,5},{5,9},{9,13},{13,1},{2,6},{6,10},{... | collective-permute-start | bytes 614408 | tf_op jit(solution)/shard_map/ppermute | solution.py:212
  10.8 28.9 %collective-permute-start.1 = (bf16[400,256]{1,0:T(8,128)(2,1)S(1)}, bf16[400,256]{1,0:T(8,128)(2,1)}, u32[]{:S(2)}, u32[]{:S(2)}) collective-permute-start(bf16[400,256]{1,0:T(8,128)(2,1)S(1)} %get-tuple-element.32), channel_id=1, source_target_pairs={{0,8},{4,12},{8,0},{12,4},{1,9},{5,13},{9,1},{13,5},{2,10},{6,14},... | collective-permute-start | bytes 614408 | tf_op jit(solution)/shard_map/ppermute | solution.py:212
  23.3 26.2 %copy-start.12 = (bf16[8,128,256]{2,1,0:T(8,128)(2,1)}, bf16[8,128,256]{2,1,0:T(8,128)(2,1)S(1)}, u32[]{:S(2)}) copy-start(bf16[8,128,256]{2,1,0:T(8,128)(2,1)S(1)} %collective-permute-done.5.rest_1_) | copy-start | bytes 1572868
  23.3 20.0 %collective-permute-start.7 = (bf16[8,128,256]{2,1,0:T(8,128)(2,1)S(1)}, bf16[8,128,256]{2,1,0:T(8,128)(2,1)S(1)}, u32[]{:S(2)}, u32[]{:S(2)}) collective-permute-start(bf16[8,128,256]{2,1,0:T(8,128)(2,1)S(1)} %collective-permute-done.5.rest_1_), channel_id=1, source_target_pairs={{0,1},{1,0},{2,3},{3,2},{4,5},{5,4},{6,7},{7,6},{8,9},{9,8},{10,11... | collective-permute-start | bytes 1572872 | tf_op jit(solution)/shard_map/ppermute | solution.py:227
  34.5 15.0 %collective-permute-start.6 = (bf16[8,128,256]{2,1,0:T(8,128)(2,1)}, bf16[8,128,256]{2,1,0:T(8,128)(2,1)S(1)}, u32[]{:S(2)}, u32[]{:S(2)}) collective-permute-start(bf16[8,128,256]{2,1,0:T(8,128)(2,1)} %collective-permute-done.4.rest_0_), channel_id=1, source_target_pairs={{0,1},{1,0},{2,3},{3,2},{4,5},{5,4},{6,7},{7,6},{8,9},{9,8},{10,11... | collective-permute-start | bytes 1572872 | tf_op jit(solution)/shard_map/ppermute | solution.py:227
  38.9 3.7 %collective-permute-start.2 = (bf16[400,256]{1,0:T(8,128)(2,1)S(1)}, bf16[400,256]{1,0:T(8,128)(2,1)S(1)}, u32[]{:S(2)}, u32[]{:S(2)}) collective-permute-start(bf16[400,256]{1,0:T(8,128)(2,1)S(1)} %get-tuple-element.33), channel_id=1, source_target_pairs={{0,12},{4,0},{8,4},{12,8},{1,13},{5,1},{9,5},{13,9},{2,14},{6,2},{... | collective-permute-start | bytes 614408 | tf_op jit(solution)/shard_map/ppermute | solution.py:212
  42.6 6.9 %copy-start.15 = (bf16[400,256]{1,0:T(8,128)(2,1)}, bf16[400,256]{1,0:T(8,128)(2,1)S(1)}, u32[]{:S(2)}) copy-start(bf16[400,256]{1,0:T(8,128)(2,1)S(1)} %collective-permute-done.2.rest_7_) | copy-start | bytes 614404
  43.3 6.2 %copy-start.13 = (bf16[8,128,256]{2,1,0:T(8,128)(2,1)}, bf16[8,128,256]{2,1,0:T(8,128)(2,1)S(1)}, u32[]{:S(2)}) copy-start(bf16[8,128,256]{2,1,0:T(8,128)(2,1)S(1)} %collective-permute-done.7.rest_3_) | copy-start | bytes 1572868
  49.5 0.8 copy-start.14
  49.5 1.5 copy-start.9
  51.1 34.6 %copy-start.4 = (s32[1,1,4,3,128,128]{5,4,3,2,1,0:T(8,128)S(1)}, s32[1,1,4,3,128,128]{5,4,3,2,1,0:T(8,128)}, u32[]{:S(2)}) copy-start(s32[1,1,4,3,128,128]{5,4,3,2,1,0:T(8,128)} %param.17) | copy-start | bytes 2359300
  51.1 34.6 %copy-start.8 = (s32[1,1,4]{2,1,0:T(1,128)S(1)}, s32[1,1,4]{2,1,0:T(1,128)}, u32[]{:S(2)}) copy-start(s32[1,1,4]{2,1,0:T(1,128)} %param.16) | copy-start | bytes 52
  73.7 11.9 %collective-permute-start.8 = (bf16[32,128,256]{2,1,0:T(8,128)(2,1)}, bf16[32,128,256]{2,1,0:T(8,128)(2,1)S(1)}, u32[]{:S(2)}, u32[]{:S(2)}) collective-permute-start(bf16[32,128,256]{2,1,0:T(8,128)(2,1)} %get-tuple-element.38), channel_id=1, source_target_pairs={{0,4},{4,0},{8,12},{12,8},{1,5},{5,1},{9,13},{13,9},{2,6},{6,2},{1... | collective-permute-start | bytes 6291464 | tf_op jit(solution)/shard_map/ppermute | solution.py:310
  73.9 6.6 %collective-permute-start.9 = (bf16[3,128,256]{2,1,0:T(8,128)(2,1)}, bf16[3,128,256]{2,1,0:T(8,128)(2,1)S(1)}, u32[]{:S(2)}, u32[]{:S(2)}) collective-permute-start(bf16[3,128,256]{2,1,0:T(8,128)(2,1)} %get-tuple-element.40), channel_id=1, source_target_pairs={{0,12},{4,0},{8,4},{12,8},{1,13},{5,1},{9,5},{13,9},{2,14},{6,2},{... | collective-permute-start | bytes 589832 | tf_op jit(solution)/shard_map/ppermute | solution.py:308
  75.0 10.7 %collective-permute-start.10 = (bf16[3,128,256]{2,1,0:T(8,128)(2,1)}, bf16[3,128,256]{2,1,0:T(8,128)(2,1)S(1)}, u32[]{:S(2)}, u32[]{:S(2)}) collective-permute-start(bf16[3,128,256]{2,1,0:T(8,128)(2,1)} %get-tuple-element.41), channel_id=1, source_target_pairs={{0,8},{4,12},{8,0},{12,4},{1,9},{5,13},{9,1},{13,5},{2,10},{6,14},... | collective-permute-start | bytes 589832 | tf_op jit(solution)/shard_map/ppermute | solution.py:308
  75.9 9.7 %collective-permute-start.11 = (bf16[3,128,256]{2,1,0:T(8,128)(2,1)}, bf16[3,128,256]{2,1,0:T(8,128)(2,1)S(1)}, u32[]{:S(2)}, u32[]{:S(2)}) collective-permute-start(bf16[3,128,256]{2,1,0:T(8,128)(2,1)} %get-tuple-element.42), channel_id=1, source_target_pairs={{0,4},{4,8},{8,12},{12,0},{1,5},{5,9},{9,13},{13,1},{2,6},{6,10},{... | collective-permute-start | bytes 589832 | tf_op jit(solution)/shard_map/ppermute | solution.py:308
  77.0 13.5 %copy-start.10 = (f32[512,256]{1,0:T(8,128)}, f32[512,256]{1,0:T(8,128)S(1)}, u32[]{:S(2)}) copy-start(f32[512,256]{1,0:T(8,128)S(1)} %pad_maximum_fusion) | copy-start | bytes 1572868
  85.7 2.2 %copy-start.2 = (f32[32,128,256]{2,1,0:T(8,128)S(1)}, f32[32,128,256]{2,1,0:T(8,128)}, u32[]{:S(2)}) copy-start(f32[32,128,256]{2,1,0:T(8,128)} %get-tuple-element.37.own_ref) | copy-start | bytes 12582916
  87.8 0.9 copy-start.6
  90.5 2.0 %copy-start = (f32[32,128,256]{2,1,0:T(8,128)}, f32[32,128,256]{2,1,0:T(8,128)S(1)}, u32[]{:S(2)}) copy-start(f32[32,128,256]{2,1,0:T(8,128)S(1)} %join.1) | copy-start | bytes 12582916
  92.5 2.6 %collective-permute-start.19 = (f32[256,256]{1,0:T(8,128)S(1)}, f32[256,256]{1,0:T(8,128)S(1)}, u32[]{:S(2)}, u32[]{:S(2)}) collective-permute-start(f32[256,256]{1,0:T(8,128)S(1)} %constant_dynamic-slice_fusion.1), channel_id=1, source_target_pairs={{0,4},{4,0},{8,12},{12,8},{1,5},{5,1},{9,13},{13,9},{2,6},{6,2},{1... | collective-permute-start | bytes 786440 | tf_op jit(solution)/shard_map/ppermute | solution.py:145
  92.6 13.9 %collective-permute-start.15 = (bf16[8,128,256]{2,1,0:T(8,128)(2,1)}, bf16[8,128,256]{2,1,0:T(8,128)(2,1)S(1)}, u32[]{:S(2)}, u32[]{:S(2)}) collective-permute-start(bf16[8,128,256]{2,1,0:T(8,128)(2,1)} %get-tuple-element.49), channel_id=1, source_target_pairs={{0,12},{4,8},{8,4},{12,0},{1,13},{5,9},{9,5},{13,1},{2,14},{6,10},... | collective-permute-start | bytes 1572872 | tf_op jit(solution)/shard_map/ppermute | solution.py:317
  93.4 42.3 %collective-permute-start.13 = (bf16[8,128,256]{2,1,0:T(8,128)(2,1)}, bf16[8,128,256]{2,1,0:T(8,128)(2,1)}, u32[]{:S(2)}, u32[]{:S(2)}) collective-permute-start(bf16[8,128,256]{2,1,0:T(8,128)(2,1)} %get-tuple-element.46), channel_id=1, source_target_pairs={{0,12},{4,8},{8,4},{12,0},{1,13},{5,9},{9,5},{13,1},{2,14},{6,10},... | collective-permute-start | bytes 1572872 | tf_op jit(solution)/shard_map/ppermute | solution.py:317
  94.4 34.6 %collective-permute-start.14 = (bf16[8,128,256]{2,1,0:T(8,128)(2,1)}, bf16[8,128,256]{2,1,0:T(8,128)(2,1)S(1)}, u32[]{:S(2)}, u32[]{:S(2)}) collective-permute-start(bf16[8,128,256]{2,1,0:T(8,128)(2,1)} %get-tuple-element.48), channel_id=1, source_target_pairs={{0,12},{4,8},{8,4},{12,0},{1,13},{5,9},{9,5},{13,1},{2,14},{6,10},... | collective-permute-start | bytes 1572872 | tf_op jit(solution)/shard_map/ppermute | solution.py:317
  96.1 72.9 %copy-start.11 = (f32[1024,256]{1,0:T(8,128)S(1)}, f32[1024,256]{1,0:T(8,128)}, u32[]{:S(2)}) copy-start(f32[1024,256]{1,0:T(8,128)} %get-tuple-element.36) | copy-start | bytes 3145732
  96.1 32.8 %collective-permute-start.20 = (f32[128,256]{1,0:T(8,128)S(1)}, f32[128,256]{1,0:T(8,128)S(1)}, u32[]{:S(2)}, u32[]{:S(2)}) collective-permute-start(f32[128,256]{1,0:T(8,128)S(1)} %constant_dynamic-slice_fusion), channel_id=1, source_target_pairs={{0,1},{1,0},{2,3},{3,2},{4,5},{5,4},{6,7},{7,6},{8,9},{9,8},{10,11... | collective-permute-start | bytes 393224 | tf_op jit(solution)/shard_map/ppermute | solution.py:145
  108.6 31.5 %collective-permute-start.16 = (bf16[8,128,256]{2,1,0:T(8,128)(2,1)}, bf16[8,128,256]{2,1,0:T(8,128)(2,1)}, u32[]{:S(2)}, u32[]{:S(2)}) collective-permute-start(bf16[8,128,256]{2,1,0:T(8,128)(2,1)} %add_convert_fusion.2), channel_id=1, source_target_pairs={{0,1},{1,0},{2,3},{3,2},{4,5},{5,4},{6,7},{7,6},{8,9},{9,8},{10,11... | collective-permute-start | bytes 1572872 | tf_op jit(solution)/shard_map/ppermute | solution.py:352
  111.2 36.4 %collective-permute-start.12 = (bf16[8,128,256]{2,1,0:T(8,128)(2,1)}, bf16[8,128,256]{2,1,0:T(8,128)(2,1)S(1)}, u32[]{:S(2)}, u32[]{:S(2)}) collective-permute-start(bf16[8,128,256]{2,1,0:T(8,128)(2,1)} %get-tuple-element.44), channel_id=1, source_target_pairs={{0,12},{4,8},{8,4},{12,0},{1,13},{5,9},{9,5},{13,1},{2,14},{6,10},... | collective-permute-start | bytes 1572872 | tf_op jit(solution)/shard_map/ppermute | solution.py:317
  129.0 10.1 %collective-permute-start.21 = (f32[128,256]{1,0:T(8,128)S(1)}, f32[128,256]{1,0:T(8,128)S(1)}, u32[]{:S(2)}, u32[]{:S(2)}) collective-permute-start(f32[128,256]{1,0:T(8,128)S(1)} %dynamic-slice_add_fusion.1), channel_id=1, source_target_pairs={{0,2},{1,3},{2,0},{3,1},{4,6},{5,7},{6,4},{7,5},{8,10},{9,11},{10,... | collective-permute-start | bytes 393224 | tf_op jit(solution)/shard_map/ppermute | solution.py:149
  133.7 28.0 %collective-permute-start.17 = (bf16[8,128,256]{2,1,0:T(8,128)(2,1)S(1)}, bf16[8,128,256]{2,1,0:T(8,128)(2,1)S(1)}, u32[]{:S(2)}, u32[]{:S(2)}) collective-permute-start(bf16[8,128,256]{2,1,0:T(8,128)(2,1)S(1)} %add_convert_fusion.1), channel_id=1, source_target_pairs={{0,1},{1,0},{2,3},{3,2},{4,5},{5,4},{6,7},{7,6},{8,9},{9,8},{10,11... | collective-permute-start | bytes 1572872 | tf_op jit(solution)/shard_map/ppermute | solution.py:352
  139.1 5.8 %collective-permute-start.22 = (f32[128,256]{1,0:T(8,128)S(1)}, f32[128,256]{1,0:T(8,128)S(1)}, u32[]{:S(2)}, u32[]{:S(2)}) collective-permute-start(f32[128,256]{1,0:T(8,128)S(1)} %add.188), channel_id=1, source_target_pairs={{0,8},{4,12},{8,0},{12,4},{1,9},{5,13},{9,1},{13,5},{2,10},{6,14},... | collective-permute-start | bytes 393224 | tf_op jit(solution)/shard_map/ppermute | solution.py:149
  142.7 26.4 %collective-permute-start.18 = (bf16[8,128,256]{2,1,0:T(8,128)(2,1)}, bf16[8,128,256]{2,1,0:T(8,128)(2,1)}, u32[]{:S(2)}, u32[]{:S(2)}) collective-permute-start(bf16[8,128,256]{2,1,0:T(8,128)(2,1)} %add_convert_fusion), channel_id=1, source_target_pairs={{0,2},{1,3},{2,0},{3,1},{4,6},{5,7},{6,4},{7,5},{8,10},{9,11},{10,... | collective-permute-start | bytes 1572872 | tf_op jit(solution)/shard_map/ppermute | solution.py:352
  144.9 16.7 %collective-permute-start.23 = (f32[128,256]{1,0:T(8,128)S(1)}, f32[128,256]{1,0:T(8,128)S(1)}, u32[]{:S(2)}, u32[]{:S(2)}) collective-permute-start(f32[128,256]{1,0:T(8,128)S(1)} %add.189), channel_id=1, source_target_pairs={{0,1},{1,0},{2,3},{3,2},{4,5},{5,4},{6,7},{7,6},{8,9},{9,8},{10,11... | collective-permute-start | bytes 393224 | tf_op jit(solution)/shard_map/ppermute | solution.py:152
  161.7 10.0 %collective-permute-start.24 = (f32[256,256]{1,0:T(8,128)S(1)}, f32[256,256]{1,0:T(8,128)S(1)}, u32[]{:S(2)}, u32[]{:S(2)}) collective-permute-start(f32[256,256]{1,0:T(8,128)S(1)} %pad_maximum_fusion.1), channel_id=1, source_target_pairs={{0,4},{4,0},{8,12},{12,8},{1,5},{5,1},{9,13},{13,9},{2,6},{6,2},{1... | collective-permute-start | bytes 786440 | tf_op jit(solution)/shard_map/ppermute | solution.py:152

commit v4 on v2

--- a/solution.py
+++ b/solution.py
@@ -134,15 +134,17 @@
                 out_ref[cols[p, s]] += outer(adj_ref[p, s].astype(BF16), ret_refs[k][s])
 
 
-def summed(value, node, member, n_node, n_feat):
+def summed(value, gates, node, member, n_node, n_feat):
     rounds = [("node", node, n_node), ("feat", member, n_feat)]
-    for axis, at, size in rounds:
+    for (axis, at, size), gate in zip(rounds, gates):
+        value, _ = lax.optimization_barrier((value, gate))
         half = value.shape[0] // 2
         bit = at % 2
         pairs = [(i, i ^ 1) for i in range(size)]
         away = lax.dynamic_slice_in_dim(value, (1 - bit) * half, half, 0)
         kept = lax.dynamic_slice_in_dim(value, bit * half, half, 0)
         value = kept + lax.ppermute(away, axis, pairs)
+    value, *_ = lax.optimization_barrier((value, *gates[2:]))
     for axis, size in (("feat", n_feat), ("node", n_node)):
         step = 2
         while step < size:
@@ -304,22 +306,20 @@
     cross_wide = results[6 : 6 + n_feat]
     send_back = results[6 + n_feat :]
 
+    in_terms = lax.ppermute(in_wide, "node", in_pairs)
+    odd_first = sorted(range(n_feat), key=lambda d: ((d & -d) if d else n_feat, -d))
+    cross_terms = {}
+
+    for d in odd_first:
+        outgoing = cross_wide[d]
+        cross_terms[d] = lax.ppermute(outgoing, "node", cross_pairs)
     returned = [send_back[0]] + [
         lax.ppermute(send_back[k], "node", dist(n_node - k)) for k in range(1, n_node)
     ]
-    in_terms = lax.ppermute(in_wide, "node", in_pairs)
-    odd_first = sorted(range(n_feat), key=lambda d: ((d & -d) if d else n_feat, -d))
-    cross_terms = {}
-    for d in odd_first:
-        outgoing = cross_wide[d]
-        if d % 2 == 0:
-            outgoing, _ = lax.optimization_barrier((outgoing, in_terms if d == 0 else returned[1]))
-        cross_terms[d] = lax.ppermute(outgoing, "node", cross_pairs)
     grad_scale = 1.0 / math.sqrt(block_rows * n_node)
-    both, _ = lax.optimization_barrier(
-        (jnp.concatenate([part_self, part_neigh], 0), returned[n_node - 1])
-    )
-    both = summed(both, node, member, n_node, n_feat)
+    both = jnp.concatenate([part_self, part_neigh], 0)
+    gates = [cross_terms[d] for d in odd_first]
+    both = summed(both, gates, node, member, n_node, n_feat)
     both = both * grad_scale
 
     base = pl.pallas_call(

time: 163 us -> 192 us (1.18)
  waiting for transfers between devices: 83.2 us -> 110 us
  other arithmetic: 8.82 us -> 12.7 us
  starting transfers between devices: 29 us -> 25.6 us
    ppermute x4, waiting for transfers between devices: 11.9 us -> 31.5 us  [shards(): cross_terms[d] = lax.ppermute(outgoing, 'node', cross_pairs)]
    ppermute x3, waiting for transfers between devices: 18.9 us -> 33.1 us  [shards(): lax.ppermute(sent, 'feat', [(i, i ^ step) for i in range(n_feat)])]
    ppermute x3, waiting for transfers between devices: 5.86 us -> 0.01 us  [shards(): lax.ppermute(send_back[k], 'node', dist(n_node - k))]
    ppermute x3, starting transfers between devices: 7.58 us -> 3.5 us  [shards(): lax.ppermute(sent, 'feat', [(i, i ^ step) for i in range(n_feat)])]
    convert_element_type x3, other arithmetic: 1.63 us -> 3.75 us  [shards(): sent = chunk.astype(BF16)]
    unnamed x34 -> x32, local copies, waits for them, and re-layouts: 9.56 us -> 9.56 us
  transfers between devices with their start and end apart: 25 -> 25, of which waited for: 16 -> 15; matrix products, arithmetic and copies ran while one was open for 9% -> 9% of each run, Pallas kernels for 2% -> 2%
where the time goes in v4:
time: 192 us; the launch traced here: 191 us
  waiting for transfers between devices  110 us (57%)
  Pallas kernels  25.7 us (13%)
  starting transfers between devices  25.6 us (13%)
  local copies, waits for them, and re-layouts  15.5 us (8%)
  other arithmetic  12.7 us (7%)
    ppermute x3, waiting for transfers between devices, shards(): lax.ppermute(sent, 'feat', [(i, i ^ step) for i in range(n_feat)])  33.1 us
    ppermute x4, waiting for transfers between devices, shards(): cross_terms[d] = lax.ppermute(outgoing, 'node', cross_pairs)  31.5 us
    pallas_call x1, Pallas kernels, shards(): pl.pallas_call(functools.partial(main_kernel, dims), out_shape=[jax.Shape...  22.6 us
    ppermute x2, waiting for transfers between devices, shards(): direct.append(lax.ppermute(piece, 'node', cross_pairs))  18.9 us
    ppermute x2, waiting for transfers between devices, summed(): lax.ppermute(value, axis, [(i, i ^ step) for i in range(size)])  11.2 us
    unnamed x32, local copies, waits for them, and re-layouts  9.56 us
    ppermute x2, waiting for transfers between devices, shards(): relayed.append(lax.ppermute(piece, 'feat', feat_pairs))  6.19 us
    ppermute x3, waiting for transfers between devices, shards(): lax.ppermute(parts[k], 'node', dist(k))  4.8 us
  transfers between devices with their start and end apart: 25, of which 15 were waited for; matrix products, arithmetic and copies ran while one was open for 9% of the time, Pallas kernels for 2%

profile of v4, /device:TPU:0, one launch (start us, length us, event | category | flops | bytes accessed | tf_op | source)
XLA Modules:
  0.0 190.6 jit_solution(17456795802374946794)
XLA Ops:
  0.6 0.5 collective-permute-start.3
  1.2 0.8 copy.17
  1.9 0.8 copy.18
  2.7 1.6 copy-done
  4.3 1.1 copy-done.2
  5.4 0.7 copy-done.6
  6.1 1.0 far_partial.1
  7.0 1.0 constant_dynamic-slice_fusion.2
  8.1 2.6 %collective-permute-start.5 = (bf16[8,128,256]{2,1,0:T(8,128)(2,1)}, bf16[8,128,256]{2,1,0:T(8,128)(2,1)S(1)}, u32[]{:S(2)}, u32[]{:S(2)}) collective-permute-start(bf16[8,128,256]{2,1,0:T(8,128)(2,1)} %get-tuple-element.33), channel_id=1, source_target_pairs={{0,12},{4,8},{8,4},{12,0},{1,13},{5,9},{9,5},{13,1},{2,14},{6,10},... | collective-permute-start | bytes 1572872 | tf_op jit(solution)/shard_map/ppermute | solution.py:227
  10.8 2.1 %collective-permute-start.1 = (bf16[400,256]{1,0:T(8,128)(2,1)S(1)}, bf16[400,256]{1,0:T(8,128)(2,1)}, u32[]{:S(2)}, u32[]{:S(2)}) collective-permute-start(bf16[400,256]{1,0:T(8,128)(2,1)S(1)} %get-tuple-element.31), channel_id=1, source_target_pairs={{0,8},{4,12},{8,0},{12,4},{1,9},{5,13},{9,1},{13,5},{2,10},{6,14},... | collective-permute-start | bytes 614408 | tf_op jit(solution)/shard_map/ppermute | solution.py:214
  12.8 0.6 fusion.5.cols
  13.5 0.6 stack.34.spot
  14.1 9.2 %collective-permute-done.5.rest_1_ = bf16[8,128,256]{2,1,0:T(8,128)(2,1)S(1)} collective-permute-done((bf16[8,128,256]{2,1,0:T(8,128)(2,1)}, bf16[8,128,256]{2,1,0:T(8,128)(2,1)S(1)}, u32[]{:S(2)}, u32[]{:S(2)}) %collective-permute-start.5) | collective-permute-done | bytes 524320 | tf_op jit(solution)/shard_map/ppermute | solution.py:227
  23.3 1.6 collective-permute-start.7
  24.9 9.7 %collective-permute-done.4.rest_0_ = bf16[8,128,256]{2,1,0:T(8,128)(2,1)} collective-permute-done((bf16[8,128,256]{2,1,0:T(8,128)(2,1)}, bf16[8,128,256]{2,1,0:T(8,128)(2,1)}, u32[]{:S(2)}, u32[]{:S(2)}) %collective-permute-start.4) | collective-permute-done | bytes 524320 | tf_op jit(solution)/shard_map/ppermute | solution.py:227
  34.5 1.6 collective-permute-start.6
  36.2 2.7 %collective-permute-done.rest_5_ = bf16[400,256]{1,0:T(8,128)(2,1)} collective-permute-done((bf16[400,256]{1,0:T(8,128)(2,1)S(1)}, bf16[400,256]{1,0:T(8,128)(2,1)}, u32[]{:S(2)}, u32[]{:S(2)}) %collective-permute-start) | collective-permute-done | bytes 204832 | tf_op jit(solution)/shard_map/ppermute | solution.py:214
  38.9 0.8 slice_reduce_fusion.2
  39.7 0.8 slice_reduce_fusion.1
  40.5 2.1 %collective-permute-done.2.rest_7_ = bf16[400,256]{1,0:T(8,128)(2,1)S(1)} collective-permute-done((bf16[400,256]{1,0:T(8,128)(2,1)S(1)}, bf16[400,256]{1,0:T(8,128)(2,1)S(1)}, u32[]{:S(2)}, u32[]{:S(2)}) %collective-permute-start.2) | collective-permute-done | bytes 204832 | tf_op jit(solution)/shard_map/ppermute | solution.py:214
  42.7 0.6 maximum_convert_fusion.rows
  43.3 6.2 %collective-permute-done.6.rest_2_ = bf16[8,128,256]{2,1,0:T(8,128)(2,1)S(1)} collective-permute-done((bf16[8,128,256]{2,1,0:T(8,128)(2,1)}, bf16[8,128,256]{2,1,0:T(8,128)(2,1)S(1)}, u32[]{:S(2)}, u32[]{:S(2)}) %collective-permute-start.6) | collective-permute-done | bytes 524320 | tf_op jit(solution)/shard_map/ppermute | solution.py:229
  49.5 0.8 copy-done.12
  50.3 0.8 copy-done.8
  51.1 22.6 %layer.1 = (bf16[1024,256]{1,0:T(8,128)(2,1)}, f32[1024,256]{1,0:T(8,128)}, f32[256,256]{1,0:T(8,128)}, f32[256,256]{1,0:T(8,128)}, f32[32,128,256]{2,1,0:T(8,12...) custom-call(s32[8,16]{1,0:T(8,128)} %fusion.5.cols, ...), custom_call_target="tpu_custom_call" | custom-call | tf_op jit(solution)/shard_map/layer/pallas_call | solution.py:247
  73.7 0.2 collective-permute-start.8
  73.8 1.1 collective-permute-start.15
  74.9 0.7 collective-permute-start.14
  75.6 1.1 pad_maximum_fusion
  76.6 11.2 %collective-permute-done.15 = bf16[8,128,256]{2,1,0:T(8,128)(2,1)} collective-permute-done((bf16[8,128,256]{2,1,0:T(8,128)(2,1)}, bf16[8,128,256]{2,1,0:T(8,128)(2,1)}, u32[]{:S(2)}, u32[]{:S(2)}) %collective-permute-start.15) | collective-permute-done | bytes 524320 | tf_op jit(solution)/shard_map/ppermute | solution.py:315
  87.8 0.7 constant_dynamic-slice_fusion.1
  88.5 1.2 collective-permute-start.19
  89.8 0.6 collective-permute-start.12
  90.4 1.1 collective-permute-start.13
  91.5 1.7 dynamic-slice_add_fusion
  93.2 5.8 %collective-permute-done.14 = bf16[8,128,256]{2,1,0:T(8,128)(2,1)} collective-permute-done((bf16[8,128,256]{2,1,0:T(8,128)(2,1)}, bf16[8,128,256]{2,1,0:T(8,128)(2,1)}, u32[]{:S(2)}, u32[]{:S(2)}) %collective-permute-start.14) | collective-permute-done | bytes 524320 | tf_op jit(solution)/shard_map/ppermute | solution.py:315
  99.0 0.9 constant_dynamic-slice_fusion
  100.0 1.7 collective-permute-start.20
  101.6 4.5 %collective-permute-done.20 = f32[128,256]{1,0:T(8,128)S(1)} collective-permute-done((f32[128,256]{1,0:T(8,128)S(1)}, f32[128,256]{1,0:T(8,128)S(1)}, u32[]{:S(2)}, u32[]{:S(2)}) %collective-permute-start.20) | collective-permute-done | bytes 131104 | tf_op jit(solution)/shard_map/ppermute | solution.py:146
  106.1 0.9 dynamic-slice_add_fusion.1
  107.1 3.2 %collective-permute-done.12 = bf16[8,128,256]{2,1,0:T(8,128)(2,1)} collective-permute-done((bf16[8,128,256]{2,1,0:T(8,128)(2,1)}, bf16[8,128,256]{2,1,0:T(8,128)(2,1)}, u32[]{:S(2)}, u32[]{:S(2)}) %collective-permute-start.12) | collective-permute-done | bytes 524320 | tf_op jit(solution)/shard_map/ppermute | solution.py:315
  110.3 11.2 %collective-permute-done.13 = bf16[8,128,256]{2,1,0:T(8,128)(2,1)} collective-permute-done((bf16[8,128,256]{2,1,0:T(8,128)(2,1)}, bf16[8,128,256]{2,1,0:T(8,128)(2,1)}, u32[]{:S(2)}, u32[]{:S(2)}) %collective-permute-start.13) | collective-permute-done | bytes 524320 | tf_op jit(solution)/shard_map/ppermute | solution.py:315
  121.5 2.5 %collective-permute-start.21 = (f32[128,256]{1,0:T(8,128)S(1)}, f32[128,256]{1,0:T(8,128)S(1)}, u32[]{:S(2)}, u32[]{:S(2)}) collective-permute-start(f32[128,256]{1,0:T(8,128)S(1)} %dynamic-slice_add_fusion.1), channel_id=1, source_target_pairs={{0,2},{1,3},{2,0},{3,1},{4,6},{5,7},{6,4},{7,5},{8,10},{9,11},{10,... | collective-permute-start | bytes 393224 | tf_op jit(solution)/shard_map/ppermute | solution.py:151
  124.0 0.8 collective-permute-start.9
  124.9 0.9 collective-permute-start.10
  125.8 5.2 %collective-permute-done.21 = f32[128,256]{1,0:T(8,128)S(1)} collective-permute-done((f32[128,256]{1,0:T(8,128)S(1)}, f32[128,256]{1,0:T(8,128)S(1)}, u32[]{:S(2)}, u32[]{:S(2)}) %collective-permute-start.21) | collective-permute-done | bytes 131104 | tf_op jit(solution)/shard_map/ppermute | solution.py:151
  131.0 0.7 add.188
  131.7 1.1 collective-permute-start.22
  132.8 5.9 %collective-permute-done.22 = f32[128,256]{1,0:T(8,128)} collective-permute-done((f32[128,256]{1,0:T(8,128)}, f32[128,256]{1,0:T(8,128)}, u32[]{:S(2)}, u32[]{:S(2)}) %collective-permute-start.22) | collective-permute-done | bytes 131104 | tf_op jit(solution)/shard_map/ppermute | solution.py:151
  138.7 1.0 add.189
  139.7 1.7 collective-permute-start.23
  141.5 2.2 %copy-done.1 = f32[32,128,256]{2,1,0:T(8,128)S(1)} copy-done((f32[32,128,256]{2,1,0:T(8,128)S(1)}, f32[32,128,256]{2,1,0:T(8,128)}, u32[]{:S(2)}) %copy-start.1) | copy-done | bytes 4194328
  143.7 0.9 copy-done.5
  144.6 2.2 %join.1 = f32[32,128,256]{2,1,0:T(8,128)S(1)} custom-call(s32[4,3]{1,0:T(4,128)S(1)} %bitcast.25, s32[4]{0:T(128)S(1)} %bitcast.28, s32[1]{0:T(128)} %bitcast.3.node, f32[32,128,256]{2,1,0:T(8,128)S(1)} %copy-done.1, bf16[32,128,256]{2,1,0:T(8,128)(2,1)S(1)} %collective-permute-done.8.in_ref, s32[4,3,128,128]{3,2,1,0:T(8,128)S(1)} %bitcast.23, ...), custom_call_target="tpu_custom_call" | custom-call | tf_op jit(solution)/shard_map/join/pallas_call | solution.py:325
  146.8 1.2 add_convert_fusion.2
  148.2 1.3 add_convert_fusion.1
  149.5 2.1 %collective-permute-start.17 = (bf16[8,128,256]{2,1,0:T(8,128)(2,1)S(1)}, bf16[8,128,256]{2,1,0:T(8,128)(2,1)S(1)}, u32[]{:S(2)}, u32[]{:S(2)}) collective-permute-start(bf16[8,128,256]{2,1,0:T(8,128)(2,1)S(1)} %add_convert_fusion.1), channel_id=1, source_target_pairs={{0,1},{1,0},{2,3},{3,2},{4,5},{5,4},{6,7},{7,6},{8,9},{9,8},{10,11... | collective-permute-start | bytes 1572872 | tf_op jit(solution)/shard_map/ppermute | solution.py:352
  151.6 11.3 %collective-permute-done.16 = bf16[8,128,256]{2,1,0:T(8,128)(2,1)S(1)} collective-permute-done((bf16[8,128,256]{2,1,0:T(8,128)(2,1)S(1)}, bf16[8,128,256]{2,1,0:T(8,128)(2,1)S(1)}, u32[]{:S(2)}, u32[]{:S(2)}) %collective-permute-start.16) | collective-permute-done | bytes 524320 | tf_op jit(solution)/shard_map/ppermute | solution.py:352
  162.8 1.3 add_convert_fusion
  164.1 1.4 collective-permute-start.18
  165.6 0.8 fusion.10
  166.4 13.5 %collective-permute-done.17 = bf16[8,128,256]{2,1,0:T(8,128)(2,1)S(1)} collective-permute-done((bf16[8,128,256]{2,1,0:T(8,128)(2,1)S(1)}, bf16[8,128,256]{2,1,0:T(8,128)(2,1)S(1)}, u32[]{:S(2)}, u32[]{:S(2)}) %collective-permute-start.17) | collective-permute-done | bytes 524320 | tf_op jit(solution)/shard_map/ppermute | solution.py:352
  179.9 8.4 %collective-permute-done.18 = bf16[8,128,256]{2,1,0:T(8,128)(2,1)S(1)} collective-permute-done((bf16[8,128,256]{2,1,0:T(8,128)(2,1)S(1)}, bf16[8,128,256]{2,1,0:T(8,128)(2,1)S(1)}, u32[]{:S(2)}, u32[]{:S(2)}) %collective-permute-start.18) | collective-permute-done | bytes 524320 | tf_op jit(solution)/shard_map/ppermute | solution.py:352
  188.2 2.3 %add_add_fusion = f32[8,128,256]{2,1,0:T(8,128)} fusion(f32[8,128,256]{2,1,0:T(8,128)S(1)} %bitcast.29, bf16[8,128,256]{2,1,0:T(8,128)(2,1)S(1)} %collective-permute-done.18, bf16[8,128,256]{2,1,0:T(8,128)(2,1)S(1)} %collective-permute-done.17, bf16[8,128,256]{2,1,0:T(8,128)(2,1)} %collective-permute-done.12, f32[32,128,256]{2,1,0:T(8,128)S(1)} %join.1, ...), kind=kLoop, calls=%fused_computation | loop fusion | flops 1835008 | bytes 4718596 | tf_op jit(solution)/shard_map/add | solution.py:347
  (45 shorter events, 0.6 us)
Async XLA Ops:
  0.6 12.2 %copy-start.14 = (s32[8,16]{1,0:T(8,128)S(1)}, s32[8,16]{1,0:T(8,128)}, u32[]{:S(2)}) copy-start(s32[8,16]{1,0:T(8,128)} %param.12) | copy-start | bytes 1540
  0.6 48.9 %collective-permute-start.3 = (bf16[32,128,256]{2,1,0:T(8,128)(2,1)}, bf16[32,128,256]{2,1,0:T(8,128)(2,1)S(1)}, u32[]{:S(2)}, u32[]{:S(2)}) collective-permute-start(bf16[32,128,256]{2,1,0:T(8,128)(2,1)} %bitcast.18), channel_id=1, source_target_pairs={{0,4},{4,0},{8,12},{12,8},{1,5},{5,1},{9,13},{13,9},{2,6},{6,2},{1... | collective-permute-start | bytes 6291464 | tf_op jit(solution)/shard_map/ppermute | solution.py:219
  2.7 1.6 copy-start
  4.3 1.1 copy-start.2
  5.4 0.7 copy-start.6
  7.0 42.5 %copy-start.4 = (bf16[400,256]{1,0:T(8,128)(2,1)}, bf16[400,256]{1,0:T(8,128)(2,1)S(1)}, u32[]{:S(2)}) copy-start(bf16[400,256]{1,0:T(8,128)(2,1)S(1)} %get-tuple-element.29.rest_4_) | copy-start | bytes 614404
  8.1 15.2 %collective-permute-start.5 = (bf16[8,128,256]{2,1,0:T(8,128)(2,1)}, bf16[8,128,256]{2,1,0:T(8,128)(2,1)S(1)}, u32[]{:S(2)}, u32[]{:S(2)}) collective-permute-start(bf16[8,128,256]{2,1,0:T(8,128)(2,1)} %get-tuple-element.33), channel_id=1, source_target_pairs={{0,12},{4,8},{8,4},{12,0},{1,13},{5,9},{9,5},{13,1},{2,14},{6,10},... | collective-permute-start | bytes 1572872 | tf_op jit(solution)/shard_map/ppermute | solution.py:227
  10.7 23.8 %collective-permute-start.4 = (bf16[8,128,256]{2,1,0:T(8,128)(2,1)}, bf16[8,128,256]{2,1,0:T(8,128)(2,1)}, u32[]{:S(2)}, u32[]{:S(2)}) collective-permute-start(bf16[8,128,256]{2,1,0:T(8,128)(2,1)} %get-tuple-element.55), channel_id=1, source_target_pairs={{0,12},{4,8},{8,4},{12,0},{1,13},{5,9},{9,5},{13,1},{2,14},{6,10},... | collective-permute-start | bytes 1572872 | tf_op jit(solution)/shard_map/ppermute | solution.py:227
  10.7 28.2 %collective-permute-start = (bf16[400,256]{1,0:T(8,128)(2,1)S(1)}, bf16[400,256]{1,0:T(8,128)(2,1)}, u32[]{:S(2)}, u32[]{:S(2)}) collective-permute-start(bf16[400,256]{1,0:T(8,128)(2,1)S(1)} %get-tuple-element.30), channel_id=1, source_target_pairs={{0,4},{4,8},{8,12},{12,0},{1,5},{5,9},{9,13},{13,1},{2,6},{6,10},{... | collective-permute-start | bytes 614408 | tf_op jit(solution)/shard_map/ppermute | solution.py:214
  10.8 28.9 %collective-permute-start.1 = (bf16[400,256]{1,0:T(8,128)(2,1)S(1)}, bf16[400,256]{1,0:T(8,128)(2,1)}, u32[]{:S(2)}, u32[]{:S(2)}) collective-permute-start(bf16[400,256]{1,0:T(8,128)(2,1)S(1)} %get-tuple-element.31), channel_id=1, source_target_pairs={{0,8},{4,12},{8,0},{12,4},{1,9},{5,13},{9,1},{13,5},{2,10},{6,14},... | collective-permute-start | bytes 614408 | tf_op jit(solution)/shard_map/ppermute | solution.py:214
  23.3 26.2 %copy-start.10 = (bf16[8,128,256]{2,1,0:T(8,128)(2,1)}, bf16[8,128,256]{2,1,0:T(8,128)(2,1)S(1)}, u32[]{:S(2)}) copy-start(bf16[8,128,256]{2,1,0:T(8,128)(2,1)S(1)} %collective-permute-done.5.rest_1_) | copy-start | bytes 1572868
  23.3 20.0 %collective-permute-start.7 = (bf16[8,128,256]{2,1,0:T(8,128)(2,1)S(1)}, bf16[8,128,256]{2,1,0:T(8,128)(2,1)S(1)}, u32[]{:S(2)}, u32[]{:S(2)}) collective-permute-start(bf16[8,128,256]{2,1,0:T(8,128)(2,1)S(1)} %collective-permute-done.5.rest_1_), channel_id=1, source_target_pairs={{0,1},{1,0},{2,3},{3,2},{4,5},{5,4},{6,7},{7,6},{8,9},{9,8},{10,11... | collective-permute-start | bytes 1572872 | tf_op jit(solution)/shard_map/ppermute | solution.py:229
  34.5 15.0 %collective-permute-start.6 = (bf16[8,128,256]{2,1,0:T(8,128)(2,1)}, bf16[8,128,256]{2,1,0:T(8,128)(2,1)S(1)}, u32[]{:S(2)}, u32[]{:S(2)}) collective-permute-start(bf16[8,128,256]{2,1,0:T(8,128)(2,1)} %collective-permute-done.4.rest_0_), channel_id=1, source_target_pairs={{0,1},{1,0},{2,3},{3,2},{4,5},{5,4},{6,7},{7,6},{8,9},{9,8},{10,11... | collective-permute-start | bytes 1572872 | tf_op jit(solution)/shard_map/ppermute | solution.py:229
  38.9 3.7 %collective-permute-start.2 = (bf16[400,256]{1,0:T(8,128)(2,1)S(1)}, bf16[400,256]{1,0:T(8,128)(2,1)S(1)}, u32[]{:S(2)}, u32[]{:S(2)}) collective-permute-start(bf16[400,256]{1,0:T(8,128)(2,1)S(1)} %get-tuple-element.32), channel_id=1, source_target_pairs={{0,12},{4,0},{8,4},{12,8},{1,13},{5,1},{9,5},{13,9},{2,14},{6,2},{... | collective-permute-start | bytes 614408 | tf_op jit(solution)/shard_map/ppermute | solution.py:214
  42.6 6.9 %copy-start.13 = (bf16[400,256]{1,0:T(8,128)(2,1)}, bf16[400,256]{1,0:T(8,128)(2,1)S(1)}, u32[]{:S(2)}) copy-start(bf16[400,256]{1,0:T(8,128)(2,1)S(1)} %collective-permute-done.2.rest_7_) | copy-start | bytes 614404
  43.3 6.2 %copy-start.11 = (bf16[8,128,256]{2,1,0:T(8,128)(2,1)}, bf16[8,128,256]{2,1,0:T(8,128)(2,1)S(1)}, u32[]{:S(2)}) copy-start(bf16[8,128,256]{2,1,0:T(8,128)(2,1)S(1)} %collective-permute-done.7.rest_3_) | copy-start | bytes 1572868
  49.5 0.8 copy-start.12
  49.5 1.5 copy-start.8
  51.0 90.4 %copy-start.7 = (s32[1,1,4]{2,1,0:T(1,128)S(1)}, s32[1,1,4]{2,1,0:T(1,128)}, u32[]{:S(2)}) copy-start(s32[1,1,4]{2,1,0:T(1,128)} %param.16) | copy-start | bytes 52
  73.7 67.8 %copy-start.3 = (s32[1,1,4,3,128,128]{5,4,3,2,1,0:T(8,128)S(1)}, s32[1,1,4,3,128,128]{5,4,3,2,1,0:T(8,128)}, u32[]{:S(2)}) copy-start(s32[1,1,4,3,128,128]{5,4,3,2,1,0:T(8,128)} %param.17) | copy-start | bytes 2359300
  73.7 67.8 %collective-permute-start.8 = (bf16[32,128,256]{2,1,0:T(8,128)(2,1)}, bf16[32,128,256]{2,1,0:T(8,128)(2,1)S(1)}, u32[]{:S(2)}, u32[]{:S(2)}) collective-permute-start(bf16[32,128,256]{2,1,0:T(8,128)(2,1)} %get-tuple-element.37), channel_id=1, source_target_pairs={{0,4},{4,0},{8,12},{12,8},{1,5},{5,1},{9,13},{13,9},{2,6},{6,2},{1... | collective-permute-start | bytes 6291464 | tf_op jit(solution)/shard_map/ppermute | solution.py:309
  73.8 14.0 %collective-permute-start.15 = (bf16[8,128,256]{2,1,0:T(8,128)(2,1)}, bf16[8,128,256]{2,1,0:T(8,128)(2,1)}, u32[]{:S(2)}, u32[]{:S(2)}) collective-permute-start(bf16[8,128,256]{2,1,0:T(8,128)(2,1)} %get-tuple-element.45), channel_id=1, source_target_pairs={{0,12},{4,8},{8,4},{12,0},{1,13},{5,9},{9,5},{13,1},{2,14},{6,10},... | collective-permute-start | bytes 1572872 | tf_op jit(solution)/shard_map/ppermute | solution.py:315
  74.9 24.1 %collective-permute-start.14 = (bf16[8,128,256]{2,1,0:T(8,128)(2,1)}, bf16[8,128,256]{2,1,0:T(8,128)(2,1)}, u32[]{:S(2)}, u32[]{:S(2)}) collective-permute-start(bf16[8,128,256]{2,1,0:T(8,128)(2,1)} %get-tuple-element.44), channel_id=1, source_target_pairs={{0,12},{4,8},{8,4},{12,0},{1,13},{5,9},{9,5},{13,1},{2,14},{6,10},... | collective-permute-start | bytes 1572872 | tf_op jit(solution)/shard_map/ppermute | solution.py:315
  88.5 3.0 %collective-permute-start.19 = (f32[256,256]{1,0:T(8,128)}, f32[256,256]{1,0:T(8,128)}, u32[]{:S(2)}, u32[]{:S(2)}) collective-permute-start(f32[256,256]{1,0:T(8,128)} %constant_dynamic-slice_fusion.1), channel_id=1, source_target_pairs={{0,4},{4,0},{8,12},{12,8},{1,5},{5,1},{9,13},{13,9},{2,6},{6,2},{1... | collective-permute-start | bytes 786440 | tf_op jit(solution)/shard_map/ppermute | solution.py:146
  89.8 20.5 %collective-permute-start.12 = (bf16[8,128,256]{2,1,0:T(8,128)(2,1)}, bf16[8,128,256]{2,1,0:T(8,128)(2,1)}, u32[]{:S(2)}, u32[]{:S(2)}) collective-permute-start(bf16[8,128,256]{2,1,0:T(8,128)(2,1)} %get-tuple-element.42), channel_id=1, source_target_pairs={{0,12},{4,8},{8,4},{12,0},{1,13},{5,9},{9,5},{13,1},{2,14},{6,10},... | collective-permute-start | bytes 1572872 | tf_op jit(solution)/shard_map/ppermute | solution.py:315
  90.4 31.1 %collective-permute-start.13 = (bf16[8,128,256]{2,1,0:T(8,128)(2,1)}, bf16[8,128,256]{2,1,0:T(8,128)(2,1)}, u32[]{:S(2)}, u32[]{:S(2)}) collective-permute-start(bf16[8,128,256]{2,1,0:T(8,128)(2,1)} %get-tuple-element.43), channel_id=1, source_target_pairs={{0,12},{4,8},{8,4},{12,0},{1,13},{5,9},{9,5},{13,1},{2,14},{6,10},... | collective-permute-start | bytes 1572872 | tf_op jit(solution)/shard_map/ppermute | solution.py:315
  100.0 6.2 %collective-permute-start.20 = (f32[128,256]{1,0:T(8,128)S(1)}, f32[128,256]{1,0:T(8,128)S(1)}, u32[]{:S(2)}, u32[]{:S(2)}) collective-permute-start(f32[128,256]{1,0:T(8,128)S(1)} %constant_dynamic-slice_fusion), channel_id=1, source_target_pairs={{0,1},{1,0},{2,3},{3,2},{4,5},{5,4},{6,7},{7,6},{8,9},{9,8},{10,11... | collective-permute-start | bytes 393224 | tf_op jit(solution)/shard_map/ppermute | solution.py:146
  121.5 9.5 %collective-permute-start.21 = (f32[128,256]{1,0:T(8,128)S(1)}, f32[128,256]{1,0:T(8,128)S(1)}, u32[]{:S(2)}, u32[]{:S(2)}) collective-permute-start(f32[128,256]{1,0:T(8,128)S(1)} %dynamic-slice_add_fusion.1), channel_id=1, source_target_pairs={{0,2},{1,3},{2,0},{3,1},{4,6},{5,7},{6,4},{7,5},{8,10},{9,11},{10,... | collective-permute-start | bytes 393224 | tf_op jit(solution)/shard_map/ppermute | solution.py:151
  124.0 17.4 %collective-permute-start.9 = (bf16[3,128,256]{2,1,0:T(8,128)(2,1)}, bf16[3,128,256]{2,1,0:T(8,128)(2,1)S(1)}, u32[]{:S(2)}, u32[]{:S(2)}) collective-permute-start(bf16[3,128,256]{2,1,0:T(8,128)(2,1)} %get-tuple-element.39), channel_id=1, source_target_pairs={{0,12},{4,0},{8,4},{12,8},{1,13},{5,1},{9,5},{13,9},{2,14},{6,2},{... | collective-permute-start | bytes 589832 | tf_op jit(solution)/shard_map/ppermute | solution.py:317
  124.9 16.6 %collective-permute-start.10 = (bf16[3,128,256]{2,1,0:T(8,128)(2,1)}, bf16[3,128,256]{2,1,0:T(8,128)(2,1)S(1)}, u32[]{:S(2)}, u32[]{:S(2)}) collective-permute-start(bf16[3,128,256]{2,1,0:T(8,128)(2,1)} %get-tuple-element.40), channel_id=1, source_target_pairs={{0,8},{4,12},{8,0},{12,4},{1,9},{5,13},{9,1},{13,5},{2,10},{6,14},... | collective-permute-start | bytes 589832 | tf_op jit(solution)/shard_map/ppermute | solution.py:317
  125.8 15.7 %collective-permute-start.11 = (bf16[3,128,256]{2,1,0:T(8,128)(2,1)}, bf16[3,128,256]{2,1,0:T(8,128)(2,1)S(1)}, u32[]{:S(2)}, u32[]{:S(2)}) collective-permute-start(bf16[3,128,256]{2,1,0:T(8,128)(2,1)} %get-tuple-element.41), channel_id=1, source_target_pairs={{0,4},{4,8},{8,12},{12,0},{1,5},{5,9},{9,13},{13,1},{2,6},{6,10},{... | collective-permute-start | bytes 589832 | tf_op jit(solution)/shard_map/ppermute | solution.py:317
  131.7 7.0 %collective-permute-start.22 = (f32[128,256]{1,0:T(8,128)}, f32[128,256]{1,0:T(8,128)}, u32[]{:S(2)}, u32[]{:S(2)}) collective-permute-start(f32[128,256]{1,0:T(8,128)} %add.188), channel_id=1, source_target_pairs={{0,8},{4,12},{8,0},{12,4},{1,9},{5,13},{9,1},{13,5},{2,10},{6,14},... | collective-permute-start | bytes 393224 | tf_op jit(solution)/shard_map/ppermute | solution.py:151
  139.7 8.4 %collective-permute-start.23 = (f32[128,256]{1,0:T(8,128)S(1)}, f32[128,256]{1,0:T(8,128)S(1)}, u32[]{:S(2)}, u32[]{:S(2)}) collective-permute-start(f32[128,256]{1,0:T(8,128)S(1)} %add.189), channel_id=1, source_target_pairs={{0,1},{1,0},{2,3},{3,2},{4,5},{5,4},{6,7},{7,6},{8,9},{9,8},{10,11... | collective-permute-start | bytes 393224 | tf_op jit(solution)/shard_map/ppermute | solution.py:154
  141.5 2.2 %copy-start.1 = (f32[32,128,256]{2,1,0:T(8,128)S(1)}, f32[32,128,256]{2,1,0:T(8,128)}, u32[]{:S(2)}) copy-start(f32[32,128,256]{2,1,0:T(8,128)} %get-tuple-element.36.own_ref) | copy-start | bytes 12582916
  143.7 0.9 copy-start.5
  148.0 14.9 %collective-permute-start.16 = (bf16[8,128,256]{2,1,0:T(8,128)(2,1)S(1)}, bf16[8,128,256]{2,1,0:T(8,128)(2,1)S(1)}, u32[]{:S(2)}, u32[]{:S(2)}) collective-permute-start(bf16[8,128,256]{2,1,0:T(8,128)(2,1)S(1)} %add_convert_fusion.2), channel_id=1, source_target_pairs={{0,1},{1,0},{2,3},{3,2},{4,5},{5,4},{6,7},{7,6},{8,9},{9,8},{10,11... | collective-permute-start | bytes 1572872 | tf_op jit(solution)/shard_map/ppermute | solution.py:352
  148.1 40.1 %copy-start.9 = (f32[1024,256]{1,0:T(8,128)S(1)}, f32[1024,256]{1,0:T(8,128)}, u32[]{:S(2)}) copy-start(f32[1024,256]{1,0:T(8,128)} %get-tuple-element.35) | copy-start | bytes 3145732
  148.1 17.3 %collective-permute-start.24 = (f32[256,256]{1,0:T(8,128)S(1)}, f32[256,256]{1,0:T(8,128)S(1)}, u32[]{:S(2)}, u32[]{:S(2)}) collective-permute-start(f32[256,256]{1,0:T(8,128)S(1)} %pad_maximum_fusion.1), channel_id=1, source_target_pairs={{0,4},{4,0},{8,12},{12,8},{1,5},{5,1},{9,13},{13,9},{2,6},{6,2},{1... | collective-permute-start | bytes 786440 | tf_op jit(solution)/shard_map/ppermute | solution.py:154
  149.5 30.4 %collective-permute-start.17 = (bf16[8,128,256]{2,1,0:T(8,128)(2,1)S(1)}, bf16[8,128,256]{2,1,0:T(8,128)(2,1)S(1)}, u32[]{:S(2)}, u32[]{:S(2)}) collective-permute-start(bf16[8,128,256]{2,1,0:T(8,128)(2,1)S(1)} %add_convert_fusion.1), channel_id=1, source_target_pairs={{0,1},{1,0},{2,3},{3,2},{4,5},{5,4},{6,7},{7,6},{8,9},{9,8},{10,11... | collective-permute-start | bytes 1572872 | tf_op jit(solution)/shard_map/ppermute | solution.py:352
  164.1 24.1 %collective-permute-start.18 = (bf16[8,128,256]{2,1,0:T(8,128)(2,1)S(1)}, bf16[8,128,256]{2,1,0:T(8,128)(2,1)S(1)}, u32[]{:S(2)}, u32[]{:S(2)}) collective-permute-start(bf16[8,128,256]{2,1,0:T(8,128)(2,1)S(1)} %add_convert_fusion), channel_id=1, source_target_pairs={{0,2},{1,3},{2,0},{3,1},{4,6},{5,7},{6,4},{7,5},{8,10},{9,11},{10,... | collective-permute-start | bytes 1572872 | tf_op jit(solution)/shard_map/ppermute | solution.py:352
